TPU v7x, 32 devices: a whole 2x2x4 slice. The times are simulated.
32 devices in a mesh: cheb: 4 (over y, core), wear: 4 (over z), age: 2 (over x).
Axes of the slice: x: 2, y: 2, z: 4, core: 2. Of those that a mesh axis runs over, the one named last changes fastest.
Arguments:
- adjoint_value: float32 [256, 128, 1024], P('wear', 'age', 'cheb'), may hold values from -6 to 6
- load_diffusion: float32 [1024], replicated, may hold values from 0.2 to 1
- load_drift: float32 [1024], replicated, may hold values from -1 to 1
- wear_speed: float32 [1024], P('cheb'), may hold values from 0.05 to 0.3
- hazard: float32 [256, 128], P('wear', 'age'), may hold values from 0.05 to 0.5
Outputs:
- next_value: float32 [256, 128, 1024], P('wear', 'age', 'cheb')
All inputs are finite; a program needn't handle non-finite values.
Results may differ from a plain program's by a relative error of at most 0.0037.
Values may be sent and summed in bfloat16 or wider, within the bound.
No kernel may reach another device: no remote copies, remote signals or barrier semaphores. Data moves between devices by JAX's collectives and lax.ppermute only.
A program may use at most 128 MiB of HBM per device.

v0:
```python
import functools

import jax
import jax.numpy as jnp
import numpy as np
from jax import lax
from jax.experimental import pallas as pl
from jax.experimental.pallas import tpu as pltpu
from jax.sharding import PartitionSpec as P

SUBSTEPS = 4
HALO = SUBSTEPS

age_courant = 0.4
wear_spread = 0.1
coupling = 0.05
GAIN = 1.0 / coupling
START = coupling**SUBSTEPS

f32 = jnp.float32
bf16 = jnp.bfloat16


def operators(points):
    modes = np.arange(points)[:, None]
    nodes = np.arange(points)[None, :]
    angles = (modes * (2 * nodes + 1)) % (4 * points) * (np.pi / (2 * points))
    cosine, sine = np.cos(angles), np.sin(angles)
    analysis = np.where(modes == 0, 1.0, 2.0) / points * cosine
    wavenumber = modes / points
    return (-(wavenumber**2) * cosine).T @ analysis, (wavenumber * sine).T @ analysis


def arrived_rows(rank):
    return -(-rank // 16) * 16


@functools.lru_cache(maxsize=None)
def factors(points, devices):
    second, first = operators(points)
    size = points // devices
    parts = [slice(b * size, (b + 1) * size) for b in range(devices)]
    slots, found = [], {}
    for shift in range(1, devices):
        groups = {}
        for c in range(devices):
            b = c ^ shift if devices & (devices - 1) == 0 else (c + shift) % devices
            joint = np.concatenate([second[parts[b], parts[c]], first[parts[b], parts[c]]])
            _, sizes, rows = np.linalg.svd(joint, full_matrices=False)
            rank = int((sizes > joint.shape[0] * np.finfo(np.float64).eps).sum())
            rank = -(-rank // 8) * 8
            basis = rows[:rank]
            found[c, b] = (basis, second[parts[b], parts[c]] @ basis.T, first[parts[b], parts[c]] @ basis.T)
            groups.setdefault(rank, []).append((c, b))
        slots += [(tuple(pairs), rank) for rank, pairs in sorted(groups.items())]
    send = np.zeros((devices, sum(rank for _, rank in slots), size))
    wide = sum(arrived_rows(rank) for _, rank in slots)
    take_second = np.zeros((devices, 2, wide, size))
    take_first = np.zeros((devices, 2, wide, size))
    at = row = 0
    for pairs, rank in slots:
        whole = rank // 16 * 16
        for c, b in pairs:
            basis, left_second, left_first = found[c, b]
            send[c, at : at + rank] = basis
            for half in range(2):
                for take, left in ((take_second, left_second.T), (take_first, left_first.T)):
                    take[b, half, row : row + whole] = left[:whole]
                    place = row + whole + half * (rank - whole)
                    take[b, half, place : place + rank - whole] = left[whole:]
        at += rank
        row += arrived_rows(rank)
    own_second = np.stack([second[p, p].T for p in parts])
    own_first = np.stack([first[p, p].T for p in parts])
    return slots, send, take_second, take_first, own_second, own_first


ANY = pl.BlockSpec(memory_space=pl.ANY)
VMEM = pl.BlockSpec(memory_space=pltpu.VMEM)
SMEM = pl.BlockSpec(memory_space=pltpu.SMEM)
ROW0 = 16
HAZARD_ROWS = 16


def in_hbm(x):
    return pltpu.with_memory_space_constraint(x, pltpu.HBM)


def in_vmem(x):
    return pltpu.with_memory_space_constraint(x, pltpu.VMEM)


def params(mebibytes):
    return pltpu.CompilerParams(vmem_limit_bytes=mebibytes * 2**20)


def cost(flops, bytes_accessed):
    return pl.CostEstimate(flops=flops, bytes_accessed=bytes_accessed, transcendentals=0)


def edge_kernel(sides, side_ref, u_hbm, hazard_hbm, *refs):
    out_refs, (tiles, hazard, sem) = refs[:sides], refs[sides:]
    wears, ages, size = u_hbm.shape
    copies = [pltpu.make_async_copy(hazard_hbm, hazard, sem.at[sides])]
    for i in range(sides):
        if sides == 1:
            start = pl.multiple_of(jnp.where(side_ref[0] == 0, ages - 8, 0), 8)
        else:
            start = (ages - 8, 0)[i]
        copies.append(pltpu.make_async_copy(u_hbm.at[:, pl.ds(start, 8)], tiles.at[i], sem.at[i]))
    for copy in copies:
        copy.start()
    for copy in copies:
        copy.wait()
    by_age = jnp.transpose(hazard[...])
    last, early = by_age[ages - HALO :], by_age[:HALO]
    for i, out_ref in enumerate(out_refs):
        for w in range(0, wears, 4):
            late = [tiles[i, w + j, 8 - HALO :] for j in range(4)]
            soon = [tiles[i, w + j, :HALO] for j in range(4)]
            late, soon = jnp.concatenate(late, axis=0), jnp.concatenate(soon, axis=0)
            if sides == 1:
                cells = jnp.where(side_ref[0] == 0, late, soon)
            else:
                cells = (late, soon)[i]
            out_ref[w * HALO : (w + 4) * HALO] = cells.astype(bf16)
        if sides == 1:
            exact = jnp.where(side_ref[0] == 0, last, early)
        else:
            exact = (last, early)[i]
        high = exact.astype(bf16).astype(f32)
        rows = jnp.concatenate([high, exact - high, jnp.zeros((HAZARD_ROWS - 2 * HALO, wears), f32)], axis=0)
        rows = jnp.concatenate([rows, jnp.zeros((HAZARD_ROWS, size - wears), f32)], axis=1)
        out_ref[wears * HALO :] = rows.astype(bf16)


def edges(side, u, hazard, sides):
    wears, ages, size = u.shape
    return pl.pallas_call(
        functools.partial(edge_kernel, sides),
        in_specs=[SMEM, ANY, ANY],
        out_specs=[VMEM] * sides,
        out_shape=[jax.ShapeDtypeStruct((wears * HALO + HAZARD_ROWS, size), bf16)] * sides,
        scratch_shapes=[
            pltpu.VMEM((sides, wears, 8, size), f32),
            pltpu.VMEM((wears, ages), f32),
            pltpu.SemaphoreType.DMA((sides + 1,)),
        ],
        compiler_params=params(8),
        cost_estimate=cost(0, 8 * wears * 8 * size),
        name="age_edges",
    )(side, in_hbm(u), in_hbm(hazard))


def pack_rows(ranks, halves):
    packed, row = [], 0
    for rank in ranks:
        cut = row + rank // 16 * 16
        pieces = [h[row:cut] for h in halves if cut > row]
        pieces += [h[cut : row + rank] for h in halves if cut < row + rank]
        packed.append(jnp.concatenate(pieces, axis=0).astype(bf16))
        row += rank
    return packed


def analyse(table, cells):
    return lax.dot_general(table, cells, (((1,), (1,)), ((), ())), preferred_element_type=f32)


def pack_kernel(ranks, at_ref, u_hbm, send_hbm, *refs):
    q_refs, (u_ref, send, send_sem, u_sem) = refs[: len(ranks)], refs[len(ranks) :]
    _, wears, ages, size = u_ref.shape
    chunk = 4
    table = pltpu.make_async_copy(send_hbm.at[at_ref[0]], send, send_sem)
    table.start()
    loads = []
    for g in range(wears // chunk):
        rows = pl.ds(g * chunk, chunk)
        loads.append(pltpu.make_async_copy(u_hbm.at[:, rows], u_ref.at[:, rows], u_sem.at[g]))
        loads[-1].start()
    table.wait()
    for g in range(wears // chunk):
        loads[g].wait()
        halves = [
            analyse(send[...], u_ref[half, g * chunk : (g + 1) * chunk].reshape(chunk * ages, size).astype(bf16))
            for half in range(2)
        ]
        for q_ref, rows in zip(q_refs, pack_rows(ranks, halves)):
            q_ref[:, g * chunk * ages : (g + 1) * chunk * ages] = rows


def pack(at, u4, send, ranks, extra):
    _, wears, ages, size = u4.shape
    cells = wears * ages
    return pl.pallas_call(
        functools.partial(pack_kernel, ranks),
        in_specs=[SMEM, ANY, ANY],
        out_specs=[VMEM] * (len(ranks) + 2),
        out_shape=[jax.ShapeDtypeStruct((2 * r, cells + extra), bf16) for r in ranks]
        + [pltpu.VMEM(u4.shape, f32), pltpu.VMEM(send.shape[1:], bf16)],
        scratch_shapes=[pltpu.SemaphoreType.DMA, pltpu.SemaphoreType.DMA((wears // 4,))],
        compiler_params=params(16),
        cost_estimate=cost(4 * cells * sum(ranks) * size, 8 * cells * size),
        name="pack_coefficients",
    )(at, in_hbm(u4), in_hbm(send))


def pack_edges_kernel(ranks, sides, send_ref, *refs):
    edge_refs, q_refs = refs[:sides], refs[sides + len(ranks) :]
    count = edge_refs[0].shape[0] - HAZARD_ROWS
    halves = []
    for half in range(2):
        cells = [r[half * count // 2 : (half + 1) * count // 2] for r in edge_refs]
        halves.append(analyse(send_ref[...], jnp.concatenate(cells, axis=0)))
    for q_ref, rows in zip(q_refs, pack_rows(ranks, halves)):
        q_ref[:, q_ref.shape[1] - rows.shape[1] :] = rows


def pack_edges(send, near, q, ranks, sides):
    return pl.pallas_call(
        functools.partial(pack_edges_kernel, ranks, sides),
        in_specs=[VMEM] * (1 + sides + len(ranks)),
        out_specs=[VMEM] * len(ranks),
        out_shape=[jax.ShapeDtypeStruct(x.shape, x.dtype) for x in q],
        input_output_aliases={1 + sides + i: i for i in range(len(ranks))},
        compiler_params=params(8),
        cost_estimate=cost(0, 2**18),
        name="pack_edges",
    )(in_vmem(send), *near, *q)


def local_kernel(sides, at_ref, u_ref, hazard_hbm, diffusion_hbm, drift_hbm, second_hbm, first_hbm, take_second_hbm,
                 take_first_hbm, *refs):
    edge_refs, refs = refs[:sides], refs[sides:]
    z, beside, take, hazard, diffusion, drift, second, first, own, take_second, take_first, sem = refs
    halves, rows, _, _ = z.shape
    _, wears, ages, size = u_ref.shape
    at = at_ref[0]
    moves = (
        (second_hbm.at[at], second), (first_hbm.at[at], first), (diffusion_hbm.at[at], diffusion),
        (drift_hbm.at[at], drift), (hazard_hbm, hazard), (take_second_hbm.at[at], take_second),
        (take_first_hbm.at[at], take_first),
    )
    copies = [pltpu.make_async_copy(src, dst, sem.at[i]) for i, (src, dst) in enumerate(moves)]
    for copy in copies:
        copy.start()
    for l in range(halves):
        zero = jnp.zeros((rows, 16, 128), f32)
        z[l, :, :ROW0, :] = zero
        z[l, :, ROW0 + ages :, :] = zero
    for copy in copies:
        copy.wait()
    scaled, moved = START * diffusion[...], START * drift[...]
    own[...] = (second[...] * scaled + first[...] * moved).astype(bf16)
    take[...] = (take_second[...] * scaled + take_first[...] * moved).astype(bf16)
    keep = jnp.transpose(START - START * hazard[...])
    chunk = 4
    for w in range(0, 2 * wears, chunk):
        half, v = divmod(w, wears)
        u = u_ref[half, v : v + chunk].reshape(chunk * ages, size)
        rate = jnp.dot(u.astype(bf16), own[...], preferred_element_type=f32)
        for i in range(chunk):
            cells = slice(i * ages, (i + 1) * ages)
            value = rate[cells] + keep[:, w + i : w + i + 1] * u[cells]
            for l in range(halves):
                z[l, HALO + w + i, ROW0 : ROW0 + ages, :] = value[:, l * 128 : (l + 1) * 128]
    for s, ref in enumerate(edge_refs):
        count = 2 * wears * HALO
        parts = ref[count:].astype(f32)
        near = START - START * (parts[:HALO, : 2 * wears] + parts[HALO : 2 * HALO, : 2 * wears])
        near = jnp.concatenate([near, near], axis=0)
        for w in range(0, 2 * wears, 4):
            place = slice(w * HALO, (w + 4) * HALO)
            u = ref[place]
            rate = jnp.dot(u, own[...], preferred_element_type=f32)
            columns = [
                jnp.broadcast_to(near[:HALO, w + j : w + j + 1], (HALO, size)) for j in range(4)
            ]
            beside[s, place] = rate + jnp.concatenate(columns, axis=0) * u.astype(f32)


def local(at, u4, hazard, diffusion, drift, tables, near, sides):
    _, wears, ages, size = u4.shape
    cells = 2 * wears * ages
    wide = tables[2].shape[2]
    return pl.pallas_call(
        functools.partial(local_kernel, sides),
        in_specs=[SMEM, VMEM] + [ANY] * 7 + [VMEM] * sides,
        out_specs=[VMEM] * 3,
        out_shape=[
            pltpu.VMEM((size // 128, 2 * wears + 2 * HALO, ages + 32, 128), f32),
            pltpu.VMEM((sides, 2 * wears * HALO, size), f32),
            pltpu.VMEM((2, wide, size), bf16),
        ],
        scratch_shapes=[
            pltpu.VMEM(hazard.shape, f32),
            pltpu.VMEM((1, size), f32),
            pltpu.VMEM((1, size), f32),
            pltpu.VMEM((size, size), f32),
            pltpu.VMEM((size, size), f32),
            pltpu.VMEM((size, size), bf16),
            pltpu.VMEM((2, wide, size), f32),
            pltpu.VMEM((2, wide, size), f32),
            pltpu.SemaphoreType.DMA((7,)),
        ],
        compiler_params=params(24),
        cost_estimate=cost(2 * cells * size * size, 8 * cells * size),
        name="local_rate",
    )(at, in_vmem(u4), *[in_hbm(x) for x in (hazard, diffusion, drift, *tables)], *near)


def arrived_tiles(ranks, q_refs, half, columns):
    tiles = []
    for rank, q in zip(ranks, q_refs):
        cut = rank // 16 * 16
        if cut:
            tiles.append(q[half * cut : (half + 1) * cut, columns])
        if rank > cut:
            tiles.append(q[2 * cut : 2 * rank, columns])
    return jnp.concatenate(tiles, axis=0)


def distant(ranks, q_refs, take_ref, half, columns):
    return lax.dot_general(
        arrived_tiles(ranks, q_refs, half, columns), take_ref[half], (((0,), (0,)), ((), ())),
        preferred_element_type=f32,
    )


def edge_columns(sides, main, each):
    return [slice(main + s * each, main + (s + 1) * each) for s in range(sides)]


def rows_kernel(ranks, sides, wears, ages, z_in, beside_ref, take_ref, *refs):
    q_refs, (z, top_ref, bottom_ref) = refs[: len(ranks)], refs[len(ranks) :]
    del z
    halves = z_in.shape[0]
    main, each = wears // 2 * ages, wears // 2 * HALO
    for half, start, ref in ((0, 0, top_ref), (1, wears - HALO, bottom_ref)):
        v = (start - half * wears // 2) * ages
        rate = distant(ranks, q_refs, take_ref, half, slice(v, v + HALO * ages))
        for i in range(HALO):
            near = [z_in[l, HALO + start + i, ROW0 : ROW0 + ages, :] for l in range(halves)]
            cells = slice(i * ages, (i + 1) * ages)
            ref[cells] = (rate[cells] + jnp.concatenate(near, axis=1)).astype(bf16)
        for s, columns in enumerate(edge_columns(sides, main, each)):
            corner = HALO * HALO
            first = 0 if half == 0 else each - corner
            rate = distant(ranks, q_refs, take_ref, half, columns)[first : first + corner]
            place = slice(start * HALO, start * HALO + corner)
            row = HALO * ages + s * corner
            ref[row : row + corner] = (rate + beside_ref[s, place]).astype(bf16)


def outer_rows(z, beside, take, q, ranks, sides, wears, ages):
    size = z.shape[0] * 128
    message = jax.ShapeDtypeStruct((HALO * ages + sides * HALO * HALO, size), bf16)
    return pl.pallas_call(
        functools.partial(rows_kernel, ranks, sides, wears, ages),
        in_specs=[VMEM] * (3 + len(ranks)),
        out_specs=[VMEM] * 3,
        out_shape=[pltpu.VMEM(z.shape, f32), message, message],
        input_output_aliases={0: 0},
        compiler_params=params(8),
        cost_estimate=cost(2 * 8 * ages * take.shape[1] * size, 2**20),
        name="outer_rows",
    )(z, in_vmem(beside), in_vmem(take), *q)


def section_kernel(ranks, sides, wears, ages, flag_ref, z_in, beside_ref, take_ref, *refs):
    q_refs, (z,) = refs[: len(ranks)], refs[len(ranks) :]
    halves = z.shape[0]
    main, each = wears // 2 * ages, wears // 2 * HALO
    chunk = 4
    for w in range(0, wears, chunk):
        half, v = divmod(w, wears // 2)
        rate = distant(ranks, q_refs, take_ref, half, slice(v * ages, (v + chunk) * ages))
        for i in range(chunk):
            for l in range(halves):
                z[l, HALO + w + i, ROW0 : ROW0 + ages, :] = (
                    z_in[l, HALO + w + i, ROW0 : ROW0 + ages, :]
                    + rate[i * ages : (i + 1) * ages, l * 128 : (l + 1) * 128]
                )
    has = [jnp.where(flag_ref[2 + i] == 1, 0.0, 1.0).astype(f32) for i in range(2)]
    for s in range(sides):
        for half in range(2):
            columns = edge_columns(sides, main, each)[s]
            place = slice(half * each, (half + 1) * each)
            cells = distant(ranks, q_refs, take_ref, half, columns) + beside_ref[s, place]
            for i, column in ((0, ROW0 - HALO), (1, ROW0 + ages)):
                if sides == 1 or s == i:
                    part = cells * has[i]
                    for w in range(wears // 2):
                        for l in range(halves):
                            z[l, HALO + half * wears // 2 + w, column : column + HALO, :] = part[
                                w * HALO : (w + 1) * HALO, l * 128 : (l + 1) * 128
                            ]


def section(flags, z, beside, take, q, ranks, sides, wears, ages):
    size = z.shape[0] * 128
    cells = wears * ages
    return pl.pallas_call(
        functools.partial(section_kernel, ranks, sides, wears, ages),
        in_specs=[SMEM] + [VMEM] * (3 + len(ranks)),
        out_specs=VMEM,
        out_shape=pltpu.VMEM(z.shape, f32),
        input_output_aliases={1: 0},
        compiler_params=params(24),
        cost_estimate=cost(2 * cells * take.shape[1] * size, 8 * cells * size),
        name="section",
    )(flags, z, in_vmem(beside), in_vmem(take), *q)


def substeps_kernel(sides, flag_ref, z_in, speed_ref, up_ref, down_ref, o_ref, za, zb, stage, out_sem):
    del z_in
    halves, rows, _, _ = za.shape
    wears, ages = rows - 2 * HALO, stage.shape[1]
    first_w, last_w, first_a, last_a = (flag_ref[i] == 1 for i in range(4))
    has = [jnp.where(x, 0.0, 1.0).astype(f32) for x in (first_a, last_a)]
    for l in range(halves):
        lanes = pl.ds(l * 128, 128)
        zb[l, :, :ROW0, :] = jnp.zeros((rows, ROW0, 128), f32)
        zb[l, :, ROW0 + ages :, :] = jnp.zeros((rows, 16, 128), f32)
        for ref, at in ((up_ref, 0), (down_ref, HALO + wears)):
            values = ref[:, lanes].astype(f32)
            za[l, at : at + HALO, ROW0 : ROW0 + ages, :] = values[: HALO * ages].reshape(HALO, ages, 128)
            for s in range(sides):
                corner = values[HALO * (ages + s * HALO) : HALO * (ages + (s + 1) * HALO)]
                for i, column in ((0, ROW0 - HALO), (1, ROW0 + ages)):
                    if sides == 1 or s == i:
                        part = corner * has[i]
                        for w in range(HALO):
                            za[l, at + w, column : column + HALO, :] = part[w * HALO : (w + 1) * HALO]

    def run(low, high, masked):
        stores = []
        keep_low = jnp.zeros((8, 128), f32) + has[0]
        keep_high = jnp.zeros((8, 128), f32) + has[1]
        for k in range(1, SUBSTEPS + 1):
            src, dst = (za, zb) if k % 2 == 1 else (zb, za)
            final = k == SUBSTEPS
            lo, hi = (ROW0, ROW0 + ages) if final else (low, high)
            pieces = 4 if final else 1
            bounds = [k + (rows - 2 * k) * p // pieces for p in range(pieces + 1)]
            for p in range(pieces):
                for l in range(halves):
                    speed = speed_ref[0:1, l * 128 : (l + 1) * 128]
                    stay = GAIN * (1.0 - age_courant - 2.0 * wear_spread - speed)
                    worn = GAIN * (speed + wear_spread)

                    def terms(w, src=src, l=l, lo=lo, hi=hi, stay=stay, worn=worn):
                        t = src[l, w, lo:hi, :]
                        older = src[l, w, lo + 1 : hi + 1, :]
                        slope = older - src[l, w, lo - 1 : hi - 1, :]
                        centre = stay * t + (GAIN * age_courant) * older
                        less = (t - slope) + t
                        return centre, worn * t + slope, less

                    def body(w, carry, dst=dst, l=l, lo=lo, hi=hi, final=final, terms=terms):
                        partial, less = carry
                        centre, more, new_less = terms(w + 1)
                        out = partial + more
                        if final:
                            stage[w - HALO, :, l * 128 : (l + 1) * 128] = out
                        elif masked:
                            dst[l, w, lo : lo + 8, :] = out[:8] * keep_low
                            dst[l, w, lo + 8 : hi - 8, :] = out[8:-8]
                            dst[l, w, hi - 8 : hi, :] = out[-8:] * keep_high
                        else:
                            dst[l, w, lo:hi, :] = out
                        return centre + less, new_less

                    start, stop = bounds[p], bounds[p + 1]
                    _, _, less0 = terms(start - 1)
                    centre1, _, less1 = terms(start)
                    count = stop - start
                    lax.fori_loop(start, stop, body, (centre1 + less0, less1), unroll=4 if count % 4 == 0 else 2)
                if final:
                    a, b = bounds[p] - HALO, bounds[p + 1] - HALO
                    copy = pltpu.make_async_copy(
                        stage.at[pl.ds(a, b - a)], o_ref.at[pl.ds(a, b - a)], out_sem.at[p]
                    )
                    copy.start()
                    stores.append(copy)
            if not final:
                for at, flag in ((HALO - 1, first_w), (HALO + wears, last_w)):
                    @pl.when(flag)
                    def _(dst=dst, at=at):
                        for l in range(halves):
                            dst[l, at, low:high, :] = jnp.zeros((high - low, 128), f32)
        for copy in stores:
            copy.wait()

    if sides == 1:
        pl.when(first_a)(lambda: run(ROW0, ROW0 + ages + 8, False))
        pl.when(last_a)(lambda: run(ROW0 - 8, ROW0 + ages, False))
    else:
        run(ROW0 - 8, ROW0 + ages + 8, True)


def run_substeps(flags, z, speed, up, down, sides, wears, ages):
    size = z.shape[0] * 128
    shape = (wears, ages, size)
    return pl.pallas_call(
        functools.partial(substeps_kernel, sides),
        out_shape=[jax.ShapeDtypeStruct(shape, f32), pltpu.VMEM(z.shape, f32)],
        in_specs=[SMEM] + [VMEM] * 4,
        out_specs=[ANY, VMEM],
        scratch_shapes=[
            pltpu.VMEM(z.shape, f32),
            pltpu.VMEM(shape, f32),
            pltpu.SemaphoreType.DMA((4,)),
        ],
        input_output_aliases={1: 1},
        compiler_params=params(32),
        cost_estimate=cost(10 * SUBSTEPS * wears * ages * size, 8 * wears * ages * size),
        name="substeps",
    )(flags, z, speed, up, down)[0]


def body(adjoint_value, load_diffusion, load_drift, wear_speed, hazard):
    wears, ages, size = adjoint_value.shape
    points = load_diffusion.shape[0]
    devices = points // size
    slots, send, take_second, take_first, own_second, own_first = factors(points, devices)
    ranks = tuple(rank for _, rank in slots)
    cheb = lax.axis_index("cheb")
    wear, age = lax.axis_index("wear"), lax.axis_index("age")
    n_wear, n_age = lax.axis_size("wear"), lax.axis_size("age")
    at = cheb.astype(jnp.int32).reshape(1)
    side = age.astype(jnp.int32).reshape(1)
    flags = jnp.stack([wear == 0, wear == n_wear - 1, age == 0, age == n_age - 1]).astype(jnp.int32)
    sides = 1 if n_age == 2 else 2
    extra = sides * wears // 2 * HALO
    u4 = adjoint_value.reshape(2, wears // 2, ages, size)
    diffusion = load_diffusion.reshape(devices, 1, size)
    drift = load_drift.reshape(devices, 1, size)
    tables = [jnp.asarray(t, f32) for t in (own_second, own_first, take_second, take_first)]

    edge = edges(side, adjoint_value, hazard, sides)
    after = [(i, i + 1) for i in range(n_age - 1)]
    before = [(i + 1, i) for i in range(n_age - 1)]
    if sides == 1:
        near = [lax.ppermute(edge[0], "age", after + before)]
    else:
        near = [lax.ppermute(x, "age", pairs) for x, pairs in zip(edge, (after, before))]
    *q, u4, send = pack(at, u4, jnp.asarray(send, bf16), ranks, extra)
    q = pack_edges(send, near, q, ranks, sides)
    arrived = [lax.ppermute(x, "cheb", list(pairs)) for x, (pairs, _) in zip(q, slots)]
    z, beside, take = local(at, u4, hazard, diffusion, drift, tables, near, sides)
    z, top, bottom = outer_rows(z, beside, take, arrived, ranks, sides, wears, ages)
    up = lax.ppermute(bottom, "wear", [(i, i + 1) for i in range(n_wear - 1)])
    down = lax.ppermute(top, "wear", [(i + 1, i) for i in range(n_wear - 1)])
    z = section(flags, z, beside, take, arrived, ranks, sides, wears, ages)
    return run_substeps(flags, z, wear_speed.reshape(1, size), up, down, sides, wears, ages)


def solution(mesh):
    placed = (P("wear", "age", "cheb"), P(), P(), P("cheb"), P("wear", "age"))
    return jax.shard_map(
        body, mesh=mesh, in_specs=placed, out_specs=P("wear", "age", "cheb"), check_vma=False
    )
```

profile of v0, /device:TPU:0, one launch (start us, length us, event | category | flops | bytes accessed | tf_op | source)
XLA Modules:
  0.0 46.3 jit_solution(9002380797804977335)
XLA Ops:
  0.0 1.2 %age_edges.1 = bf16[272,256]{1,0:T(8,128)(2,1)S(1)} custom-call(s32[1]{0:T(128)} %bitcast.8.side_ref, f32[64,64,256]{2,1,0:T(8,128)} %u_hbm.1, f32[64,64]{1,0:T(8,128)} %hazard_hbm.3), custom_call_target="tpu_custom_call" | custom-call | bytes 1048576 | tf_op jit(solution)/shard_map/age_edges/pallas_call | solution.py:139
  1.2 3.0 %collective-permute-start = (bf16[272,256]{1,0:T(8,128)(2,1)S(1)}, bf16[272,256]{1,0:T(8,128)(2,1)S(1)}, u32[]{:S(2)}, u32[]{:S(2)}) collective-permute-start(bf16[272,256]{1,0:T(8,128)(2,1)S(1)} %age_edges.1), channel_id=1, source_target_pairs={{0,1},{1,0},{2,3},{3,2},{4,5},{5,4},{6,7},{7,6},{8,9},{9,8},{10,11... | collective-permute-start | bytes 417800 | tf_op jit(solution)/shard_map/ppermute | solution.py:545
  4.2 3.6 %pack_coefficients.1 = (bf16[48,2176]{1,0:T(8,128)(2,1)S(1)}, bf16[16,2176]{1,0:T(8,128)(2,1)S(1)}, bf16[16,2176]{1,0:T(8,128)(2,1)S(1)}, bf16[48,2176]{1,0:T(8,...) custom-call(s32[1]{0:T(128)} %bitcast.4.at_ref, f32[2,32,64,256]{3,2,1,0:T(8,128)} %bitcast.11, ...), custom_call_target="tpu_custom_call" | custom-call | flops 134217728 | bytes 4194304 | tf_op jit(solution)/shard_map/pack_coefficients/pallas_call | solution.py:195
  7.8 0.0 collective-permute-done.refs_0_
  7.9 0.2 pack_edges.1
  8.0 0.1 collective-permute-start.1
  8.1 0.7 %collective-permute-start.4 = (bf16[48,2176]{1,0:T(8,128)(2,1)S(1)}, bf16[48,2176]{1,0:T(8,128)(2,1)S(1)}, u32[]{:S(2)}, u32[]{:S(2)}) collective-permute-start(bf16[48,2176]{1,0:T(8,128)(2,1)S(1)} %get-tuple-element.34), channel_id=1, source_target_pairs={{8,16},{16,8},{9,17},{17,9},{10,18},{18,10},{11,19},{19,11},{12,20... | collective-permute-start | bytes 626696 | tf_op jit(solution)/shard_map/ppermute | solution.py:550
  8.8 3.4 %collective-permute-start.2 = (bf16[16,2176]{1,0:T(8,128)(2,1)S(1)}, bf16[16,2176]{1,0:T(8,128)(2,1)S(1)}, u32[]{:S(2)}, u32[]{:S(2)}) collective-permute-start(bf16[16,2176]{1,0:T(8,128)(2,1)S(1)} %get-tuple-element.32), channel_id=1, source_target_pairs={{0,16},{8,24},{16,0},{24,8},{1,17},{9,25},{17,1},{25,9},{2,18},{10... | collective-permute-start | bytes 208904 | tf_op jit(solution)/shard_map/ppermute | solution.py:550
  12.2 3.0 %collective-permute-start.3 = (bf16[16,2176]{1,0:T(8,128)(2,1)S(1)}, bf16[16,2176]{1,0:T(8,128)(2,1)S(1)}, u32[]{:S(2)}, u32[]{:S(2)}) collective-permute-start(bf16[16,2176]{1,0:T(8,128)(2,1)S(1)} %get-tuple-element.33), channel_id=1, source_target_pairs={{0,24},{24,0},{1,25},{25,1},{2,26},{26,2},{3,27},{27,3},{4,28},{28... | collective-permute-start | bytes 208904 | tf_op jit(solution)/shard_map/ppermute | solution.py:550
  15.2 2.4 %local_rate.1 = (f32[2,72,96,128]{3,2,1,0:T(8,128)S(1)}, f32[1,256,256]{2,1,0:T(8,128)S(1)}, bf16[2,96,256]{2,1,0:T(8,128)(2,1)S(1)}) custom-call(s32[1]{0:T(128)} %bitcast.4.at_ref, f32[2,32,64,256]{3,2,1,0:T(8,128)S(1)} %get-tuple-element.22.u_ref, f32[64,64]{1,0:T(8,128)} %hazard_hbm.3, f32[4,1,256]{2,1,0:T(1,128)} %bitcast.12, f32[4,1,256]{2,1,0:T(1,128)} %bitcast.13, ...), custom_call_target="tpu_custom_call" | custom-call | flops 536870912 | bytes 8388608 | tf_op jit(solution)/shard_map/local_rate/pallas_call | solution.py:286
  17.7 0.0 collective-permute-done.2.refs_1_
  17.7 0.4 collective-permute-done.3.refs_2_
  18.1 0.0 collective-permute-done.1.refs_0_
  18.1 0.0 collective-permute-done.4.refs_3_
  18.1 0.3 outer_rows.1
  18.4 0.0 copy-start
  18.4 2.9 %copy-done = f32[2,72,96,128]{3,2,1,0:T(8,128)} copy-done((f32[2,72,96,128]{3,2,1,0:T(8,128)}, f32[2,72,96,128]{3,2,1,0:T(8,128)S(1)}, u32[]{:S(2)}) %copy-start) | copy-done | bytes 7077912
  21.3 3.7 %collective-permute-start.5 = (bf16[272,256]{1,0:T(8,128)(2,1)S(1)}, bf16[272,256]{1,0:T(8,128)(2,1)S(1)}, u32[]{:S(2)}, u32[]{:S(2)}) collective-permute-start(bf16[272,256]{1,0:T(8,128)(2,1)S(1)} %get-tuple-element.36), channel_id=1, source_target_pairs={{0,2},{2,4},{4,6},{1,3},{3,5},{5,7},{8,10},{10,12},{12,14},{9,11},... | collective-permute-start | bytes 417800 | tf_op jit(solution)/shard_map/ppermute | solution.py:553
  25.0 1.3 %collective-permute-start.6 = (bf16[272,256]{1,0:T(8,128)(2,1)S(1)}, bf16[272,256]{1,0:T(8,128)(2,1)S(1)}, u32[]{:S(2)}, u32[]{:S(2)}) collective-permute-start(bf16[272,256]{1,0:T(8,128)(2,1)S(1)} %get-tuple-element.37), channel_id=1, source_target_pairs={{2,0},{4,2},{6,4},{3,1},{5,3},{7,5},{10,8},{12,10},{14,12},{11,9},... | collective-permute-start | bytes 417800 | tf_op jit(solution)/shard_map/ppermute | solution.py:554
  26.4 0.1 add_convert_fusion.flag_ref
  26.4 0.0 copy-start.1
  26.4 3.0 %copy-done.1 = f32[2,72,96,128]{3,2,1,0:T(8,128)S(1)} copy-done((f32[2,72,96,128]{3,2,1,0:T(8,128)S(1)}, f32[2,72,96,128]{3,2,1,0:T(8,128)}, u32[]{:S(2)}) %copy-start.1) | copy-done | bytes 7077912
  29.4 0.0 copy-start.4
  29.4 1.7 %section.1.z_in = f32[2,72,96,128]{3,2,1,0:T(8,128)S(1)} custom-call(s32[4]{0:T(128)S(1)} %add_convert_fusion.flag_ref, f32[2,72,96,128]{3,2,1,0:T(8,128)S(1)} %copy-done.1, f32[1,256,256]{2,1,0:T(8,128)S(1)} %get-tuple-element.24.beside_ref, bf16[2,96,256]{2,1,0:T(8,128)(2,1)S(1)} %get-tuple-element.25.take_ref, ...), custom_call_target="tpu_custom_call", output_to_operand_aliasing={{}: (1, {})} | custom-call | flops 201326592 | bytes 8388608 | tf_op jit(solution)/shard_map/section/pallas_call | solution.py:403
  31.1 0.0 copy-start.2
  31.1 2.9 %copy-done.2 = f32[2,72,96,128]{3,2,1,0:T(8,128)} copy-done((f32[2,72,96,128]{3,2,1,0:T(8,128)}, f32[2,72,96,128]{3,2,1,0:T(8,128)S(1)}, u32[]{:S(2)}) %copy-start.2) | copy-done | bytes 7077912
  34.0 0.0 collective-permute-done.5.up_ref
  34.0 0.0 collective-permute-done.6.down_ref
  34.0 0.0 copy-done.4
  34.0 0.0 copy-start.3
  34.0 3.0 %copy-done.3 = f32[2,72,96,128]{3,2,1,0:T(8,128)S(1)} copy-done((f32[2,72,96,128]{3,2,1,0:T(8,128)S(1)}, f32[2,72,96,128]{3,2,1,0:T(8,128)}, u32[]{:S(2)}) %copy-start.3) | copy-done | bytes 7077912
  37.0 9.3 %substeps.1 = (f32[64,64,256]{2,1,0:T(8,128)}, f32[2,72,96,128]{3,2,1,0:T(8,128)S(1)}) custom-call(s32[4]{0:T(128)S(1)} %add_convert_fusion.flag_ref, f32[2,72,96,128]{3,2,1,0:T(8,128)S(1)} %copy-done.3, f32[1,256]{1,0:T(1,128)S(1)} %bitcast.10, bf16[272,256]{1,0:T(8,128)(2,1)S(1)} %collective-permute-done.5.up_ref, ...), custom_call_target="tpu_custom_call", output_to_operand_aliasing={{1}: (1, {})} | custom-call | flops 41943040 | bytes 8388608 | tf_op jit(solution)/shard_map/substeps/pallas_call | solution.py:505
Async XLA Ops:
  1.2 6.7 %collective-permute-start = (bf16[272,256]{1,0:T(8,128)(2,1)S(1)}, bf16[272,256]{1,0:T(8,128)(2,1)S(1)}, u32[]{:S(2)}, u32[]{:S(2)}) collective-permute-start(bf16[272,256]{1,0:T(8,128)(2,1)S(1)} %age_edges.1), channel_id=1, source_target_pairs={{0,1},{1,0},{2,3},{3,2},{4,5},{5,4},{6,7},{7,6},{8,9},{9,8},{10,11... | collective-permute-start | bytes 417800 | tf_op jit(solution)/shard_map/ppermute | solution.py:545
  8.0 10.1 %collective-permute-start.1 = (bf16[48,2176]{1,0:T(8,128)(2,1)S(1)}, bf16[48,2176]{1,0:T(8,128)(2,1)S(1)}, u32[]{:S(2)}, u32[]{:S(2)}) collective-permute-start(bf16[48,2176]{1,0:T(8,128)(2,1)S(1)} %get-tuple-element.31), channel_id=1, source_target_pairs={{0,8},{8,0},{16,24},{24,16},{1,9},{9,1},{17,25},{25,17},{2,10},{10... | collective-permute-start | bytes 626696 | tf_op jit(solution)/shard_map/ppermute | solution.py:550
  8.1 10.0 %collective-permute-start.4 = (bf16[48,2176]{1,0:T(8,128)(2,1)S(1)}, bf16[48,2176]{1,0:T(8,128)(2,1)S(1)}, u32[]{:S(2)}, u32[]{:S(2)}) collective-permute-start(bf16[48,2176]{1,0:T(8,128)(2,1)S(1)} %get-tuple-element.34), channel_id=1, source_target_pairs={{8,16},{16,8},{9,17},{17,9},{10,18},{18,10},{11,19},{19,11},{12,20... | collective-permute-start | bytes 626696 | tf_op jit(solution)/shard_map/ppermute | solution.py:550
  8.8 8.9 %collective-permute-start.2 = (bf16[16,2176]{1,0:T(8,128)(2,1)S(1)}, bf16[16,2176]{1,0:T(8,128)(2,1)S(1)}, u32[]{:S(2)}, u32[]{:S(2)}) collective-permute-start(bf16[16,2176]{1,0:T(8,128)(2,1)S(1)} %get-tuple-element.32), channel_id=1, source_target_pairs={{0,16},{8,24},{16,0},{24,8},{1,17},{9,25},{17,1},{25,9},{2,18},{10... | collective-permute-start | bytes 208904 | tf_op jit(solution)/shard_map/ppermute | solution.py:550
  12.2 5.9 %collective-permute-start.3 = (bf16[16,2176]{1,0:T(8,128)(2,1)S(1)}, bf16[16,2176]{1,0:T(8,128)(2,1)S(1)}, u32[]{:S(2)}, u32[]{:S(2)}) collective-permute-start(bf16[16,2176]{1,0:T(8,128)(2,1)S(1)} %get-tuple-element.33), channel_id=1, source_target_pairs={{0,24},{24,0},{1,25},{25,1},{2,26},{26,2},{3,27},{27,3},{4,28},{28... | collective-permute-start | bytes 208904 | tf_op jit(solution)/shard_map/ppermute | solution.py:550
  18.4 2.9 %copy-start = (f32[2,72,96,128]{3,2,1,0:T(8,128)}, f32[2,72,96,128]{3,2,1,0:T(8,128)S(1)}, u32[]{:S(2)}) copy-start(f32[2,72,96,128]{3,2,1,0:T(8,128)S(1)} %get-tuple-element.35.z_in) | copy-start | bytes 21233668
  21.3 12.7 %collective-permute-start.5 = (bf16[272,256]{1,0:T(8,128)(2,1)S(1)}, bf16[272,256]{1,0:T(8,128)(2,1)S(1)}, u32[]{:S(2)}, u32[]{:S(2)}) collective-permute-start(bf16[272,256]{1,0:T(8,128)(2,1)S(1)} %get-tuple-element.36), channel_id=1, source_target_pairs={{0,2},{2,4},{4,6},{1,3},{3,5},{5,7},{8,10},{10,12},{12,14},{9,11},... | collective-permute-start | bytes 417800 | tf_op jit(solution)/shard_map/ppermute | solution.py:553
  25.0 9.0 %collective-permute-start.6 = (bf16[272,256]{1,0:T(8,128)(2,1)S(1)}, bf16[272,256]{1,0:T(8,128)(2,1)S(1)}, u32[]{:S(2)}, u32[]{:S(2)}) collective-permute-start(bf16[272,256]{1,0:T(8,128)(2,1)S(1)} %get-tuple-element.37), channel_id=1, source_target_pairs={{2,0},{4,2},{6,4},{3,1},{5,3},{7,5},{10,8},{12,10},{14,12},{11,9},... | collective-permute-start | bytes 417800 | tf_op jit(solution)/shard_map/ppermute | solution.py:554
  26.4 3.0 %copy-start.1 = (f32[2,72,96,128]{3,2,1,0:T(8,128)S(1)}, f32[2,72,96,128]{3,2,1,0:T(8,128)}, u32[]{:S(2)}) copy-start(f32[2,72,96,128]{3,2,1,0:T(8,128)} %copy-done) | copy-start | bytes 21233668
  29.4 4.6 %copy-start.4 = (f32[256]{0:T(256)S(1)}, f32[256]{0:T(256)}, u32[]{:S(2)}) copy-start(f32[256]{0:T(256)} %param.13) | copy-start | bytes 3076
  31.1 2.9 %copy-start.2 = (f32[2,72,96,128]{3,2,1,0:T(8,128)}, f32[2,72,96,128]{3,2,1,0:T(8,128)S(1)}, u32[]{:S(2)}) copy-start(f32[2,72,96,128]{3,2,1,0:T(8,128)S(1)} %section.1.z_in) | copy-start | bytes 21233668
  34.0 3.0 %copy-start.3 = (f32[2,72,96,128]{3,2,1,0:T(8,128)S(1)}, f32[2,72,96,128]{3,2,1,0:T(8,128)}, u32[]{:S(2)}) copy-start(f32[2,72,96,128]{3,2,1,0:T(8,128)} %copy-done.2) | copy-start | bytes 21233668
where the time goes:
time: 46.6 us; the launch traced here: 46.3 us
  Pallas kernels  18.6 us (40%)
  starting transfers between devices  15.2 us (33%)
  local copies, waits for them, and re-layouts  11.8 us (25%)
  waiting for transfers between devices  0.5 us (1%)
    unnamed x10, local copies, waits for them, and re-layouts  11.8 us
    pallas_call x1, Pallas kernels, run_substeps(): pl.pallas_call(functools.partial(substeps_kernel, sides), out_shape=[jax....  9.27 us
    ppermute x4, starting transfers between devices, body(): lax.ppermute(x, 'cheb', list(pairs))  7.17 us
    ppermute x1, starting transfers between devices, body(): up = lax.ppermute(bottom, 'wear', [(i, i + 1) for i in range(n_wear - 1)])  3.73 us
    pallas_call x1, Pallas kernels, pack(): pl.pallas_call(functools.partial(pack_kernel, ranks), in_specs=[SMEM, ANY...  3.62 us
    ppermute x1, starting transfers between devices, body(): near = [lax.ppermute(edge[0], 'age', after + before)]  3 us
    pallas_call x1, Pallas kernels, local(): pl.pallas_call(functools.partial(local_kernel, sides), in_specs=[SMEM, VM...  2.44 us
    pallas_call x1, Pallas kernels, section(): pl.pallas_call(functools.partial(section_kernel, ranks, sides, wears, age...  1.65 us
  transfers between devices with their start and end apart: 7, of which 1 were waited for; matrix products, arithmetic and copies ran while one was open for 0% of the time, Pallas kernels for 17%

commit v1 on v0

v1 whole, which is shorter than its diff:
```python
import functools

import jax
import jax.numpy as jnp
import numpy as np
from jax import lax
from jax.experimental import pallas as pl
from jax.experimental.pallas import tpu as pltpu
from jax.sharding import PartitionSpec as P

SUBSTEPS = 4
HALO = SUBSTEPS

age_courant = 0.4
wear_spread = 0.1
coupling = 0.05
GAIN = 1.0 / coupling
START = coupling**SUBSTEPS

f32 = jnp.float32
bf16 = jnp.bfloat16


def operators(points):
    modes = np.arange(points)[:, None]
    nodes = np.arange(points)[None, :]
    angles = (modes * (2 * nodes + 1)) % (4 * points) * (np.pi / (2 * points))
    cosine, sine = np.cos(angles), np.sin(angles)
    analysis = np.where(modes == 0, 1.0, 2.0) / points * cosine
    wavenumber = modes / points
    return (-(wavenumber**2) * cosine).T @ analysis, (wavenumber * sine).T @ analysis


def arrived_rows(rank):
    return -(-rank // 16) * 16


@functools.lru_cache(maxsize=None)
def factors(points, devices):
    second, first = operators(points)
    size = points // devices
    parts = [slice(b * size, (b + 1) * size) for b in range(devices)]
    slots, found = [], {}
    for shift in range(1, devices):
        pairs, most = [], 0
        for c in range(devices):
            b = c ^ shift if devices & (devices - 1) == 0 else (c + shift) % devices
            joint = np.concatenate([second[parts[b], parts[c]], first[parts[b], parts[c]]])
            _, sizes, rows = np.linalg.svd(joint, full_matrices=False)
            rank = int((sizes > joint.shape[0] * np.finfo(np.float64).eps).sum())
            rank = -(-rank // 8) * 8
            basis = rows[:rank]
            found[c, b] = (basis, second[parts[b], parts[c]] @ basis.T, first[parts[b], parts[c]] @ basis.T)
            pairs.append((c, b))
            most = max(most, rank)
        slots.append((tuple(pairs), most))
    send = np.zeros((devices, sum(rank for _, rank in slots), size))
    wide = sum(arrived_rows(rank) for _, rank in slots)
    take_second = np.zeros((devices, 2, wide, size))
    take_first = np.zeros((devices, 2, wide, size))
    at = row = 0
    for pairs, rank in slots:
        whole = rank // 16 * 16
        for c, b in pairs:
            basis, left_second, left_first = (
                np.pad(x, ((0, rank - len(found[c, b][0])), (0, 0))) for x in (found[c, b][0], found[c, b][1].T, found[c, b][2].T)
            )
            send[c, at : at + rank] = basis
            for half in range(2):
                for take, left in ((take_second, left_second), (take_first, left_first)):
                    take[b, half, row : row + whole] = left[:whole]
                    place = row + whole + half * (rank - whole)
                    take[b, half, place : place + rank - whole] = left[whole:]
        at += rank
        row += arrived_rows(rank)
    own_second = np.stack([second[p, p].T for p in parts])
    own_first = np.stack([first[p, p].T for p in parts])
    return slots, send, take_second, take_first, own_second, own_first


ANY = pl.BlockSpec(memory_space=pl.ANY)
VMEM = pl.BlockSpec(memory_space=pltpu.VMEM)
SMEM = pl.BlockSpec(memory_space=pltpu.SMEM)
FIRST_WEAR, LAST_WEAR, FIRST_AGE, LAST_AGE, CHEB = range(5)
ROW0 = 16
HAZARD_ROWS = 16


def in_hbm(x):
    return pltpu.with_memory_space_constraint(x, pltpu.HBM)


def in_vmem(x):
    return pltpu.with_memory_space_constraint(x, pltpu.VMEM)


def params(mebibytes):
    return pltpu.CompilerParams(vmem_limit_bytes=mebibytes * 2**20)


def cost(flops, bytes_accessed):
    return pl.CostEstimate(flops=flops, bytes_accessed=bytes_accessed, transcendentals=0)


def edge_kernel(sides, flag_ref, u_hbm, hazard_hbm, *refs):
    out_refs, (tiles, hazard, sem) = refs[:sides], refs[sides:]
    wears, ages, size = u_hbm.shape
    copies = [pltpu.make_async_copy(hazard_hbm, hazard, sem.at[sides])]
    for i in range(sides):
        if sides == 1:
            start = pl.multiple_of(jnp.where(flag_ref[FIRST_AGE] == 1, ages - 8, 0), 8)
        else:
            start = (ages - 8, 0)[i]
        copies.append(pltpu.make_async_copy(u_hbm.at[:, pl.ds(start, 8)], tiles.at[i], sem.at[i]))
    for copy in copies:
        copy.start()
    for copy in copies:
        copy.wait()
    by_age = jnp.transpose(hazard[...])
    last, early = by_age[ages - HALO :], by_age[:HALO]
    for i, out_ref in enumerate(out_refs):
        for w in range(0, wears, 4):
            late = [tiles[i, w + j, 8 - HALO :] for j in range(4)]
            soon = [tiles[i, w + j, :HALO] for j in range(4)]
            late, soon = jnp.concatenate(late, axis=0), jnp.concatenate(soon, axis=0)
            if sides == 1:
                cells = jnp.where(flag_ref[FIRST_AGE] == 1, late, soon)
            else:
                cells = (late, soon)[i]
            out_ref[w * HALO : (w + 4) * HALO] = cells.astype(bf16)
        if sides == 1:
            exact = jnp.where(flag_ref[FIRST_AGE] == 1, last, early)
        else:
            exact = (last, early)[i]
        high = exact.astype(bf16).astype(f32)
        rows = jnp.concatenate([high, exact - high, jnp.zeros((HAZARD_ROWS - 2 * HALO, wears), f32)], axis=0)
        rows = jnp.concatenate([rows, jnp.zeros((HAZARD_ROWS, size - wears), f32)], axis=1)
        out_ref[wears * HALO :] = rows.astype(bf16)


def edges(flags, u, hazard, sides):
    wears, ages, size = u.shape
    return pl.pallas_call(
        functools.partial(edge_kernel, sides),
        in_specs=[SMEM, ANY, ANY],
        out_specs=[VMEM] * sides,
        out_shape=[jax.ShapeDtypeStruct((wears * HALO + HAZARD_ROWS, size), bf16)] * sides,
        scratch_shapes=[
            pltpu.VMEM((sides, wears, 8, size), f32),
            pltpu.VMEM((wears, ages), f32),
            pltpu.SemaphoreType.DMA((sides + 1,)),
        ],
        compiler_params=params(16),
        cost_estimate=cost(0, 8 * wears * 8 * size),
        name="age_edges",
    )(flags, in_hbm(u), in_hbm(hazard))


def pack_rows(ranks, halves):
    packed, row = [], 0
    for rank in ranks:
        cut = row + rank // 16 * 16
        pieces = [h[row:cut] for h in halves if cut > row]
        pieces += [h[cut : row + rank] for h in halves if cut < row + rank]
        packed.append(jnp.concatenate(pieces, axis=0).astype(bf16))
        row += rank
    return packed


def analyse(table, cells):
    return lax.dot_general(table, cells, (((1,), (1,)), ((), ())), preferred_element_type=f32)


def pack_kernel(ranks, flag_ref, u_hbm, send_hbm, *refs):
    q_refs, (u_ref, send, send_sem, u_sem) = refs[: len(ranks)], refs[len(ranks) :]
    _, wears, ages, size = u_ref.shape
    chunk = 4
    table = pltpu.make_async_copy(send_hbm.at[flag_ref[CHEB]], send, send_sem)
    table.start()
    loads = []
    for g in range(wears // chunk):
        rows = pl.ds(g * chunk, chunk)
        loads.append(pltpu.make_async_copy(u_hbm.at[:, rows], u_ref.at[:, rows], u_sem.at[g]))
        loads[-1].start()
    table.wait()
    for g in range(wears // chunk):
        loads[g].wait()
        halves = [
            analyse(send[...], u_ref[half, g * chunk : (g + 1) * chunk].reshape(chunk * ages, size).astype(bf16))
            for half in range(2)
        ]
        for q_ref, rows in zip(q_refs, pack_rows(ranks, halves)):
            q_ref[:, g * chunk * ages : (g + 1) * chunk * ages] = rows


def pack(flags, u4, send, ranks, extra):
    _, wears, ages, size = u4.shape
    cells = wears * ages
    return pl.pallas_call(
        functools.partial(pack_kernel, ranks),
        in_specs=[SMEM, ANY, ANY],
        out_specs=[VMEM] * (len(ranks) + 2),
        out_shape=[jax.ShapeDtypeStruct((2 * r, cells + extra), bf16) for r in ranks]
        + [pltpu.VMEM(u4.shape, f32), pltpu.VMEM(send.shape[1:], bf16)],
        scratch_shapes=[pltpu.SemaphoreType.DMA, pltpu.SemaphoreType.DMA((wears // 4,))],
        compiler_params=params(16),
        cost_estimate=cost(4 * cells * sum(ranks) * size, 8 * cells * size),
        name="pack_coefficients",
    )(flags, in_hbm(u4), in_hbm(send))


def pack_edges_kernel(ranks, sides, send_ref, *refs):
    edge_refs, q_refs = refs[:sides], refs[sides + len(ranks) :]
    count = edge_refs[0].shape[0] - HAZARD_ROWS
    halves = []
    for half in range(2):
        cells = [r[half * count // 2 : (half + 1) * count // 2] for r in edge_refs]
        halves.append(analyse(send_ref[...], jnp.concatenate(cells, axis=0)))
    for q_ref, rows in zip(q_refs, pack_rows(ranks, halves)):
        q_ref[:, q_ref.shape[1] - rows.shape[1] :] = rows


def pack_edges(send, near, q, ranks, sides):
    return pl.pallas_call(
        functools.partial(pack_edges_kernel, ranks, sides),
        in_specs=[VMEM] * (1 + sides + len(ranks)),
        out_specs=[VMEM] * len(ranks),
        out_shape=[jax.ShapeDtypeStruct(x.shape, x.dtype) for x in q],
        input_output_aliases={1 + sides + i: i for i in range(len(ranks))},
        compiler_params=params(16),
        cost_estimate=cost(0, 2**18),
        name="pack_edges",
    )(in_vmem(send), *near, *q)


def local_kernel(sides, flag_ref, u_ref, hazard_hbm, diffusion_hbm, drift_hbm, second_hbm, first_hbm, take_second_hbm,
                 take_first_hbm, *refs):
    edge_refs, refs = refs[:sides], refs[sides:]
    z, beside, ends, take, hazard, diffusion, drift, second, first, own, take_second, take_first, sem = refs
    halves, rows, _, _ = z.shape
    _, wears, ages, size = u_ref.shape
    at = flag_ref[CHEB]
    moves = (
        (second_hbm.at[at], second), (first_hbm.at[at], first), (diffusion_hbm.at[at], diffusion),
        (drift_hbm.at[at], drift), (hazard_hbm, hazard), (take_second_hbm.at[at], take_second),
        (take_first_hbm.at[at], take_first),
    )
    copies = [pltpu.make_async_copy(src, dst, sem.at[i]) for i, (src, dst) in enumerate(moves)]
    for copy in copies:
        copy.start()
    for l in range(halves):
        zero = jnp.zeros((rows, 16, 128), f32)
        z[l, :, :ROW0, :] = zero
        z[l, :, ROW0 + ages :, :] = zero
    for copy in copies:
        copy.wait()
    scaled, moved = START * diffusion[...], START * drift[...]
    own[...] = (second[...] * scaled + first[...] * moved).astype(bf16)
    take[...] = (take_second[...] * scaled + take_first[...] * moved).astype(bf16)
    keep = jnp.transpose(START - START * hazard[...])
    chunk = 4
    for w in range(0, 2 * wears, chunk):
        half, v = divmod(w, wears)
        u = u_ref[half, v : v + chunk].reshape(chunk * ages, size)
        rate = jnp.dot(u.astype(bf16), own[...], preferred_element_type=f32)
        for i in range(chunk):
            cells = slice(i * ages, (i + 1) * ages)
            value = rate[cells] + keep[:, w + i : w + i + 1] * u[cells]
            for l in range(halves):
                z[l, HALO + w + i, ROW0 : ROW0 + ages, :] = value[:, l * 128 : (l + 1) * 128]
            for e, start in enumerate((0, 2 * wears - HALO)):
                if start <= w + i < start + HALO:
                    ends[e, (w + i - start) * ages : (w + i - start + 1) * ages] = value
    for s, ref in enumerate(edge_refs):
        count = 2 * wears * HALO
        parts = ref[count:].astype(f32)
        near = START - START * (parts[:HALO, : 2 * wears] + parts[HALO : 2 * HALO, : 2 * wears])
        near = jnp.concatenate([near, near], axis=0)
        for w in range(0, 2 * wears, 4):
            place = slice(w * HALO, (w + 4) * HALO)
            u = ref[place]
            rate = jnp.dot(u, own[...], preferred_element_type=f32)
            columns = [
                jnp.broadcast_to(near[:HALO, w + j : w + j + 1], (HALO, size)) for j in range(4)
            ]
            beside[s, place] = rate + jnp.concatenate(columns, axis=0) * u.astype(f32)


def local(flags, u4, hazard, diffusion, drift, tables, near, sides):
    _, wears, ages, size = u4.shape
    cells = 2 * wears * ages
    wide = tables[2].shape[2]
    return pl.pallas_call(
        functools.partial(local_kernel, sides),
        in_specs=[SMEM, VMEM] + [ANY] * 7 + [VMEM] * sides,
        out_specs=[VMEM] * 4,
        out_shape=[
            pltpu.VMEM((size // 128, 2 * wears + 2 * HALO, ages + 32, 128), f32),
            pltpu.VMEM((sides, 2 * wears * HALO, size), f32),
            pltpu.VMEM((2, HALO * ages, size), f32),
            pltpu.VMEM((2, wide, size), bf16),
        ],
        scratch_shapes=[
            pltpu.VMEM(hazard.shape, f32),
            pltpu.VMEM((1, size), f32),
            pltpu.VMEM((1, size), f32),
            pltpu.VMEM((size, size), f32),
            pltpu.VMEM((size, size), f32),
            pltpu.VMEM((size, size), bf16),
            pltpu.VMEM((2, wide, size), f32),
            pltpu.VMEM((2, wide, size), f32),
            pltpu.SemaphoreType.DMA((7,)),
        ],
        compiler_params=params(16),
        cost_estimate=cost(2 * cells * size * size, 8 * cells * size),
        name="local_rate",
    )(flags, in_vmem(u4), *[in_hbm(x) for x in (hazard, diffusion, drift, *tables)], *near)


def arrived_tiles(ranks, q_refs, half, columns):
    tiles = []
    for rank, q in zip(ranks, q_refs):
        cut = rank // 16 * 16
        if cut:
            tiles.append(q[half * cut : (half + 1) * cut, columns])
        if rank > cut:
            tiles.append(q[2 * cut : 2 * rank, columns])
    return jnp.concatenate(tiles, axis=0)


def distant(ranks, q_refs, take_ref, half, columns):
    return lax.dot_general(
        arrived_tiles(ranks, q_refs, half, columns), take_ref[half], (((0,), (0,)), ((), ())),
        preferred_element_type=f32,
    )


def edge_columns(sides, main, each):
    return [slice(main + s * each, main + (s + 1) * each) for s in range(sides)]


def rows_kernel(ranks, sides, wears, ages, ends_ref, beside_ref, take_ref, *refs):
    q_refs, out_refs = refs[: len(ranks)], refs[len(ranks) :]
    main, each = wears // 2 * ages, wears // 2 * HALO
    corner = HALO * HALO
    for half, (start, out_ref) in enumerate(zip((0, wears - HALO), out_refs)):
        v = (start - half * wears // 2) * ages
        rate = distant(ranks, q_refs, take_ref, half, slice(v, v + HALO * ages))
        out_ref[: HALO * ages] = (rate + ends_ref[half]).astype(bf16)
        for s, columns in enumerate(edge_columns(sides, main, each)):
            first = 0 if half == 0 else each - corner
            rate = distant(ranks, q_refs, take_ref, half, columns)[first : first + corner]
            place = slice(start * HALO, start * HALO + corner)
            row = HALO * ages + s * corner
            out_ref[row : row + corner] = (rate + beside_ref[s, place]).astype(bf16)


def outer_rows(ends, beside, take, q, ranks, sides, wears, ages):
    size = ends.shape[-1]
    message = jax.ShapeDtypeStruct((HALO * ages + sides * HALO * HALO, size), bf16)
    return pl.pallas_call(
        functools.partial(rows_kernel, ranks, sides, wears, ages),
        in_specs=[VMEM] * (3 + len(ranks)),
        out_specs=[VMEM] * 2,
        out_shape=[message, message],
        compiler_params=params(16),
        cost_estimate=cost(2 * 8 * ages * take.shape[1] * size, 2**20),
        name="outer_rows",
    )(in_vmem(ends), in_vmem(beside), in_vmem(take), *q)


def section_kernel(ranks, sides, wears, ages, flag_ref, z_in, beside_ref, take_ref, *refs):
    q_refs, (z,) = refs[: len(ranks)], refs[len(ranks) :]
    halves = z.shape[0]
    main, each = wears // 2 * ages, wears // 2 * HALO
    chunk = 4
    for w in range(0, wears, chunk):
        half, v = divmod(w, wears // 2)
        rate = distant(ranks, q_refs, take_ref, half, slice(v * ages, (v + chunk) * ages))
        for i in range(chunk):
            for l in range(halves):
                z[l, HALO + w + i, ROW0 : ROW0 + ages, :] = (
                    z_in[l, HALO + w + i, ROW0 : ROW0 + ages, :]
                    + rate[i * ages : (i + 1) * ages, l * 128 : (l + 1) * 128]
                )
    has = [jnp.where(flag_ref[FIRST_AGE + i] == 1, 0.0, 1.0).astype(f32) for i in range(2)]
    for s in range(sides):
        for half in range(2):
            columns = edge_columns(sides, main, each)[s]
            place = slice(half * each, (half + 1) * each)
            cells = distant(ranks, q_refs, take_ref, half, columns) + beside_ref[s, place]
            for i, column in ((0, ROW0 - HALO), (1, ROW0 + ages)):
                if sides == 1 or s == i:
                    part = cells * has[i]
                    for w in range(wears // 2):
                        for l in range(halves):
                            z[l, HALO + half * wears // 2 + w, column : column + HALO, :] = part[
                                w * HALO : (w + 1) * HALO, l * 128 : (l + 1) * 128
                            ]


def section(flags, z, beside, take, q, ranks, sides, wears, ages):
    size = z.shape[0] * 128
    cells = wears * ages
    return pl.pallas_call(
        functools.partial(section_kernel, ranks, sides, wears, ages),
        in_specs=[SMEM] + [VMEM] * (3 + len(ranks)),
        out_specs=VMEM,
        out_shape=pltpu.VMEM(z.shape, f32),
        input_output_aliases={1: 0},
        compiler_params=params(16),
        cost_estimate=cost(2 * cells * take.shape[1] * size, 8 * cells * size),
        name="section",
    )(flags, z, in_vmem(beside), in_vmem(take), *q)


def lane_terms(speed_ref, l):
    speed = speed_ref[0:1, l * 128 : (l + 1) * 128]
    stay = GAIN * (1.0 - age_courant - 2.0 * wear_spread - speed)
    worn = GAIN * (speed + wear_spread)
    return stay, worn


def row_terms(src, l, w, lo, hi, stay, worn):
    t = src[l, w, lo:hi, :]
    older = src[l, w, lo + 1 : hi + 1, :]
    slope = older - src[l, w, lo - 1 : hi - 1, :]
    centre = stay * t + (GAIN * age_courant) * older
    less = (t - slope) + t
    return centre, worn * t + slope, less


def rows_step(src, l, start, stop, lo, hi, factors, put, unroll):
    def step(w, carry):
        partial, less = carry
        centre, more, new_less = row_terms(src, l, w + 1, lo, hi, *factors)
        put(w, partial + more)
        return centre + less, new_less

    _, _, less0 = row_terms(src, l, start - 1, lo, hi, *factors)
    centre1, _, less1 = row_terms(src, l, start, lo, hi, *factors)
    lax.fori_loop(start, stop, step, (centre1 + less0, less1), unroll=unroll)


def put_in(dst, l, lo, hi, keeps, factor=None):
    def put(w, out):
        if factor is not None:
            out = out * factor(w)
        if keeps is None:
            dst[l, w, lo:hi, :] = out
        else:
            dst[l, w, lo : lo + 8, :] = out[:8] * keeps[0]
            dst[l, w, lo + 8 : hi - 8, :] = out[8:-8]
            dst[l, w, hi - 8 : hi, :] = out[-8:] * keeps[1]

    return put


def by_sides(sides, flag_ref, ages, run):
    if sides == 1:
        pl.when(flag_ref[FIRST_AGE] == 1)(lambda: run(ROW0, ROW0 + ages + 8, None))
        pl.when(flag_ref[FIRST_AGE] == 0)(lambda: run(ROW0 - 8, ROW0 + ages, None))
    else:
        has = [jnp.where(flag_ref[FIRST_AGE + i] == 1, 0.0, 1.0).astype(f32) for i in range(2)]
        run(ROW0 - 8, ROW0 + ages + 8, [jnp.zeros((8, 128), f32) + h for h in has])


def inner_kernel(sides, flag_ref, z0, speed_ref, o_ref, z1, z2, z3, stage, out_sem):
    halves, rows, _, _ = z0.shape
    count, ages = stage.shape[:2]
    fields = (z0, z1, z2, z3)

    def run(low, high, keeps):
        for z in fields[1:]:
            for l in range(halves):
                if low == ROW0:
                    z[l, :, ROW0 - 8 : ROW0, :] = jnp.zeros((rows, 8, 128), f32)
                if high == ROW0 + ages:
                    z[l, :, high : high + 8, :] = jnp.zeros((rows, 8, 128), f32)
        for k in range(1, SUBSTEPS):
            for l in range(halves):
                rows_step(
                    fields[k - 1], l, HALO + k, rows - HALO - k, low, high, lane_terms(speed_ref, l),
                    put_in(fields[k], l, low, high, keeps), 2,
                )
        stores = []
        first = HALO + SUBSTEPS
        bounds = [0, count * 3 // 7, count * 5 // 7, count * 6 // 7, count]
        for a, b in zip(bounds, bounds[1:]):
            for l in range(halves):
                def put(w, out, l=l):
                    stage[w - first, :, l * 128 : (l + 1) * 128] = out

                rows_step(
                    fields[-1], l, first + a, first + b, ROW0, ROW0 + ages, lane_terms(speed_ref, l), put, 4,
                )
            copy = pltpu.make_async_copy(
                stage.at[pl.ds(a, b - a)], o_ref.at[pl.ds(SUBSTEPS + a, b - a)], out_sem.at[len(stores)]
            )
            copy.start()
            stores.append(copy)
        for copy in stores:
            copy.wait()

    by_sides(sides, flag_ref, ages, run)


def inner_substeps(flags, z, speed, sides, wears, ages):
    size = z.shape[0] * 128
    shape = (wears, ages, size)
    return pl.pallas_call(
        functools.partial(inner_kernel, sides),
        out_shape=[jax.ShapeDtypeStruct(shape, f32)] + [pltpu.VMEM(z.shape, f32)] * 3,
        in_specs=[SMEM] + [VMEM] * 2,
        out_specs=[ANY] + [VMEM] * 3,
        scratch_shapes=[pltpu.VMEM((wears - 2 * SUBSTEPS, ages, size), f32), pltpu.SemaphoreType.DMA((4,))],
        compiler_params=params(16),
        cost_estimate=cost(10 * SUBSTEPS * wears * ages * size, 8 * wears * ages * size),
        name="inner_substeps",
    )(flags, in_vmem(z), speed)


def outer_kernel(sides, flag_ref, o_in, z0_in, z1_in, z2_in, z3_in, speed_ref, up_ref, down_ref, o_ref, z0, z1, z2, z3,
                 stage, out_sem):
    del o_in, z0_in, z1_in, z2_in, z3_in
    halves, rows, _, _ = z0.shape
    wears, ages = rows - 2 * HALO, stage.shape[2]
    fields = (z0, z1, z2, z3)
    has = [jnp.where(flag_ref[FIRST_AGE + i] == 1, 0.0, 1.0).astype(f32) for i in range(2)]
    near = [jnp.where(flag_ref[FIRST_WEAR + i] == 1, 0.0, 1.0).astype(f32) for i in range(2)]
    for l in range(halves):
        lanes = pl.ds(l * 128, 128)
        for e, (ref, at) in enumerate(((up_ref, 0), (down_ref, HALO + wears))):
            values = ref[:, lanes].astype(f32) * near[e]
            z0[l, at : at + HALO, ROW0 : ROW0 + ages, :] = values[: HALO * ages].reshape(HALO, ages, 128)
            for s in range(sides):
                corner = values[HALO * (ages + s * HALO) : HALO * (ages + (s + 1) * HALO)]
                for i, column in ((0, ROW0 - HALO), (1, ROW0 + ages)):
                    if sides == 1 or s == i:
                        part = corner * has[i]
                        for w in range(HALO):
                            z0[l, at + w, column : column + HALO, :] = part[w * HALO : (w + 1) * HALO]

    def run(low, high, keeps):
        for k in range(1, SUBSTEPS):
            for l in range(halves):
                for e, start in enumerate((k, rows - HALO - k)):
                    beyond = (lambda w: w < HALO, lambda w: w >= HALO + wears)[e]
                    rows_step(
                        fields[k - 1], l, start, start + HALO, low, high, lane_terms(speed_ref, l),
                        put_in(
                            fields[k], l, low, high, keeps,
                            lambda w, e=e, beyond=beyond: jnp.where(beyond(w), near[e], 1.0).astype(f32),
                        ), 4,
                    )
        stores = []
        for e, start in enumerate((HALO, rows - 2 * HALO)):
            for l in range(halves):
                def put(w, out, l=l, e=e, start=start):
                    stage[e, w - start, :, l * 128 : (l + 1) * 128] = out

                rows_step(fields[-1], l, start, start + HALO, ROW0, ROW0 + ages, lane_terms(speed_ref, l), put, 4)
            copy = pltpu.make_async_copy(stage.at[e], o_ref.at[pl.ds(start - HALO, HALO)], out_sem.at[e])
            copy.start()
            stores.append(copy)
        for copy in stores:
            copy.wait()

    by_sides(sides, flag_ref, ages, run)


def outer_substeps(flags, o, fields, speed, up, down, sides):
    wears, ages, size = o.shape
    return pl.pallas_call(
        functools.partial(outer_kernel, sides),
        out_shape=[jax.ShapeDtypeStruct(o.shape, f32)] + [pltpu.VMEM(z.shape, f32) for z in fields],
        in_specs=[SMEM, ANY] + [VMEM] * 7,
        out_specs=[ANY] + [VMEM] * 4,
        scratch_shapes=[pltpu.VMEM((2, HALO, ages, size), f32), pltpu.SemaphoreType.DMA((2,))],
        input_output_aliases={1 + i: i for i in range(5)},
        compiler_params=params(16),
        cost_estimate=cost(20 * SUBSTEPS * 2 * HALO * ages * size, 2**20),
        name="outer_substeps",
    )(flags, o, *fields, speed, up, down)[0]


def body(adjoint_value, load_diffusion, load_drift, wear_speed, hazard):
    wears, ages, size = adjoint_value.shape
    points = load_diffusion.shape[0]
    devices = points // size
    slots, send, take_second, take_first, own_second, own_first = factors(points, devices)
    ranks = tuple(rank for _, rank in slots)
    cheb = lax.axis_index("cheb")
    wear, age = lax.axis_index("wear"), lax.axis_index("age")
    n_wear, n_age = lax.axis_size("wear"), lax.axis_size("age")
    flags = jnp.stack([wear == 0, wear == n_wear - 1, age == 0, age == n_age - 1, cheb]).astype(jnp.int32)
    sides = 1 if n_age == 2 else 2
    extra = sides * wears // 2 * HALO
    u4 = adjoint_value.reshape(2, wears // 2, ages, size)
    diffusion = load_diffusion.reshape(devices, 1, size)
    drift = load_drift.reshape(devices, 1, size)
    tables = [jnp.asarray(t, f32) for t in (own_second, own_first, take_second, take_first)]

    def ring(n):
        after = [(i, (i + 1) % n) for i in range(n)]
        return after, [(j, i) for i, j in after]

    edge = edges(flags, adjoint_value, hazard, sides)
    near = [lax.ppermute(x, "age", pairs) for x, pairs in zip(edge, ring(n_age))]
    *q, u4, send = pack(flags, u4, jnp.asarray(send, bf16), ranks, extra)
    q = pack_edges(send, near, q, ranks, sides)
    arrived = [lax.ppermute(x, "cheb", list(pairs)) for x, (pairs, _) in zip(q, slots)]
    z, beside, ends, take = local(flags, u4, hazard, diffusion, drift, tables, near, sides)
    top, bottom = outer_rows(ends, beside, take, arrived, ranks, sides, wears, ages)
    after, before = ring(n_wear)
    up, down = lax.ppermute(bottom, "wear", after), lax.ppermute(top, "wear", before)
    z = section(flags, z, beside, take, arrived, ranks, sides, wears, ages)
    speed = wear_speed.reshape(1, size)
    o, *fields = inner_substeps(flags, z, speed, sides, wears, ages)
    return outer_substeps(flags, o, [z, *fields], speed, up, down, sides)


def solution(mesh):
    placed = (P("wear", "age", "cheb"), P(), P(), P("cheb"), P("wear", "age"))
    return jax.shard_map(
        body, mesh=mesh, in_specs=placed, out_specs=P("wear", "age", "cheb"), check_vma=False
    )
```

time: 46.6 us -> 35.2 us (0.76)
  local copies, waits for them, and re-layouts: 11.8 us -> 0.09 us
  starting transfers between devices: 15.2 us -> 9.09 us
  waiting for transfers between devices: 0.5 us -> 3.91 us
  Pallas kernels: 18.6 us -> 21.9 us
    unnamed x10 -> x2, local copies, waits for them, and re-layouts: 11.8 us -> 0.01 us
    ppermute x4 -> x3, starting transfers between devices: 7.17 us -> 2.21 us  [body(): lax.ppermute(x, 'cheb', list(pairs))]
    ppermute x4 -> x3, waiting for transfers between devices: 0.46 us -> 3.9 us  [body(): lax.ppermute(x, 'cheb', list(pairs))]
    pallas_call x1 -> x2, Pallas kernels: 9.27 us -> 10.8 us  [the longest x1 8.54 us: inner_substeps(): pl.pallas_call(functools.partial(inner_kernel, sides), out_shape=[jax.Sha...]
    ppermute x3, starting transfers between devices: 8.02 us -> 6.88 us  [the longest x1 3 us: body(): lax.ppermute(x, 'age', pairs)]
    pallas_call x1, Pallas kernels: 3.62 us -> 4.3 us  [pack(): pl.pallas_call(functools.partial(pack_kernel, ranks), in_specs=[SMEM, ANY...]
    pallas_call x1, Pallas kernels: 1.17 us -> 1.71 us  [edges(): pl.pallas_call(functools.partial(edge_kernel, sides), in_specs=[SMEM, ANY...]
    pallas_call x1, Pallas kernels: 2.44 us -> 2.98 us  [local(): pl.pallas_call(functools.partial(local_kernel, sides), in_specs=[SMEM, VM...]
  transfers between devices with their start and end apart: 7 -> 6, of which waited for: 1 -> 1; matrix products, arithmetic and copies ran while one was open for 0% -> 0% of each run, Pallas kernels for 17% -> 50%
where the time goes in v1:
time: 35.2 us; the launch traced here: 35.1 us
  Pallas kernels  21.9 us (62%)
  starting transfers between devices  9.09 us (26%)
  waiting for transfers between devices  3.91 us (11%)
    pallas_call x1, Pallas kernels, inner_substeps(): pl.pallas_call(functools.partial(inner_kernel, sides), out_shape=[jax.Sha...  8.54 us
    pallas_call x1, Pallas kernels, pack(): pl.pallas_call(functools.partial(pack_kernel, ranks), in_specs=[SMEM, ANY...  4.3 us
    ppermute x3, waiting for transfers between devices, body(): lax.ppermute(x, 'cheb', list(pairs))  3.9 us
    ppermute x1, starting transfers between devices, body(): lax.ppermute(x, 'age', pairs)  3 us
    pallas_call x1, Pallas kernels, local(): pl.pallas_call(functools.partial(local_kernel, sides), in_specs=[SMEM, VM...  2.98 us
    ppermute x1, starting transfers between devices, body(): lax.ppermute(top, 'wear', before)  2.25 us
    pallas_call x1, Pallas kernels, outer_substeps(): pl.pallas_call(functools.partial(outer_kernel, sides), out_shape=[jax.Sha...  2.22 us
    ppermute x3, starting transfers between devices, body(): lax.ppermute(x, 'cheb', list(pairs))  2.21 us
  transfers between devices with their start and end apart: 6, of which 1 were waited for; matrix products, arithmetic and copies ran while one was open for 0% of the time, Pallas kernels for 50%

profile of v1, /device:TPU:0, one launch (start us, length us, event | category | flops | bytes accessed | tf_op | source)
XLA Modules:
  0.0 35.1 jit_solution(3122279640861480421)
XLA Ops:
  0.0 0.1 stack.39.flag_ref
  0.1 1.7 %age_edges.1 = bf16[272,256]{1,0:T(8,128)(2,1)S(1)} custom-call(s32[5]{0:T(128)S(1)} %stack.39.flag_ref, f32[64,64,256]{2,1,0:T(8,128)} %u_hbm.1, f32[64,64]{1,0:T(8,128)} %hazard_hbm.3), custom_call_target="tpu_custom_call" | custom-call | bytes 1048576 | tf_op jit(solution)/shard_map/age_edges/pallas_call | solution.py:143
  1.8 3.0 %collective-permute-start = (bf16[272,256]{1,0:T(8,128)(2,1)S(1)}, bf16[272,256]{1,0:T(8,128)(2,1)S(1)}, u32[]{:S(2)}, u32[]{:S(2)}) collective-permute-start(bf16[272,256]{1,0:T(8,128)(2,1)S(1)} %age_edges.1), channel_id=1, source_target_pairs={{0,1},{1,0},{2,3},{3,2},{4,5},{5,4},{6,7},{7,6},{8,9},{9,8},{10,11... | collective-permute-start | bytes 417800 | tf_op jit(solution)/shard_map/ppermute | solution.py:609
  4.8 4.3 %pack_coefficients.1 = (bf16[48,2176]{1,0:T(8,128)(2,1)S(1)}, bf16[16,2176]{1,0:T(8,128)(2,1)S(1)}, bf16[48,2176]{1,0:T(8,128)(2,1)S(1)}, f32[2,32,64,256]{3,2,1,0:T(8,128)S(1)}, bf16[56,256]{1,0:T(8,128)(2,1)S(1)}) custom-call(s32[5]{0:T(128)S(1)} %stack.39.flag_ref, f32[2,32,64,256]{3,2,1,0:T(8,128)} %bitcast.11, bf16[4,56,256]{2,1,0:T(8,128)(2,1)} %constant.31.clone.send_hbm), custom_call_target="tpu_custom_call" | custom-call | flops 117440512 | bytes 4194304 | tf_op jit(solution)/shard_map/pack_coefficients/pallas_call | solution.py:199
  9.1 0.0 collective-permute-done.refs_0_
  9.1 0.2 pack_edges.1
  9.3 0.1 collective-permute-start.1
  9.4 1.6 %collective-permute-start.3 = (bf16[48,2176]{1,0:T(8,128)(2,1)S(1)}, bf16[48,2176]{1,0:T(8,128)(2,1)S(1)}, u32[]{:S(2)}, u32[]{:S(2)}) collective-permute-start(bf16[48,2176]{1,0:T(8,128)(2,1)S(1)} %get-tuple-element.34), channel_id=1, source_target_pairs={{0,24},{8,16},{16,8},{24,0},{1,25},{9,17},{17,9},{25,1},{2,26},{10... | collective-permute-start | bytes 626696 | tf_op jit(solution)/shard_map/ppermute | solution.py:612
  11.0 0.5 %collective-permute-start.2 = (bf16[16,2176]{1,0:T(8,128)(2,1)S(1)}, bf16[16,2176]{1,0:T(8,128)(2,1)S(1)}, u32[]{:S(2)}, u32[]{:S(2)}) collective-permute-start(bf16[16,2176]{1,0:T(8,128)(2,1)S(1)} %get-tuple-element.33), channel_id=1, source_target_pairs={{0,16},{8,24},{16,0},{24,8},{1,17},{9,25},{17,1},{25,9},{2,18},{10... | collective-permute-start | bytes 208904 | tf_op jit(solution)/shard_map/ppermute | solution.py:612
  11.5 3.0 %local_rate.1 = (f32[2,72,96,128]{3,2,1,0:T(8,128)S(1)}, f32[1,256,256]{2,1,0:T(8,128)S(1)}, f32[2,256,256]{2,1,0:T(8,128)S(1)}, bf16[2,80,256]{2,1,0:T(8,128)(2,1)S(1)}) custom-call(s32[5]{0:T(128)S(1)} %stack.39.flag_ref, f32[2,32,64,256]{3,2,1,0:T(8,128)S(1)} %get-tuple-element.24.u_ref, f32[64,64]{1,0:T(8,128)} %hazard_hbm.3, f32[4,1,256]{2,1,0:T(1,128)} %bitcast.12, ...), custom_call_target="tpu_custom_call" | custom-call | flops 536870912 | bytes 8388608 | tf_op jit(solution)/shard_map/local_rate/pallas_call | solution.py:293
  14.5 3.9 %collective-permute-done.2.refs_1_ = bf16[16,2176]{1,0:T(8,128)(2,1)S(1)} collective-permute-done((bf16[16,2176]{1,0:T(8,128)(2,1)S(1)}, bf16[16,2176]{1,0:T(8,128)(2,1)S(1)}, u32[]{:S(2)}, u32[]{:S(2)}) %collective-permute-start.2) | collective-permute-done | bytes 69664 | tf_op jit(solution)/shard_map/ppermute | solution.py:612
  18.4 0.0 collective-permute-done.1.refs_0_
  18.4 0.0 collective-permute-done.3.refs_2_
  18.4 0.3 outer_rows.1
  18.7 1.6 %collective-permute-start.4 = (bf16[272,256]{1,0:T(8,128)(2,1)S(1)}, bf16[272,256]{1,0:T(8,128)(2,1)S(1)}, u32[]{:S(2)}, u32[]{:S(2)}) collective-permute-start(bf16[272,256]{1,0:T(8,128)(2,1)S(1)} %get-tuple-element.40), channel_id=1, source_target_pairs={{0,2},{2,4},{4,6},{6,0},{1,3},{3,5},{5,7},{7,1},{8,10},{10,12},{12... | collective-permute-start | bytes 417800 | tf_op jit(solution)/shard_map/ppermute | solution.py:616
  20.3 2.2 %collective-permute-start.5 = (bf16[272,256]{1,0:T(8,128)(2,1)S(1)}, bf16[272,256]{1,0:T(8,128)(2,1)S(1)}, u32[]{:S(2)}, u32[]{:S(2)}) collective-permute-start(bf16[272,256]{1,0:T(8,128)(2,1)S(1)} %get-tuple-element.41), channel_id=1, source_target_pairs={{2,0},{4,2},{6,4},{0,6},{3,1},{5,3},{7,5},{1,7},{10,8},{12,10},{14... | collective-permute-start | bytes 417800 | tf_op jit(solution)/shard_map/ppermute | solution.py:616
  22.6 0.0 copy-start
  22.6 1.7 %section.1.z0.z0_in = f32[2,72,96,128]{3,2,1,0:T(8,128)S(1)} custom-call(s32[5]{0:T(128)S(1)} %stack.39.flag_ref, f32[2,72,96,128]{3,2,1,0:T(8,128)S(1)} %get-tuple-element.25.z_in, f32[1,256,256]{2,1,0:T(8,128)S(1)} %get-tuple-element.26.beside_ref, bf16[2,80,256]{2,1,0:T(8,128)(2,1)S(1)} %get-tuple-element.27.take_ref, ...), custom_call_target="tpu_custom_call", output_to_operand_aliasing={{}: (1, {})} | custom-call | flops 167772160 | bytes 8388608 | tf_op jit(solution)/shard_map/section/pallas_call | solution.py:405
  24.3 0.0 copy-done
  24.3 8.5 %inner_substeps.1 = (f32[64,64,256]{2,1,0:T(8,128)}, f32[2,72,96,128]{3,2,1,0:T(8,128)S(1)}, f32[2,72,96,128]{3,2,1,0:T(8,128)S(1)}, f32[2,72,96,128]{3,2,1,0:T(8,128)S(1)}) custom-call(s32[5]{0:T(128)S(1)} %stack.39.flag_ref, f32[2,72,96,128]{3,2,1,0:T(8,128)S(1)} %section.1.z0.z0_in, f32[1,256]{1,0:T(1,128)S(1)} %bitcast.9), custom_call_target="tpu_custom_call" | custom-call | flops 41943040 | bytes 8388608 | tf_op jit(solution)/shard_map/inner_substeps/pallas_call | solution.py:511
  32.8 0.0 collective-permute-done.4.up_ref
  32.8 0.0 collective-permute-done.5.down_ref
  32.9 2.2 %outer_substeps.1 = (f32[64,64,256]{2,1,0:T(8,128)}, f32[2,72,96,128]{3,2,1,0:T(8,128)S(1)}, f32[2,72,96,128]{3,2,1,0:T(8,128)S(1)}, f32[2,72,96,128]{3,2,1,0:T(8,128)S(1)}, f32[2,72,96,128]{3,2,1,0:T(8,128)S(1)}) custom-call(s32[5]{0:T(128)S(1)} %stack.39.flag_ref, ...), custom_call_target="tpu_custom_call", output_to_operand_aliasing={{0}: (1, {}), {1}: (2, {}), {2}: (3, {}), {3}: (4, {}), {4}... | custom-call | flops 10485760 | bytes 1048576 | tf_op jit(solution)/shard_map/outer_substeps/pallas_call | solution.py:574
Async XLA Ops:
  1.8 7.3 %collective-permute-start = (bf16[272,256]{1,0:T(8,128)(2,1)S(1)}, bf16[272,256]{1,0:T(8,128)(2,1)S(1)}, u32[]{:S(2)}, u32[]{:S(2)}) collective-permute-start(bf16[272,256]{1,0:T(8,128)(2,1)S(1)} %age_edges.1), channel_id=1, source_target_pairs={{0,1},{1,0},{2,3},{3,2},{4,5},{5,4},{6,7},{7,6},{8,9},{9,8},{10,11... | collective-permute-start | bytes 417800 | tf_op jit(solution)/shard_map/ppermute | solution.py:609
  9.3 9.1 %collective-permute-start.1 = (bf16[48,2176]{1,0:T(8,128)(2,1)S(1)}, bf16[48,2176]{1,0:T(8,128)(2,1)S(1)}, u32[]{:S(2)}, u32[]{:S(2)}) collective-permute-start(bf16[48,2176]{1,0:T(8,128)(2,1)S(1)} %get-tuple-element.32), channel_id=1, source_target_pairs={{0,8},{8,0},{16,24},{24,16},{1,9},{9,1},{17,25},{25,17},{2,10},{10... | collective-permute-start | bytes 626696 | tf_op jit(solution)/shard_map/ppermute | solution.py:612
  9.4 9.0 %collective-permute-start.3 = (bf16[48,2176]{1,0:T(8,128)(2,1)S(1)}, bf16[48,2176]{1,0:T(8,128)(2,1)S(1)}, u32[]{:S(2)}, u32[]{:S(2)}) collective-permute-start(bf16[48,2176]{1,0:T(8,128)(2,1)S(1)} %get-tuple-element.34), channel_id=1, source_target_pairs={{0,24},{8,16},{16,8},{24,0},{1,25},{9,17},{17,9},{25,1},{2,26},{10... | collective-permute-start | bytes 626696 | tf_op jit(solution)/shard_map/ppermute | solution.py:612
  11.0 7.4 %collective-permute-start.2 = (bf16[16,2176]{1,0:T(8,128)(2,1)S(1)}, bf16[16,2176]{1,0:T(8,128)(2,1)S(1)}, u32[]{:S(2)}, u32[]{:S(2)}) collective-permute-start(bf16[16,2176]{1,0:T(8,128)(2,1)S(1)} %get-tuple-element.33), channel_id=1, source_target_pairs={{0,16},{8,24},{16,0},{24,8},{1,17},{9,25},{17,1},{25,9},{2,18},{10... | collective-permute-start | bytes 208904 | tf_op jit(solution)/shard_map/ppermute | solution.py:612
  18.7 14.1 %collective-permute-start.4 = (bf16[272,256]{1,0:T(8,128)(2,1)S(1)}, bf16[272,256]{1,0:T(8,128)(2,1)S(1)}, u32[]{:S(2)}, u32[]{:S(2)}) collective-permute-start(bf16[272,256]{1,0:T(8,128)(2,1)S(1)} %get-tuple-element.40), channel_id=1, source_target_pairs={{0,2},{2,4},{4,6},{6,0},{1,3},{3,5},{5,7},{7,1},{8,10},{10,12},{12... | collective-permute-start | bytes 417800 | tf_op jit(solution)/shard_map/ppermute | solution.py:616
  20.3 12.5 %collective-permute-start.5 = (bf16[272,256]{1,0:T(8,128)(2,1)S(1)}, bf16[272,256]{1,0:T(8,128)(2,1)S(1)}, u32[]{:S(2)}, u32[]{:S(2)}) collective-permute-start(bf16[272,256]{1,0:T(8,128)(2,1)S(1)} %get-tuple-element.41), channel_id=1, source_target_pairs={{2,0},{4,2},{6,4},{0,6},{3,1},{5,3},{7,5},{1,7},{10,8},{12,10},{14... | collective-permute-start | bytes 417800 | tf_op jit(solution)/shard_map/ppermute | solution.py:616
  22.6 1.7 %copy-start = (f32[256]{0:T(256)S(1)}, f32[256]{0:T(256)}, u32[]{:S(2)}) copy-start(f32[256]{0:T(256)} %param.13) | copy-start | bytes 3076

commit v2 on v1

--- a/solution.py
+++ b/solution.py
@@ -81,11 +81,14 @@
 ANY = pl.BlockSpec(memory_space=pl.ANY)
 VMEM = pl.BlockSpec(memory_space=pltpu.VMEM)
 SMEM = pl.BlockSpec(memory_space=pltpu.SMEM)
-FIRST_WEAR, LAST_WEAR, FIRST_AGE, LAST_AGE, CHEB = range(5)
 ROW0 = 16
 HAZARD_ROWS = 16
 
 
+def at_end(axis, last):
+    return lax.axis_index(axis) == (lax.axis_size(axis) - 1 if last else 0)
+
+
 def in_hbm(x):
     return pltpu.with_memory_space_constraint(x, pltpu.HBM)
 
@@ -102,13 +105,13 @@
     return pl.CostEstimate(flops=flops, bytes_accessed=bytes_accessed, transcendentals=0)
 
 
-def edge_kernel(sides, flag_ref, u_hbm, hazard_hbm, *refs):
+def edge_kernel(sides, u_hbm, hazard_hbm, *refs):
     out_refs, (tiles, hazard, sem) = refs[:sides], refs[sides:]
     wears, ages, size = u_hbm.shape
     copies = [pltpu.make_async_copy(hazard_hbm, hazard, sem.at[sides])]
     for i in range(sides):
         if sides == 1:
-            start = pl.multiple_of(jnp.where(flag_ref[FIRST_AGE] == 1, ages - 8, 0), 8)
+            start = pl.multiple_of(jnp.where(at_end("age", False), ages - 8, 0), 8)
         else:
             start = (ages - 8, 0)[i]
         copies.append(pltpu.make_async_copy(u_hbm.at[:, pl.ds(start, 8)], tiles.at[i], sem.at[i]))
@@ -124,12 +127,12 @@
             soon = [tiles[i, w + j, :HALO] for j in range(4)]
             late, soon = jnp.concatenate(late, axis=0), jnp.concatenate(soon, axis=0)
             if sides == 1:
-                cells = jnp.where(flag_ref[FIRST_AGE] == 1, late, soon)
+                cells = jnp.where(at_end("age", False), late, soon)
             else:
                 cells = (late, soon)[i]
             out_ref[w * HALO : (w + 4) * HALO] = cells.astype(bf16)
         if sides == 1:
-            exact = jnp.where(flag_ref[FIRST_AGE] == 1, last, early)
+            exact = jnp.where(at_end("age", False), last, early)
         else:
             exact = (last, early)[i]
         high = exact.astype(bf16).astype(f32)
@@ -138,11 +141,11 @@
         out_ref[wears * HALO :] = rows.astype(bf16)
 
 
-def edges(flags, u, hazard, sides):
+def edges(u, hazard, sides):
     wears, ages, size = u.shape
     return pl.pallas_call(
         functools.partial(edge_kernel, sides),
-        in_specs=[SMEM, ANY, ANY],
+        in_specs=[ANY, ANY],
         out_specs=[VMEM] * sides,
         out_shape=[jax.ShapeDtypeStruct((wears * HALO + HAZARD_ROWS, size), bf16)] * sides,
         scratch_shapes=[
@@ -153,7 +156,7 @@
         compiler_params=params(16),
         cost_estimate=cost(0, 8 * wears * 8 * size),
         name="age_edges",
-    )(flags, in_hbm(u), in_hbm(hazard))
+    )(in_hbm(u), in_hbm(hazard))
 
 
 def pack_rows(ranks, halves):
@@ -171,11 +174,11 @@
     return lax.dot_general(table, cells, (((1,), (1,)), ((), ())), preferred_element_type=f32)
 
 
-def pack_kernel(ranks, flag_ref, u_hbm, send_hbm, *refs):
+def pack_kernel(ranks, u_hbm, send_hbm, *refs):
     q_refs, (u_ref, send, send_sem, u_sem) = refs[: len(ranks)], refs[len(ranks) :]
     _, wears, ages, size = u_ref.shape
     chunk = 4
-    table = pltpu.make_async_copy(send_hbm.at[flag_ref[CHEB]], send, send_sem)
+    table = pltpu.make_async_copy(send_hbm.at[lax.axis_index("cheb")], send, send_sem)
     table.start()
     loads = []
     for g in range(wears // chunk):
@@ -193,12 +196,12 @@
             q_ref[:, g * chunk * ages : (g + 1) * chunk * ages] = rows
 
 
-def pack(flags, u4, send, ranks, extra):
+def pack(u4, send, ranks, extra):
     _, wears, ages, size = u4.shape
     cells = wears * ages
     return pl.pallas_call(
         functools.partial(pack_kernel, ranks),
-        in_specs=[SMEM, ANY, ANY],
+        in_specs=[ANY, ANY],
         out_specs=[VMEM] * (len(ranks) + 2),
         out_shape=[jax.ShapeDtypeStruct((2 * r, cells + extra), bf16) for r in ranks]
         + [pltpu.VMEM(u4.shape, f32), pltpu.VMEM(send.shape[1:], bf16)],
@@ -206,7 +209,7 @@
         compiler_params=params(16),
         cost_estimate=cost(4 * cells * sum(ranks) * size, 8 * cells * size),
         name="pack_coefficients",
-    )(flags, in_hbm(u4), in_hbm(send))
+    )(in_hbm(u4), in_hbm(send))
 
 
 def pack_edges_kernel(ranks, sides, send_ref, *refs):
@@ -233,13 +236,13 @@
     )(in_vmem(send), *near, *q)
 
 
-def local_kernel(sides, flag_ref, u_ref, hazard_hbm, diffusion_hbm, drift_hbm, second_hbm, first_hbm, take_second_hbm,
+def local_kernel(sides, u_ref, hazard_hbm, diffusion_hbm, drift_hbm, second_hbm, first_hbm, take_second_hbm,
                  take_first_hbm, *refs):
     edge_refs, refs = refs[:sides], refs[sides:]
     z, beside, ends, take, hazard, diffusion, drift, second, first, own, take_second, take_first, sem = refs
     halves, rows, _, _ = z.shape
     _, wears, ages, size = u_ref.shape
-    at = flag_ref[CHEB]
+    at = lax.axis_index("cheb")
     moves = (
         (second_hbm.at[at], second), (first_hbm.at[at], first), (diffusion_hbm.at[at], diffusion),
         (drift_hbm.at[at], drift), (hazard_hbm, hazard), (take_second_hbm.at[at], take_second),
@@ -286,13 +289,13 @@
             beside[s, place] = rate + jnp.concatenate(columns, axis=0) * u.astype(f32)
 
 
-def local(flags, u4, hazard, diffusion, drift, tables, near, sides):
+def local(u4, hazard, diffusion, drift, tables, near, sides):
     _, wears, ages, size = u4.shape
     cells = 2 * wears * ages
     wide = tables[2].shape[2]
     return pl.pallas_call(
         functools.partial(local_kernel, sides),
-        in_specs=[SMEM, VMEM] + [ANY] * 7 + [VMEM] * sides,
+        in_specs=[VMEM] + [ANY] * 7 + [VMEM] * sides,
         out_specs=[VMEM] * 4,
         out_shape=[
             pltpu.VMEM((size // 128, 2 * wears + 2 * HALO, ages + 32, 128), f32),
@@ -314,7 +317,7 @@
         compiler_params=params(16),
         cost_estimate=cost(2 * cells * size * size, 8 * cells * size),
         name="local_rate",
-    )(flags, in_vmem(u4), *[in_hbm(x) for x in (hazard, diffusion, drift, *tables)], *near)
+    )(in_vmem(u4), *[in_hbm(x) for x in (hazard, diffusion, drift, *tables)], *near)
 
 
 def arrived_tiles(ranks, q_refs, half, columns):
@@ -369,7 +372,7 @@
     )(in_vmem(ends), in_vmem(beside), in_vmem(take), *q)
 
 
-def section_kernel(ranks, sides, wears, ages, flag_ref, z_in, beside_ref, take_ref, *refs):
+def section_kernel(ranks, sides, wears, ages, z_in, beside_ref, take_ref, *refs):
     q_refs, (z,) = refs[: len(ranks)], refs[len(ranks) :]
     halves = z.shape[0]
     main, each = wears // 2 * ages, wears // 2 * HALO
@@ -383,7 +386,7 @@
                     z_in[l, HALO + w + i, ROW0 : ROW0 + ages, :]
                     + rate[i * ages : (i + 1) * ages, l * 128 : (l + 1) * 128]
                 )
-    has = [jnp.where(flag_ref[FIRST_AGE + i] == 1, 0.0, 1.0).astype(f32) for i in range(2)]
+    has = [jnp.where(at_end("age", i == 1), 0.0, 1.0).astype(f32) for i in range(2)]
     for s in range(sides):
         for half in range(2):
             columns = edge_columns(sides, main, each)[s]
@@ -399,19 +402,19 @@
                             ]
 
 
-def section(flags, z, beside, take, q, ranks, sides, wears, ages):
+def section(z, beside, take, q, ranks, sides, wears, ages):
     size = z.shape[0] * 128
     cells = wears * ages
     return pl.pallas_call(
         functools.partial(section_kernel, ranks, sides, wears, ages),
-        in_specs=[SMEM] + [VMEM] * (3 + len(ranks)),
+        in_specs=[VMEM] * (3 + len(ranks)),
         out_specs=VMEM,
         out_shape=pltpu.VMEM(z.shape, f32),
-        input_output_aliases={1: 0},
+        input_output_aliases={0: 0},
         compiler_params=params(16),
         cost_estimate=cost(2 * cells * take.shape[1] * size, 8 * cells * size),
         name="section",
-    )(flags, z, in_vmem(beside), in_vmem(take), *q)
+    )(z, in_vmem(beside), in_vmem(take), *q)
 
 
 def lane_terms(speed_ref, l):
@@ -456,16 +459,16 @@
     return put
 
 
-def by_sides(sides, flag_ref, ages, run):
+def by_sides(sides, ages, run):
     if sides == 1:
-        pl.when(flag_ref[FIRST_AGE] == 1)(lambda: run(ROW0, ROW0 + ages + 8, None))
-        pl.when(flag_ref[FIRST_AGE] == 0)(lambda: run(ROW0 - 8, ROW0 + ages, None))
+        pl.when(at_end("age", False))(lambda: run(ROW0, ROW0 + ages + 8, None))
+        pl.when(at_end("age", True))(lambda: run(ROW0 - 8, ROW0 + ages, None))
     else:
-        has = [jnp.where(flag_ref[FIRST_AGE + i] == 1, 0.0, 1.0).astype(f32) for i in range(2)]
+        has = [jnp.where(at_end("age", i == 1), 0.0, 1.0).astype(f32) for i in range(2)]
         run(ROW0 - 8, ROW0 + ages + 8, [jnp.zeros((8, 128), f32) + h for h in has])
 
 
-def inner_kernel(sides, flag_ref, z0, speed_ref, o_ref, z1, z2, z3, stage, out_sem):
+def inner_kernel(sides, z0, speed_ref, o_ref, z1, z2, z3, stage, out_sem):
     halves, rows, _, _ = z0.shape
     count, ages = stage.shape[:2]
     fields = (z0, z1, z2, z3)
@@ -502,32 +505,32 @@
         for copy in stores:
             copy.wait()
 
-    by_sides(sides, flag_ref, ages, run)
-
-
-def inner_substeps(flags, z, speed, sides, wears, ages):
+    by_sides(sides, ages, run)
+
+
+def inner_substeps(z, speed, sides, wears, ages):
     size = z.shape[0] * 128
     shape = (wears, ages, size)
     return pl.pallas_call(
         functools.partial(inner_kernel, sides),
         out_shape=[jax.ShapeDtypeStruct(shape, f32)] + [pltpu.VMEM(z.shape, f32)] * 3,
-        in_specs=[SMEM] + [VMEM] * 2,
+        in_specs=[VMEM] * 2,
         out_specs=[ANY] + [VMEM] * 3,
         scratch_shapes=[pltpu.VMEM((wears - 2 * SUBSTEPS, ages, size), f32), pltpu.SemaphoreType.DMA((4,))],
         compiler_params=params(16),
         cost_estimate=cost(10 * SUBSTEPS * wears * ages * size, 8 * wears * ages * size),
         name="inner_substeps",
-    )(flags, in_vmem(z), speed)
-
-
-def outer_kernel(sides, flag_ref, o_in, z0_in, z1_in, z2_in, z3_in, speed_ref, up_ref, down_ref, o_ref, z0, z1, z2, z3,
+    )(in_vmem(z), speed)
+
+
+def outer_kernel(sides, o_in, z0_in, z1_in, z2_in, z3_in, speed_ref, up_ref, down_ref, o_ref, z0, z1, z2, z3,
                  stage, out_sem):
     del o_in, z0_in, z1_in, z2_in, z3_in
     halves, rows, _, _ = z0.shape
     wears, ages = rows - 2 * HALO, stage.shape[2]
     fields = (z0, z1, z2, z3)
-    has = [jnp.where(flag_ref[FIRST_AGE + i] == 1, 0.0, 1.0).astype(f32) for i in range(2)]
-    near = [jnp.where(flag_ref[FIRST_WEAR + i] == 1, 0.0, 1.0).astype(f32) for i in range(2)]
+    has = [jnp.where(at_end("age", i == 1), 0.0, 1.0).astype(f32) for i in range(2)]
+    near = [jnp.where(at_end("wear", i == 1), 0.0, 1.0).astype(f32) for i in range(2)]
     for l in range(halves):
         lanes = pl.ds(l * 128, 128)
         for e, (ref, at) in enumerate(((up_ref, 0), (down_ref, HALO + wears))):
@@ -566,22 +569,22 @@
         for copy in stores:
             copy.wait()
 
-    by_sides(sides, flag_ref, ages, run)
-
-
-def outer_substeps(flags, o, fields, speed, up, down, sides):
+    by_sides(sides, ages, run)
+
+
+def outer_substeps(o, fields, speed, up, down, sides):
     wears, ages, size = o.shape
     return pl.pallas_call(
         functools.partial(outer_kernel, sides),
         out_shape=[jax.ShapeDtypeStruct(o.shape, f32)] + [pltpu.VMEM(z.shape, f32) for z in fields],
-        in_specs=[SMEM, ANY] + [VMEM] * 7,
+        in_specs=[ANY] + [VMEM] * 7,
         out_specs=[ANY] + [VMEM] * 4,
         scratch_shapes=[pltpu.VMEM((2, HALO, ages, size), f32), pltpu.SemaphoreType.DMA((2,))],
-        input_output_aliases={1 + i: i for i in range(5)},
+        input_output_aliases={i: i for i in range(5)},
         compiler_params=params(16),
         cost_estimate=cost(20 * SUBSTEPS * 2 * HALO * ages * size, 2**20),
         name="outer_substeps",
-    )(flags, o, *fields, speed, up, down)[0]
+    )(o, *fields, speed, up, down)[0]
 
 
 def body(adjoint_value, load_diffusion, load_drift, wear_speed, hazard):
@@ -590,10 +593,7 @@
     devices = points // size
     slots, send, take_second, take_first, own_second, own_first = factors(points, devices)
     ranks = tuple(rank for _, rank in slots)
-    cheb = lax.axis_index("cheb")
-    wear, age = lax.axis_index("wear"), lax.axis_index("age")
     n_wear, n_age = lax.axis_size("wear"), lax.axis_size("age")
-    flags = jnp.stack([wear == 0, wear == n_wear - 1, age == 0, age == n_age - 1, cheb]).astype(jnp.int32)
     sides = 1 if n_age == 2 else 2
     extra = sides * wears // 2 * HALO
     u4 = adjoint_value.reshape(2, wears // 2, ages, size)
@@ -605,19 +605,19 @@
         after = [(i, (i + 1) % n) for i in range(n)]
         return after, [(j, i) for i, j in after]
 
-    edge = edges(flags, adjoint_value, hazard, sides)
+    edge = edges(adjoint_value, hazard, sides)
     near = [lax.ppermute(x, "age", pairs) for x, pairs in zip(edge, ring(n_age))]
-    *q, u4, send = pack(flags, u4, jnp.asarray(send, bf16), ranks, extra)
+    *q, u4, send = pack(u4, jnp.asarray(send, bf16), ranks, extra)
     q = pack_edges(send, near, q, ranks, sides)
     arrived = [lax.ppermute(x, "cheb", list(pairs)) for x, (pairs, _) in zip(q, slots)]
-    z, beside, ends, take = local(flags, u4, hazard, diffusion, drift, tables, near, sides)
+    z, beside, ends, take = local(u4, hazard, diffusion, drift, tables, near, sides)
     top, bottom = outer_rows(ends, beside, take, arrived, ranks, sides, wears, ages)
     after, before = ring(n_wear)
     up, down = lax.ppermute(bottom, "wear", after), lax.ppermute(top, "wear", before)
-    z = section(flags, z, beside, take, arrived, ranks, sides, wears, ages)
+    z = section(z, beside, take, arrived, ranks, sides, wears, ages)
     speed = wear_speed.reshape(1, size)
-    o, *fields = inner_substeps(flags, z, speed, sides, wears, ages)
-    return outer_substeps(flags, o, [z, *fields], speed, up, down, sides)
+    o, *fields = inner_substeps(z, speed, sides, wears, ages)
+    return outer_substeps(o, [z, *fields], speed, up, down, sides)
 
 
 def solution(mesh):

time: 35.2 us -> 32.5 us (0.923)
  Pallas kernels: 21.9 us -> 18.8 us
  waiting for transfers between devices: 3.91 us -> 4.3 us
    pallas_call x3, Pallas kernels: 8.99 us -> 7.52 us  [the longest x1 3.77 us: pack(): pl.pallas_call(functools.partial(pack_kernel, ranks), in_specs=[ANY, ANY]...]
    pallas_call x1, Pallas kernels: 2.22 us -> 1.67 us  [outer_substeps(): pl.pallas_call(functools.partial(outer_kernel, sides), out_shape=[jax.Sha...]
    pallas_call x1, Pallas kernels: 1.68 us -> 1.15 us  [section(): pl.pallas_call(functools.partial(section_kernel, ranks, sides, wears, age...]
    pallas_call x1, Pallas kernels: 8.54 us -> 8.01 us  [inner_substeps(): pl.pallas_call(functools.partial(inner_kernel, sides), out_shape=[jax.Sha...]
    ppermute x3, waiting for transfers between devices: 3.9 us -> 4.29 us  [body(): lax.ppermute(x, 'cheb', list(pairs))]
  transfers between devices with their start and end apart: 6 -> 6, of which waited for: 1 -> 1; matrix products, arithmetic and copies ran while one was open for 0% -> 0% of each run, Pallas kernels for 50% -> 48%
where the time goes in v2:
time: 32.5 us; the launch traced here: 32.3 us
  Pallas kernels  18.8 us (58%)
  starting transfers between devices  9.09 us (28%)
  waiting for transfers between devices  4.3 us (13%)
    pallas_call x1, Pallas kernels, inner_substeps(): pl.pallas_call(functools.partial(inner_kernel, sides), out_shape=[jax.Sha...  8.01 us
    ppermute x3, waiting for transfers between devices, body(): lax.ppermute(x, 'cheb', list(pairs))  4.29 us
    pallas_call x1, Pallas kernels, pack(): pl.pallas_call(functools.partial(pack_kernel, ranks), in_specs=[ANY, ANY]...  3.77 us
    ppermute x1, starting transfers between devices, body(): lax.ppermute(x, 'age', pairs)  3 us
    pallas_call x1, Pallas kernels, local(): pl.pallas_call(functools.partial(local_kernel, sides), in_specs=[VMEM] +...  2.58 us
    ppermute x3, starting transfers between devices, body(): lax.ppermute(x, 'cheb', list(pairs))  2.21 us
    ppermute x1, starting transfers between devices, body(): lax.ppermute(top, 'wear', before)  2.12 us
    ppermute x1, starting transfers between devices, body(): lax.ppermute(bottom, 'wear', after)  1.76 us
  transfers between devices with their start and end apart: 6, of which 1 were waited for; matrix products, arithmetic and copies ran while one was open for 0% of the time, Pallas kernels for 48%

profile of v2, /device:TPU:0, one launch (start us, length us, event | category | flops | bytes accessed | tf_op | source)
XLA Modules:
  0.0 32.3 jit_solution(5171466052389710944)
XLA Ops:
  0.0 1.2 %age_edges.1 = bf16[272,256]{1,0:T(8,128)(2,1)S(1)} custom-call(f32[64,64,256]{2,1,0:T(8,128)} %u_hbm.1, f32[64,64]{1,0:T(8,128)} %hazard_hbm.3), custom_call_target="tpu_custom_call" | custom-call | bytes 1048576 | tf_op jit(solution)/shard_map/age_edges/pallas_call | solution.py:146
  1.2 3.0 %collective-permute-start = (bf16[272,256]{1,0:T(8,128)(2,1)S(1)}, bf16[272,256]{1,0:T(8,128)(2,1)S(1)}, u32[]{:S(2)}, u32[]{:S(2)}) collective-permute-start(bf16[272,256]{1,0:T(8,128)(2,1)S(1)} %age_edges.1), channel_id=1, source_target_pairs={{0,1},{1,0},{2,3},{3,2},{4,5},{5,4},{6,7},{7,6},{8,9},{9,8},{10,11... | collective-permute-start | bytes 417800 | tf_op jit(solution)/shard_map/ppermute | solution.py:609
  4.2 3.8 %pack_coefficients.1 = (bf16[48,2176]{1,0:T(8,128)(2,1)S(1)}, bf16[16,2176]{1,0:T(8,128)(2,1)S(1)}, bf16[48,2176]{1,0:T(8,128)(2,1)S(1)}, f32[2,32,64,256]{3,2,1,0:T(8,128)S(1)}, bf16[56,256]{1,0:T(8,128)(2,1)S(1)}) custom-call(f32[2,32,64,256]{3,2,1,0:T(8,128)} %bitcast.6, bf16[4,56,256]{2,1,0:T(8,128)(2,1)} %constant.14.clone.send_hbm), custom_call_target="tpu_custom_call" | custom-call | flops 117440512 | bytes 4194304 | tf_op jit(solution)/shard_map/pack_coefficients/pallas_call | solution.py:202
  8.0 0.0 collective-permute-done.refs_0_
  8.0 0.2 pack_edges.1
  8.1 0.1 collective-permute-start.1
  8.2 1.8 %collective-permute-start.3 = (bf16[48,2176]{1,0:T(8,128)(2,1)S(1)}, bf16[48,2176]{1,0:T(8,128)(2,1)S(1)}, u32[]{:S(2)}, u32[]{:S(2)}) collective-permute-start(bf16[48,2176]{1,0:T(8,128)(2,1)S(1)} %get-tuple-element.34), channel_id=1, source_target_pairs={{0,24},{8,16},{16,8},{24,0},{1,25},{9,17},{17,9},{25,1},{2,26},{10... | collective-permute-start | bytes 626696 | tf_op jit(solution)/shard_map/ppermute | solution.py:612
  10.0 0.4 %collective-permute-start.2 = (bf16[16,2176]{1,0:T(8,128)(2,1)S(1)}, bf16[16,2176]{1,0:T(8,128)(2,1)S(1)}, u32[]{:S(2)}, u32[]{:S(2)}) collective-permute-start(bf16[16,2176]{1,0:T(8,128)(2,1)S(1)} %get-tuple-element.33), channel_id=1, source_target_pairs={{0,16},{8,24},{16,0},{24,8},{1,17},{9,25},{17,1},{25,9},{2,18},{10... | collective-permute-start | bytes 208904 | tf_op jit(solution)/shard_map/ppermute | solution.py:612
  10.4 2.6 %local_rate.1 = (f32[2,72,96,128]{3,2,1,0:T(8,128)S(1)}, f32[1,256,256]{2,1,0:T(8,128)S(1)}, f32[2,256,256]{2,1,0:T(8,128)S(1)}, bf16[2,80,256]{2,1,0:T(8,128)(2,1)S(1)}) custom-call(f32[2,32,64,256]{3,2,1,0:T(8,128)S(1)} %get-tuple-element.24.u_ref, f32[64,64]{1,0:T(8,128)} %hazard_hbm.3, f32[4,1,256]{2,1,0:T(1,128)} %bitcast.7, f32[4,1,256]{2,1,0:T(1,128)} %bitcast.8, ...), custom_call_target="tpu_custom_call" | custom-call | flops 536870912 | bytes 8388608 | tf_op jit(solution)/shard_map/local_rate/pallas_call | solution.py:296
  12.9 4.3 %collective-permute-done.2.refs_1_ = bf16[16,2176]{1,0:T(8,128)(2,1)S(1)} collective-permute-done((bf16[16,2176]{1,0:T(8,128)(2,1)S(1)}, bf16[16,2176]{1,0:T(8,128)(2,1)S(1)}, u32[]{:S(2)}, u32[]{:S(2)}) %collective-permute-start.2) | collective-permute-done | bytes 69664 | tf_op jit(solution)/shard_map/ppermute | solution.py:612
  17.2 0.0 collective-permute-done.1.refs_0_
  17.2 0.0 collective-permute-done.3.refs_2_
  17.2 0.3 outer_rows.1
  17.5 1.8 %collective-permute-start.4 = (bf16[272,256]{1,0:T(8,128)(2,1)S(1)}, bf16[272,256]{1,0:T(8,128)(2,1)S(1)}, u32[]{:S(2)}, u32[]{:S(2)}) collective-permute-start(bf16[272,256]{1,0:T(8,128)(2,1)S(1)} %get-tuple-element.40), channel_id=1, source_target_pairs={{0,2},{2,4},{4,6},{6,0},{1,3},{3,5},{5,7},{7,1},{8,10},{10,12},{12... | collective-permute-start | bytes 417800 | tf_op jit(solution)/shard_map/ppermute | solution.py:616
  19.3 2.1 %collective-permute-start.5 = (bf16[272,256]{1,0:T(8,128)(2,1)S(1)}, bf16[272,256]{1,0:T(8,128)(2,1)S(1)}, u32[]{:S(2)}, u32[]{:S(2)}) collective-permute-start(bf16[272,256]{1,0:T(8,128)(2,1)S(1)} %get-tuple-element.41), channel_id=1, source_target_pairs={{2,0},{4,2},{6,4},{0,6},{3,1},{5,3},{7,5},{1,7},{10,8},{12,10},{14... | collective-permute-start | bytes 417800 | tf_op jit(solution)/shard_map/ppermute | solution.py:616
  21.4 0.0 copy-start
  21.4 1.1 %section.1.z0.z0_in = f32[2,72,96,128]{3,2,1,0:T(8,128)S(1)} custom-call(f32[2,72,96,128]{3,2,1,0:T(8,128)S(1)} %get-tuple-element.25.z_in, f32[1,256,256]{2,1,0:T(8,128)S(1)} %get-tuple-element.26.beside_ref, bf16[2,80,256]{2,1,0:T(8,128)(2,1)S(1)} %get-tuple-element.27.take_ref, ...), custom_call_target="tpu_custom_call", output_to_operand_aliasing={{}: (0, {})} | custom-call | flops 167772160 | bytes 8388608 | tf_op jit(solution)/shard_map/section/pallas_call | solution.py:408
  22.6 0.0 copy-done
  22.6 8.0 %inner_substeps.1 = (f32[64,64,256]{2,1,0:T(8,128)}, f32[2,72,96,128]{3,2,1,0:T(8,128)S(1)}, f32[2,72,96,128]{3,2,1,0:T(8,128)S(1)}, f32[2,72,96,128]{3,2,1,0:T(8,128)S(1)}) custom-call(f32[2,72,96,128]{3,2,1,0:T(8,128)S(1)} %section.1.z0.z0_in, f32[1,256]{1,0:T(1,128)S(1)} %bitcast.4), custom_call_target="tpu_custom_call" | custom-call | flops 41943040 | bytes 8388608 | tf_op jit(solution)/shard_map/inner_substeps/pallas_call | solution.py:514
  30.6 0.0 collective-permute-done.4.up_ref
  30.6 0.0 collective-permute-done.5.down_ref
  30.6 1.7 %outer_substeps.1 = (f32[64,64,256]{2,1,0:T(8,128)}, f32[2,72,96,128]{3,2,1,0:T(8,128)S(1)}, f32[2,72,96,128]{3,2,1,0:T(8,128)S(1)}, f32[2,72,96,128]{3,2,1,0:T(8,128)S(1)}, f32[2,72,96,128]{3,2,1,0:T(8,128)S(1)}) custom-call(f32[64,64,256]{2,1,0:T(8,128)} %get-tuple-element.35.o_in, ...), custom_call_target="tpu_custom_call", output_to_operand_aliasing={{0}: (0, {}), {1}: (1, {}), {2}: (2, {}), {3}: (3, {}), {4}... | custom-call | flops 10485760 | bytes 1048576 | tf_op jit(solution)/shard_map/outer_substeps/pallas_call | solution.py:577
Async XLA Ops:
  1.2 6.8 %collective-permute-start = (bf16[272,256]{1,0:T(8,128)(2,1)S(1)}, bf16[272,256]{1,0:T(8,128)(2,1)S(1)}, u32[]{:S(2)}, u32[]{:S(2)}) collective-permute-start(bf16[272,256]{1,0:T(8,128)(2,1)S(1)} %age_edges.1), channel_id=1, source_target_pairs={{0,1},{1,0},{2,3},{3,2},{4,5},{5,4},{6,7},{7,6},{8,9},{9,8},{10,11... | collective-permute-start | bytes 417800 | tf_op jit(solution)/shard_map/ppermute | solution.py:609
  8.1 9.1 %collective-permute-start.1 = (bf16[48,2176]{1,0:T(8,128)(2,1)S(1)}, bf16[48,2176]{1,0:T(8,128)(2,1)S(1)}, u32[]{:S(2)}, u32[]{:S(2)}) collective-permute-start(bf16[48,2176]{1,0:T(8,128)(2,1)S(1)} %get-tuple-element.32), channel_id=1, source_target_pairs={{0,8},{8,0},{16,24},{24,16},{1,9},{9,1},{17,25},{25,17},{2,10},{10... | collective-permute-start | bytes 626696 | tf_op jit(solution)/shard_map/ppermute | solution.py:612
  8.2 9.0 %collective-permute-start.3 = (bf16[48,2176]{1,0:T(8,128)(2,1)S(1)}, bf16[48,2176]{1,0:T(8,128)(2,1)S(1)}, u32[]{:S(2)}, u32[]{:S(2)}) collective-permute-start(bf16[48,2176]{1,0:T(8,128)(2,1)S(1)} %get-tuple-element.34), channel_id=1, source_target_pairs={{0,24},{8,16},{16,8},{24,0},{1,25},{9,17},{17,9},{25,1},{2,26},{10... | collective-permute-start | bytes 626696 | tf_op jit(solution)/shard_map/ppermute | solution.py:612
  10.0 7.3 %collective-permute-start.2 = (bf16[16,2176]{1,0:T(8,128)(2,1)S(1)}, bf16[16,2176]{1,0:T(8,128)(2,1)S(1)}, u32[]{:S(2)}, u32[]{:S(2)}) collective-permute-start(bf16[16,2176]{1,0:T(8,128)(2,1)S(1)} %get-tuple-element.33), channel_id=1, source_target_pairs={{0,16},{8,24},{16,0},{24,8},{1,17},{9,25},{17,1},{25,9},{2,18},{10... | collective-permute-start | bytes 208904 | tf_op jit(solution)/shard_map/ppermute | solution.py:612
  17.5 13.1 %collective-permute-start.4 = (bf16[272,256]{1,0:T(8,128)(2,1)S(1)}, bf16[272,256]{1,0:T(8,128)(2,1)S(1)}, u32[]{:S(2)}, u32[]{:S(2)}) collective-permute-start(bf16[272,256]{1,0:T(8,128)(2,1)S(1)} %get-tuple-element.40), channel_id=1, source_target_pairs={{0,2},{2,4},{4,6},{6,0},{1,3},{3,5},{5,7},{7,1},{8,10},{10,12},{12... | collective-permute-start | bytes 417800 | tf_op jit(solution)/shard_map/ppermute | solution.py:616
  19.3 11.3 %collective-permute-start.5 = (bf16[272,256]{1,0:T(8,128)(2,1)S(1)}, bf16[272,256]{1,0:T(8,128)(2,1)S(1)}, u32[]{:S(2)}, u32[]{:S(2)}) collective-permute-start(bf16[272,256]{1,0:T(8,128)(2,1)S(1)} %get-tuple-element.41), channel_id=1, source_target_pairs={{2,0},{4,2},{6,4},{0,6},{3,1},{5,3},{7,5},{1,7},{10,8},{12,10},{14... | collective-permute-start | bytes 417800 | tf_op jit(solution)/shard_map/ppermute | solution.py:616
  21.4 1.2 %copy-start = (f32[256]{0:T(256)S(1)}, f32[256]{0:T(256)}, u32[]{:S(2)}) copy-start(f32[256]{0:T(256)} %param.13) | copy-start | bytes 3076

commit v3 on v2

--- a/solution.py
+++ b/solution.py
@@ -80,7 +80,7 @@
 
 ANY = pl.BlockSpec(memory_space=pl.ANY)
 VMEM = pl.BlockSpec(memory_space=pltpu.VMEM)
-SMEM = pl.BlockSpec(memory_space=pltpu.SMEM)
+PIN = pltpu.VMEM
 ROW0 = 16
 HAZARD_ROWS = 16
 
@@ -138,16 +138,17 @@
         high = exact.astype(bf16).astype(f32)
         rows = jnp.concatenate([high, exact - high, jnp.zeros((HAZARD_ROWS - 2 * HALO, wears), f32)], axis=0)
         rows = jnp.concatenate([rows, jnp.zeros((HAZARD_ROWS, size - wears), f32)], axis=1)
-        out_ref[wears * HALO :] = rows.astype(bf16)
-
-
-def edges(u, hazard, sides):
+        out_ref[wears * HALO : wears * HALO + HAZARD_ROWS] = rows.astype(bf16)
+        out_ref[wears * HALO + HAZARD_ROWS :] = jnp.zeros_like(out_ref[wears * HALO + HAZARD_ROWS :])
+
+
+def edges(u, hazard, sides, rows):
     wears, ages, size = u.shape
     return pl.pallas_call(
         functools.partial(edge_kernel, sides),
         in_specs=[ANY, ANY],
         out_specs=[VMEM] * sides,
-        out_shape=[jax.ShapeDtypeStruct((wears * HALO + HAZARD_ROWS, size), bf16)] * sides,
+        out_shape=[PIN((rows, size), bf16)] * sides,
         scratch_shapes=[
             pltpu.VMEM((sides, wears, 8, size), f32),
             pltpu.VMEM((wears, ages), f32),
@@ -174,20 +175,14 @@
     return lax.dot_general(table, cells, (((1,), (1,)), ((), ())), preferred_element_type=f32)
 
 
-def pack_kernel(ranks, u_hbm, send_hbm, *refs):
-    q_refs, (u_ref, send, send_sem, u_sem) = refs[: len(ranks)], refs[len(ranks) :]
+def pack_kernel(ranks, sides, u_ref, send_hbm, *refs):
+    q_refs, (send, send_sem) = refs[sides : sides + len(ranks)], refs[sides + len(ranks) :]
     _, wears, ages, size = u_ref.shape
     chunk = 4
     table = pltpu.make_async_copy(send_hbm.at[lax.axis_index("cheb")], send, send_sem)
     table.start()
-    loads = []
-    for g in range(wears // chunk):
-        rows = pl.ds(g * chunk, chunk)
-        loads.append(pltpu.make_async_copy(u_hbm.at[:, rows], u_ref.at[:, rows], u_sem.at[g]))
-        loads[-1].start()
     table.wait()
     for g in range(wears // chunk):
-        loads[g].wait()
         halves = [
             analyse(send[...], u_ref[half, g * chunk : (g + 1) * chunk].reshape(chunk * ages, size).astype(bf16))
             for half in range(2)
@@ -196,44 +191,43 @@
             q_ref[:, g * chunk * ages : (g + 1) * chunk * ages] = rows
 
 
-def pack(u4, send, ranks, extra):
+def pack(u4, send, edge, ranks):
     _, wears, ages, size = u4.shape
     cells = wears * ages
     return pl.pallas_call(
-        functools.partial(pack_kernel, ranks),
-        in_specs=[ANY, ANY],
-        out_specs=[VMEM] * (len(ranks) + 2),
-        out_shape=[jax.ShapeDtypeStruct((2 * r, cells + extra), bf16) for r in ranks]
-        + [pltpu.VMEM(u4.shape, f32), pltpu.VMEM(send.shape[1:], bf16)],
-        scratch_shapes=[pltpu.SemaphoreType.DMA, pltpu.SemaphoreType.DMA((wears // 4,))],
+        functools.partial(pack_kernel, ranks, len(edge)),
+        in_specs=[VMEM, ANY] + [ANY] * len(edge),
+        out_specs=[VMEM] * (len(ranks) + 1),
+        out_shape=[PIN((2 * r, cells), bf16) for r in ranks] + [PIN(send.shape[1:], bf16)],
+        scratch_shapes=[pltpu.SemaphoreType.DMA],
         compiler_params=params(16),
         cost_estimate=cost(4 * cells * sum(ranks) * size, 8 * cells * size),
         name="pack_coefficients",
-    )(in_hbm(u4), in_hbm(send))
+    )(in_vmem(u4), in_hbm(send), *[in_vmem(x) for x in edge])
 
 
 def pack_edges_kernel(ranks, sides, send_ref, *refs):
-    edge_refs, q_refs = refs[:sides], refs[sides + len(ranks) :]
-    count = edge_refs[0].shape[0] - HAZARD_ROWS
+    edge_refs, q_refs = refs[:sides], refs[sides + 2 :]
+    count = 2 * q_refs[0].shape[1] // sides
     halves = []
     for half in range(2):
         cells = [r[half * count // 2 : (half + 1) * count // 2] for r in edge_refs]
         halves.append(analyse(send_ref[...], jnp.concatenate(cells, axis=0)))
     for q_ref, rows in zip(q_refs, pack_rows(ranks, halves)):
-        q_ref[:, q_ref.shape[1] - rows.shape[1] :] = rows
-
-
-def pack_edges(send, near, q, ranks, sides):
+        q_ref[...] = rows
+
+
+def pack_edges(send, near, arrived, ranks, sides, extra):
     return pl.pallas_call(
         functools.partial(pack_edges_kernel, ranks, sides),
-        in_specs=[VMEM] * (1 + sides + len(ranks)),
-        out_specs=[VMEM] * len(ranks),
-        out_shape=[jax.ShapeDtypeStruct(x.shape, x.dtype) for x in q],
-        input_output_aliases={1 + sides + i: i for i in range(len(ranks))},
+        in_specs=[VMEM] * (2 + sides),
+        out_specs=[VMEM] * (1 + len(ranks)),
+        out_shape=[PIN(arrived.shape, bf16)] + [PIN((2 * r, extra), bf16) for r in ranks],
+        input_output_aliases={1 + sides: 0},
         compiler_params=params(16),
         cost_estimate=cost(0, 2**18),
         name="pack_edges",
-    )(in_vmem(send), *near, *q)
+    )(*[in_vmem(x) for x in (send, *near, arrived)])
 
 
 def local_kernel(sides, u_ref, hazard_hbm, diffusion_hbm, drift_hbm, second_hbm, first_hbm, take_second_hbm,
@@ -276,7 +270,7 @@
                     ends[e, (w + i - start) * ages : (w + i - start + 1) * ages] = value
     for s, ref in enumerate(edge_refs):
         count = 2 * wears * HALO
-        parts = ref[count:].astype(f32)
+        parts = ref[count : count + HAZARD_ROWS].astype(f32)
         near = START - START * (parts[:HALO, : 2 * wears] + parts[HALO : 2 * HALO, : 2 * wears])
         near = jnp.concatenate([near, near], axis=0)
         for w in range(0, 2 * wears, 4):
@@ -317,69 +311,59 @@
         compiler_params=params(16),
         cost_estimate=cost(2 * cells * size * size, 8 * cells * size),
         name="local_rate",
-    )(in_vmem(u4), *[in_hbm(x) for x in (hazard, diffusion, drift, *tables)], *near)
-
-
-def arrived_tiles(ranks, q_refs, half, columns):
+    )(in_vmem(u4), *[in_hbm(x) for x in (hazard, diffusion, drift, *tables)], *[in_vmem(x) for x in near])
+
+
+def distant(ranks, q_refs, take_ref, half, columns):
     tiles = []
-    for rank, q in zip(ranks, q_refs):
+    for rank, q, place in zip(ranks, q_refs, columns):
         cut = rank // 16 * 16
         if cut:
-            tiles.append(q[half * cut : (half + 1) * cut, columns])
+            tiles.append(q[half * cut : (half + 1) * cut, place])
         if rank > cut:
-            tiles.append(q[2 * cut : 2 * rank, columns])
-    return jnp.concatenate(tiles, axis=0)
-
-
-def distant(ranks, q_refs, take_ref, half, columns):
+            tiles.append(q[2 * cut : 2 * rank, place])
     return lax.dot_general(
-        arrived_tiles(ranks, q_refs, half, columns), take_ref[half], (((0,), (0,)), ((), ())),
-        preferred_element_type=f32,
+        jnp.concatenate(tiles, axis=0), take_ref[half], (((0,), (0,)), ((), ())), preferred_element_type=f32
     )
 
 
-def edge_columns(sides, main, each):
-    return [slice(main + s * each, main + (s + 1) * each) for s in range(sides)]
-
-
 def rows_kernel(ranks, sides, wears, ages, ends_ref, beside_ref, take_ref, *refs):
-    q_refs, out_refs = refs[: len(ranks)], refs[len(ranks) :]
-    main, each = wears // 2 * ages, wears // 2 * HALO
-    corner = HALO * HALO
+    q_refs, edge_refs, out_refs = refs[: len(ranks)], refs[len(ranks) : -2], refs[-2:]
+    each, corner = wears // 2 * HALO, HALO * HALO
     for half, (start, out_ref) in enumerate(zip((0, wears - HALO), out_refs)):
         v = (start - half * wears // 2) * ages
-        rate = distant(ranks, q_refs, take_ref, half, slice(v, v + HALO * ages))
+        rate = distant(ranks, q_refs, take_ref, half, [slice(v, v + HALO * ages)] * len(ranks))
         out_ref[: HALO * ages] = (rate + ends_ref[half]).astype(bf16)
-        for s, columns in enumerate(edge_columns(sides, main, each)):
-            first = 0 if half == 0 else each - corner
-            rate = distant(ranks, q_refs, take_ref, half, columns)[first : first + corner]
+        first = 0 if half == 0 else each - corner
+        for s in range(sides):
+            rate = distant(ranks, edge_refs, take_ref, half, [slice(s * each, (s + 1) * each)] * len(ranks))
             place = slice(start * HALO, start * HALO + corner)
             row = HALO * ages + s * corner
-            out_ref[row : row + corner] = (rate + beside_ref[s, place]).astype(bf16)
-
-
-def outer_rows(ends, beside, take, q, ranks, sides, wears, ages):
+            out_ref[row : row + corner] = (rate[first : first + corner] + beside_ref[s, place]).astype(bf16)
+
+
+def outer_rows(ends, beside, take, q, q_edges, ranks, sides, wears, ages):
     size = ends.shape[-1]
-    message = jax.ShapeDtypeStruct((HALO * ages + sides * HALO * HALO, size), bf16)
+    message = PIN((HALO * ages + sides * HALO * HALO, size), bf16)
     return pl.pallas_call(
         functools.partial(rows_kernel, ranks, sides, wears, ages),
-        in_specs=[VMEM] * (3 + len(ranks)),
+        in_specs=[VMEM] * (3 + 2 * len(ranks)),
         out_specs=[VMEM] * 2,
         out_shape=[message, message],
         compiler_params=params(16),
         cost_estimate=cost(2 * 8 * ages * take.shape[1] * size, 2**20),
         name="outer_rows",
-    )(in_vmem(ends), in_vmem(beside), in_vmem(take), *q)
+    )(*[in_vmem(x) for x in (ends, beside, take, *q, *q_edges)])
 
 
 def section_kernel(ranks, sides, wears, ages, z_in, beside_ref, take_ref, *refs):
-    q_refs, (z,) = refs[: len(ranks)], refs[len(ranks) :]
+    q_refs, edge_refs, z = refs[: len(ranks)], refs[len(ranks) : -1], refs[-1]
     halves = z.shape[0]
-    main, each = wears // 2 * ages, wears // 2 * HALO
+    each = wears // 2 * HALO
     chunk = 4
     for w in range(0, wears, chunk):
         half, v = divmod(w, wears // 2)
-        rate = distant(ranks, q_refs, take_ref, half, slice(v * ages, (v + chunk) * ages))
+        rate = distant(ranks, q_refs, take_ref, half, [slice(v * ages, (v + chunk) * ages)] * len(ranks))
         for i in range(chunk):
             for l in range(halves):
                 z[l, HALO + w + i, ROW0 : ROW0 + ages, :] = (
@@ -389,9 +373,9 @@
     has = [jnp.where(at_end("age", i == 1), 0.0, 1.0).astype(f32) for i in range(2)]
     for s in range(sides):
         for half in range(2):
-            columns = edge_columns(sides, main, each)[s]
             place = slice(half * each, (half + 1) * each)
-            cells = distant(ranks, q_refs, take_ref, half, columns) + beside_ref[s, place]
+            cells = distant(ranks, edge_refs, take_ref, half, [slice(s * each, (s + 1) * each)] * len(ranks))
+            cells += beside_ref[s, place]
             for i, column in ((0, ROW0 - HALO), (1, ROW0 + ages)):
                 if sides == 1 or s == i:
                     part = cells * has[i]
@@ -402,19 +386,19 @@
                             ]
 
 
-def section(z, beside, take, q, ranks, sides, wears, ages):
+def section(z, beside, take, q, q_edges, ranks, sides, wears, ages):
     size = z.shape[0] * 128
     cells = wears * ages
     return pl.pallas_call(
         functools.partial(section_kernel, ranks, sides, wears, ages),
-        in_specs=[VMEM] * (3 + len(ranks)),
+        in_specs=[VMEM] * (3 + 2 * len(ranks)),
         out_specs=VMEM,
         out_shape=pltpu.VMEM(z.shape, f32),
         input_output_aliases={0: 0},
         compiler_params=params(16),
         cost_estimate=cost(2 * cells * take.shape[1] * size, 8 * cells * size),
         name="section",
-    )(z, in_vmem(beside), in_vmem(take), *q)
+    )(z, *[in_vmem(x) for x in (beside, take, *q, *q_edges)])
 
 
 def lane_terms(speed_ref, l):
@@ -584,7 +568,7 @@
         compiler_params=params(16),
         cost_estimate=cost(20 * SUBSTEPS * 2 * HALO * ages * size, 2**20),
         name="outer_substeps",
-    )(o, *fields, speed, up, down)[0]
+    )(o, *fields, speed, in_vmem(up), in_vmem(down))[0]
 
 
 def body(adjoint_value, load_diffusion, load_drift, wear_speed, hazard):
@@ -605,16 +589,19 @@
         after = [(i, (i + 1) % n) for i in range(n)]
         return after, [(j, i) for i, j in after]
 
-    edge = edges(adjoint_value, hazard, sides)
+    most = 2 * max(ranks) * (wears // 2 * ages) // size
+    edge = edges(adjoint_value, hazard, sides, max(wears * HALO + HAZARD_ROWS, -(-most // 16) * 16))
     near = [lax.ppermute(x, "age", pairs) for x, pairs in zip(edge, ring(n_age))]
-    *q, u4, send = pack(u4, jnp.asarray(send, bf16), ranks, extra)
-    q = pack_edges(send, near, q, ranks, sides)
-    arrived = [lax.ppermute(x, "cheb", list(pairs)) for x, (pairs, _) in zip(q, slots)]
+    *q, send = pack(u4, jnp.asarray(send, bf16), edge, ranks)
+    moves = [list(pairs) for pairs, _ in slots]
+    arrived = [lax.ppermute(x, "cheb", pairs) for x, pairs in zip(q, moves)]
+    arrived[0], *q_edges = pack_edges(send, near, arrived[0], ranks, sides, extra)
+    arrived_edges = [lax.ppermute(x, "cheb", pairs) for x, pairs in zip(q_edges, moves)]
     z, beside, ends, take = local(u4, hazard, diffusion, drift, tables, near, sides)
-    top, bottom = outer_rows(ends, beside, take, arrived, ranks, sides, wears, ages)
+    top, bottom = outer_rows(ends, beside, take, arrived, arrived_edges, ranks, sides, wears, ages)
     after, before = ring(n_wear)
     up, down = lax.ppermute(bottom, "wear", after), lax.ppermute(top, "wear", before)
-    z = section(z, beside, take, arrived, ranks, sides, wears, ages)
+    z = section(z, beside, take, arrived, arrived_edges, ranks, sides, wears, ages)
     speed = wear_speed.reshape(1, size)
     o, *fields = inner_substeps(z, speed, sides, wears, ages)
     return outer_substeps(o, [z, *fields], speed, up, down, sides)

time: 32.5 us -> 30.1 us (0.926)
  waiting for transfers between devices: 4.3 us -> 1.85 us
  starting transfers between devices: 9.09 us -> 11.3 us
  Pallas kernels: 18.8 us -> 16.6 us
    ppermute x3 -> x6, waiting for transfers between devices: 4.29 us -> 0.69 us  [the longest x3 0.64 us: body(): arrived = [lax.ppermute(x, 'cheb', pairs) for x, pairs in zip(q, moves)]]
    pallas_call x1, Pallas kernels: 3.77 us -> 1.51 us  [pack(): pl.pallas_call(functools.partial(pack_kernel, ranks, len(edge)), in_specs...]
    ppermute x3 -> x6, starting transfers between devices: 2.21 us -> 4.42 us  [the longest x3 2.21 us: body(): arrived = [lax.ppermute(x, 'cheb', pairs) for x, pairs in zip(q, moves)]]
    ppermute x1, waiting for transfers between devices: 0.01 us -> 1.16 us  [body(): lax.ppermute(x, 'age', pairs)]
  transfers between devices with their start and end apart: 6 -> 9, of which waited for: 1 -> 2; matrix products, arithmetic and copies ran while one was open for 0% -> 0% of each run, Pallas kernels for 48% -> 45%
where the time goes in v3:
time: 30.1 us; the launch traced here: 29.9 us
  Pallas kernels  16.6 us (55%)
  starting transfers between devices  11.3 us (38%)
  waiting for transfers between devices  1.85 us (6%)
    pallas_call x1, Pallas kernels, inner_substeps(): pl.pallas_call(functools.partial(inner_kernel, sides), out_shape=[jax.Sha...  8.01 us
    ppermute x1, starting transfers between devices, body(): lax.ppermute(x, 'age', pairs)  3 us
    pallas_call x1, Pallas kernels, local(): pl.pallas_call(functools.partial(local_kernel, sides), in_specs=[VMEM] +...  2.53 us
    ppermute x1, starting transfers between devices, body(): lax.ppermute(top, 'wear', before)  2.25 us
    ppermute x3, starting transfers between devices, body(): arrived = [lax.ppermute(x, 'cheb', pairs) for x, pairs in zip(q, moves)]  2.21 us
    ppermute x3, starting transfers between devices, body(): lax.ppermute(x, 'cheb', pairs)  2.21 us
    pallas_call x1, Pallas kernels, outer_substeps(): pl.pallas_call(functools.partial(outer_kernel, sides), out_shape=[jax.Sha...  1.67 us
    ppermute x1, starting transfers between devices, body(): lax.ppermute(bottom, 'wear', after)  1.63 us
  transfers between devices with their start and end apart: 9, of which 2 were waited for; matrix products, arithmetic and copies ran while one was open for 0% of the time, Pallas kernels for 45%

profile of v3, /device:TPU:0, one launch (start us, length us, event | category | flops | bytes accessed | tf_op | source)
XLA Modules:
  0.0 29.9 jit_solution(16851637565921175024)
XLA Ops:
  0.0 0.0 copy-start
  0.0 1.3 %age_edges.1.refs_0_ = bf16[384,256]{1,0:T(8,128)(2,1)S(1)} custom-call(f32[64,64,256]{2,1,0:T(8,128)} %u_hbm.1, f32[64,64]{1,0:T(8,128)} %hazard_hbm.3), custom_call_target="tpu_custom_call" | custom-call | bytes 1048576 | tf_op jit(solution)/shard_map/age_edges/pallas_call | solution.py:147
  1.3 3.0 %collective-permute-start = (bf16[384,256]{1,0:T(8,128)(2,1)S(1)}, bf16[384,256]{1,0:T(8,128)(2,1)S(1)}, u32[]{:S(2)}, u32[]{:S(2)}) collective-permute-start(bf16[384,256]{1,0:T(8,128)(2,1)S(1)} %age_edges.1.refs_0_), channel_id=1, source_target_pairs={{0,1},{1,0},{2,3},{3,2},{4,5},{5,4},{6,7},{7,6},{8,9},{9,8},{10,11... | collective-permute-start | bytes 589832 | tf_op jit(solution)/shard_map/ppermute | solution.py:594
  4.3 0.0 copy-done
  4.3 1.5 %pack_coefficients.1 = (bf16[48,2048]{1,0:T(8,128)(2,1)S(1)}, bf16[16,2048]{1,0:T(8,128)(2,1)S(1)}, bf16[48,2048]{1,0:T(8,128)(2,1)S(1)}, bf16[56,256]{1,0:T(8,128)(2,1)S(1)}) custom-call(f32[2,32,64,256]{3,2,1,0:T(8,128)S(1)} %bitcast.4, bf16[4,56,256]{2,1,0:T(8,128)(2,1)} %constant.14.clone.send_hbm, bf16[384,256]{1,0:T(8,128)(2,1)S(1)} %age_edges.1.refs_0_), custom_call_target="tpu_custom_call" | custom-call | flops 117440512 | bytes 4194304 | tf_op jit(solution)/shard_map/pack_coefficients/pallas_call | solution.py:197
  5.9 0.1 collective-permute-start.1
  5.9 1.6 %collective-permute-start.3 = (bf16[48,2048]{1,0:T(8,128)(2,1)S(1)}, bf16[48,2048]{1,0:T(8,128)(2,1)S(1)}, u32[]{:S(2)}, u32[]{:S(2)}) collective-permute-start(bf16[48,2048]{1,0:T(8,128)(2,1)S(1)} %get-tuple-element.31), channel_id=1, source_target_pairs={{0,24},{8,16},{16,8},{24,0},{1,25},{9,17},{17,9},{25,1},{2,26},{10... | collective-permute-start | bytes 589832 | tf_op jit(solution)/shard_map/ppermute | solution.py:597
  7.6 0.5 %collective-permute-start.2 = (bf16[16,2048]{1,0:T(8,128)(2,1)S(1)}, bf16[16,2048]{1,0:T(8,128)(2,1)S(1)}, u32[]{:S(2)}, u32[]{:S(2)}) collective-permute-start(bf16[16,2048]{1,0:T(8,128)(2,1)S(1)} %get-tuple-element.30), channel_id=1, source_target_pairs={{0,16},{8,24},{16,0},{24,8},{1,17},{9,25},{17,1},{25,9},{2,18},{10... | collective-permute-start | bytes 196616 | tf_op jit(solution)/shard_map/ppermute | solution.py:597
  8.1 1.2 %collective-permute-done.refs_0_ = bf16[384,256]{1,0:T(8,128)(2,1)S(1)} collective-permute-done((bf16[384,256]{1,0:T(8,128)(2,1)S(1)}, bf16[384,256]{1,0:T(8,128)(2,1)S(1)}, u32[]{:S(2)}, u32[]{:S(2)}) %collective-permute-start) | collective-permute-done | bytes 196640 | tf_op jit(solution)/shard_map/ppermute | solution.py:594
  9.2 0.0 collective-permute-done.1.refs_1_
  9.2 0.2 pack_edges.1
  9.4 1.8 %collective-permute-start.5 = (bf16[16,128]{1,0:T(8,128)(2,1)S(1)}, bf16[16,128]{1,0:T(8,128)(2,1)S(1)}, u32[]{:S(2)}, u32[]{:S(2)}) collective-permute-start(bf16[16,128]{1,0:T(8,128)(2,1)S(1)} %get-tuple-element.33), channel_id=1, source_target_pairs={{0,16},{8,24},{16,0},{24,8},{1,17},{9,25},{17,1},{25,9},{2,18},{10... | collective-permute-start | bytes 12296 | tf_op jit(solution)/shard_map/ppermute | solution.py:599
  11.2 0.0 collective-permute-start.4
  11.2 0.4 %collective-permute-start.6 = (bf16[48,128]{1,0:T(8,128)(2,1)S(1)}, bf16[48,128]{1,0:T(8,128)(2,1)S(1)}, u32[]{:S(2)}, u32[]{:S(2)}) collective-permute-start(bf16[48,128]{1,0:T(8,128)(2,1)S(1)} %get-tuple-element.34), channel_id=1, source_target_pairs={{0,24},{8,16},{16,8},{24,0},{1,25},{9,17},{17,9},{25,1},{2,26},{10... | collective-permute-start | bytes 36872 | tf_op jit(solution)/shard_map/ppermute | solution.py:599
  11.6 2.5 %local_rate.1 = (f32[2,72,96,128]{3,2,1,0:T(8,128)S(1)}, f32[1,256,256]{2,1,0:T(8,128)S(1)}, f32[2,256,256]{2,1,0:T(8,128)S(1)}, bf16[2,80,256]{2,1,0:T(8,128)(2,1)S(1)}) custom-call(f32[2,32,64,256]{3,2,1,0:T(8,128)S(1)} %bitcast.5, f32[64,64]{1,0:T(8,128)} %hazard_hbm.3, f32[4,1,256]{2,1,0:T(1,128)} %bitcast.8, f32[4,1,256]{2,1,0:T(1,128)} %bitcast.9, ...), custom_call_target="tpu_custom_call" | custom-call | flops 536870912 | bytes 8388608 | tf_op jit(solution)/shard_map/local_rate/pallas_call | solution.py:290
  14.1 0.6 %collective-permute-done.2.refs_1_ = bf16[16,2048]{1,0:T(8,128)(2,1)S(1)} collective-permute-done((bf16[16,2048]{1,0:T(8,128)(2,1)S(1)}, bf16[16,2048]{1,0:T(8,128)(2,1)S(1)}, u32[]{:S(2)}, u32[]{:S(2)}) %collective-permute-start.2) | collective-permute-done | bytes 65568 | tf_op jit(solution)/shard_map/ppermute | solution.py:597
  14.8 0.0 collective-permute-done.3.refs_2_
  14.8 0.0 collective-permute-done.5.refs_4_
  14.8 0.0 collective-permute-done.4.refs_3_
  14.8 0.0 collective-permute-done.6.refs_5_
  14.8 0.3 outer_rows.1
  15.1 1.6 %collective-permute-start.7 = (bf16[272,256]{1,0:T(8,128)(2,1)S(1)}, bf16[272,256]{1,0:T(8,128)(2,1)S(1)}, u32[]{:S(2)}, u32[]{:S(2)}) collective-permute-start(bf16[272,256]{1,0:T(8,128)(2,1)S(1)} %get-tuple-element.40), channel_id=1, source_target_pairs={{0,2},{2,4},{4,6},{6,0},{1,3},{3,5},{5,7},{7,1},{8,10},{10,12},{12... | collective-permute-start | bytes 417800 | tf_op jit(solution)/shard_map/ppermute | solution.py:603
  16.8 2.2 %collective-permute-start.8 = (bf16[272,256]{1,0:T(8,128)(2,1)S(1)}, bf16[272,256]{1,0:T(8,128)(2,1)S(1)}, u32[]{:S(2)}, u32[]{:S(2)}) collective-permute-start(bf16[272,256]{1,0:T(8,128)(2,1)S(1)} %get-tuple-element.41), channel_id=1, source_target_pairs={{2,0},{4,2},{6,4},{0,6},{3,1},{5,3},{7,5},{1,7},{10,8},{12,10},{14... | collective-permute-start | bytes 417800 | tf_op jit(solution)/shard_map/ppermute | solution.py:603
  19.0 0.0 copy-start.1
  19.0 1.1 %section.1.z0.z0_in = f32[2,72,96,128]{3,2,1,0:T(8,128)S(1)} custom-call(f32[2,72,96,128]{3,2,1,0:T(8,128)S(1)} %get-tuple-element.24.z_in, f32[1,256,256]{2,1,0:T(8,128)S(1)} %get-tuple-element.25.beside_ref, bf16[2,80,256]{2,1,0:T(8,128)(2,1)S(1)} %get-tuple-element.26.take_ref, ...), custom_call_target="tpu_custom_call", output_to_operand_aliasing={{}: (0, {})} | custom-call | flops 167772160 | bytes 8388608 | tf_op jit(solution)/shard_map/section/pallas_call | solution.py:392
  20.1 0.0 copy-done.1
  20.1 8.0 %inner_substeps.1 = (f32[64,64,256]{2,1,0:T(8,128)}, f32[2,72,96,128]{3,2,1,0:T(8,128)S(1)}, f32[2,72,96,128]{3,2,1,0:T(8,128)S(1)}, f32[2,72,96,128]{3,2,1,0:T(8,128)S(1)}) custom-call(f32[2,72,96,128]{3,2,1,0:T(8,128)S(1)} %section.1.z0.z0_in, f32[1,256]{1,0:T(1,128)S(1)} %bitcast.6), custom_call_target="tpu_custom_call" | custom-call | flops 41943040 | bytes 8388608 | tf_op jit(solution)/shard_map/inner_substeps/pallas_call | solution.py:498
  28.2 0.0 collective-permute-done.7.up_ref
  28.2 0.0 collective-permute-done.8.down_ref
  28.2 1.7 %outer_substeps.1 = (f32[64,64,256]{2,1,0:T(8,128)}, f32[2,72,96,128]{3,2,1,0:T(8,128)S(1)}, f32[2,72,96,128]{3,2,1,0:T(8,128)S(1)}, f32[2,72,96,128]{3,2,1,0:T(8,128)S(1)}, f32[2,72,96,128]{3,2,1,0:T(8,128)S(1)}) custom-call(f32[64,64,256]{2,1,0:T(8,128)} %get-tuple-element.35.o_in, ...), custom_call_target="tpu_custom_call", output_to_operand_aliasing={{0}: (0, {}), {1}: (1, {}), {2}: (2, {}), {3}: (3, {}), {4}... | custom-call | flops 10485760 | bytes 1048576 | tf_op jit(solution)/shard_map/outer_substeps/pallas_call | solution.py:561
Async XLA Ops:
  0.0 4.3 %copy-start = (f32[64,64,256]{2,1,0:T(8,128)S(1)}, f32[64,64,256]{2,1,0:T(8,128)}, u32[]{:S(2)}) copy-start(f32[64,64,256]{2,1,0:T(8,128)} %u_hbm.1) | copy-start | bytes 12582916
  1.3 7.9 %collective-permute-start = (bf16[384,256]{1,0:T(8,128)(2,1)S(1)}, bf16[384,256]{1,0:T(8,128)(2,1)S(1)}, u32[]{:S(2)}, u32[]{:S(2)}) collective-permute-start(bf16[384,256]{1,0:T(8,128)(2,1)S(1)} %age_edges.1.refs_0_), channel_id=1, source_target_pairs={{0,1},{1,0},{2,3},{3,2},{4,5},{5,4},{6,7},{7,6},{8,9},{9,8},{10,11... | collective-permute-start | bytes 589832 | tf_op jit(solution)/shard_map/ppermute | solution.py:594
  5.9 3.4 %collective-permute-start.1 = (bf16[48,2048]{1,0:T(8,128)(2,1)S(1)}, bf16[48,2048]{1,0:T(8,128)(2,1)S(1)}, u32[]{:S(2)}, u32[]{:S(2)}) collective-permute-start(bf16[48,2048]{1,0:T(8,128)(2,1)S(1)} %get-tuple-element.28), channel_id=1, source_target_pairs={{0,8},{8,0},{16,24},{24,16},{1,9},{9,1},{17,25},{25,17},{2,10},{10... | collective-permute-start | bytes 589832 | tf_op jit(solution)/shard_map/ppermute | solution.py:597
  5.9 8.9 %collective-permute-start.3 = (bf16[48,2048]{1,0:T(8,128)(2,1)S(1)}, bf16[48,2048]{1,0:T(8,128)(2,1)S(1)}, u32[]{:S(2)}, u32[]{:S(2)}) collective-permute-start(bf16[48,2048]{1,0:T(8,128)(2,1)S(1)} %get-tuple-element.31), channel_id=1, source_target_pairs={{0,24},{8,16},{16,8},{24,0},{1,25},{9,17},{17,9},{25,1},{2,26},{10... | collective-permute-start | bytes 589832 | tf_op jit(solution)/shard_map/ppermute | solution.py:597
  7.6 7.2 %collective-permute-start.2 = (bf16[16,2048]{1,0:T(8,128)(2,1)S(1)}, bf16[16,2048]{1,0:T(8,128)(2,1)S(1)}, u32[]{:S(2)}, u32[]{:S(2)}) collective-permute-start(bf16[16,2048]{1,0:T(8,128)(2,1)S(1)} %get-tuple-element.30), channel_id=1, source_target_pairs={{0,16},{8,24},{16,0},{24,8},{1,17},{9,25},{17,1},{25,9},{2,18},{10... | collective-permute-start | bytes 196616 | tf_op jit(solution)/shard_map/ppermute | solution.py:597
  9.4 5.4 %collective-permute-start.5 = (bf16[16,128]{1,0:T(8,128)(2,1)S(1)}, bf16[16,128]{1,0:T(8,128)(2,1)S(1)}, u32[]{:S(2)}, u32[]{:S(2)}) collective-permute-start(bf16[16,128]{1,0:T(8,128)(2,1)S(1)} %get-tuple-element.33), channel_id=1, source_target_pairs={{0,16},{8,24},{16,0},{24,8},{1,17},{9,25},{17,1},{25,9},{2,18},{10... | collective-permute-start | bytes 12296 | tf_op jit(solution)/shard_map/ppermute | solution.py:599
  11.2 3.6 %collective-permute-start.4 = (bf16[48,128]{1,0:T(8,128)(2,1)S(1)}, bf16[48,128]{1,0:T(8,128)(2,1)S(1)}, u32[]{:S(2)}, u32[]{:S(2)}) collective-permute-start(bf16[48,128]{1,0:T(8,128)(2,1)S(1)} %get-tuple-element.32), channel_id=1, source_target_pairs={{0,8},{8,0},{16,24},{24,16},{1,9},{9,1},{17,25},{25,17},{2,10},{10... | collective-permute-start | bytes 36872 | tf_op jit(solution)/shard_map/ppermute | solution.py:599
  11.2 3.6 %collective-permute-start.6 = (bf16[48,128]{1,0:T(8,128)(2,1)S(1)}, bf16[48,128]{1,0:T(8,128)(2,1)S(1)}, u32[]{:S(2)}, u32[]{:S(2)}) collective-permute-start(bf16[48,128]{1,0:T(8,128)(2,1)S(1)} %get-tuple-element.34), channel_id=1, source_target_pairs={{0,24},{8,16},{16,8},{24,0},{1,25},{9,17},{17,9},{25,1},{2,26},{10... | collective-permute-start | bytes 36872 | tf_op jit(solution)/shard_map/ppermute | solution.py:599
  15.1 13.0 %collective-permute-start.7 = (bf16[272,256]{1,0:T(8,128)(2,1)S(1)}, bf16[272,256]{1,0:T(8,128)(2,1)S(1)}, u32[]{:S(2)}, u32[]{:S(2)}) collective-permute-start(bf16[272,256]{1,0:T(8,128)(2,1)S(1)} %get-tuple-element.40), channel_id=1, source_target_pairs={{0,2},{2,4},{4,6},{6,0},{1,3},{3,5},{5,7},{7,1},{8,10},{10,12},{12... | collective-permute-start | bytes 417800 | tf_op jit(solution)/shard_map/ppermute | solution.py:603
  16.8 11.4 %collective-permute-start.8 = (bf16[272,256]{1,0:T(8,128)(2,1)S(1)}, bf16[272,256]{1,0:T(8,128)(2,1)S(1)}, u32[]{:S(2)}, u32[]{:S(2)}) collective-permute-start(bf16[272,256]{1,0:T(8,128)(2,1)S(1)} %get-tuple-element.41), channel_id=1, source_target_pairs={{2,0},{4,2},{6,4},{0,6},{3,1},{5,3},{7,5},{1,7},{10,8},{12,10},{14... | collective-permute-start | bytes 417800 | tf_op jit(solution)/shard_map/ppermute | solution.py:603
  19.0 1.1 %copy-start.1 = (f32[256]{0:T(256)S(1)}, f32[256]{0:T(256)}, u32[]{:S(2)}) copy-start(f32[256]{0:T(256)} %param.13) | copy-start | bytes 3076

commit v4 on v3

--- a/solution.py
+++ b/solution.py
@@ -16,6 +16,8 @@
 coupling = 0.05
 GAIN = 1.0 / coupling
 START = coupling**SUBSTEPS
+
+NEGLIGIBLE = 2.0**-32
 
 f32 = jnp.float32
 bf16 = jnp.bfloat16
@@ -47,7 +49,7 @@
             b = c ^ shift if devices & (devices - 1) == 0 else (c + shift) % devices
             joint = np.concatenate([second[parts[b], parts[c]], first[parts[b], parts[c]]])
             _, sizes, rows = np.linalg.svd(joint, full_matrices=False)
-            rank = int((sizes > joint.shape[0] * np.finfo(np.float64).eps).sum())
+            rank = int((sizes > NEGLIGIBLE).sum())
             rank = -(-rank // 8) * 8
             basis = rows[:rank]
             found[c, b] = (basis, second[parts[b], parts[c]] @ basis.T, first[parts[b], parts[c]] @ basis.T)
@@ -139,7 +141,9 @@
         rows = jnp.concatenate([high, exact - high, jnp.zeros((HAZARD_ROWS - 2 * HALO, wears), f32)], axis=0)
         rows = jnp.concatenate([rows, jnp.zeros((HAZARD_ROWS, size - wears), f32)], axis=1)
         out_ref[wears * HALO : wears * HALO + HAZARD_ROWS] = rows.astype(bf16)
-        out_ref[wears * HALO + HAZARD_ROWS :] = jnp.zeros_like(out_ref[wears * HALO + HAZARD_ROWS :])
+        used = wears * HALO + HAZARD_ROWS
+        if out_ref.shape[0] > used:
+            out_ref[used:] = jnp.zeros((out_ref.shape[0] - used, size), bf16)
 
 
 def edges(u, hazard, sides, rows):
@@ -175,13 +179,19 @@
     return lax.dot_general(table, cells, (((1,), (1,)), ((), ())), preferred_element_type=f32)
 
 
-def pack_kernel(ranks, sides, u_ref, send_hbm, *refs):
-    q_refs, (send, send_sem) = refs[sides : sides + len(ranks)], refs[sides + len(ranks) :]
+def pack_kernel(ranks, u_ref, *refs):
+    shared, refs = refs[:SHARED], refs[SHARED:]
+    tables, refs = refs[:TABLES], refs[-(len(ranks) + SHARED + TABLES + 1) :]
+    q_refs, send = refs[: len(ranks)], refs[len(ranks)]
+    copied, sem = refs[len(ranks) + 1 : -1], refs[-1]
     _, wears, ages, size = u_ref.shape
+    at = lax.axis_index("cheb")
+    sources = [t.at[at] for t in tables[:1]] + list(shared) + [t.at[at] for t in tables[1:]]
+    copies = [pltpu.make_async_copy(a, b, sem.at[i]) for i, (a, b) in enumerate(zip(sources, (send, *copied)))]
+    for copy in copies:
+        copy.start()
+    copies[0].wait()
     chunk = 4
-    table = pltpu.make_async_copy(send_hbm.at[lax.axis_index("cheb")], send, send_sem)
-    table.start()
-    table.wait()
     for g in range(wears // chunk):
         halves = [
             analyse(send[...], u_ref[half, g * chunk : (g + 1) * chunk].reshape(chunk * ages, size).astype(bf16))
@@ -189,21 +199,28 @@
         ]
         for q_ref, rows in zip(q_refs, pack_rows(ranks, halves)):
             q_ref[:, g * chunk * ages : (g + 1) * chunk * ages] = rows
-
-
-def pack(u4, send, edge, ranks):
+    for copy in copies[1:]:
+        copy.wait()
+
+
+SHARED, TABLES = 1, 7
+
+
+def pack(u4, hazard, tables, edge, ranks):
     _, wears, ages, size = u4.shape
     cells = wears * ages
-    return pl.pallas_call(
-        functools.partial(pack_kernel, ranks, len(edge)),
-        in_specs=[VMEM, ANY] + [ANY] * len(edge),
-        out_specs=[VMEM] * (len(ranks) + 1),
-        out_shape=[PIN((2 * r, cells), bf16) for r in ranks] + [PIN(send.shape[1:], bf16)],
-        scratch_shapes=[pltpu.SemaphoreType.DMA],
+    copied = [PIN(hazard.shape, f32)] + [PIN(t.shape[1:], f32) for t in tables[1:]]
+    out = pl.pallas_call(
+        functools.partial(pack_kernel, ranks),
+        in_specs=[VMEM] + [ANY] * (SHARED + TABLES + len(edge)),
+        out_specs=[VMEM] * (len(ranks) + SHARED + TABLES),
+        out_shape=[PIN((2 * r, cells), bf16) for r in ranks] + [PIN(tables[0].shape[1:], bf16)] + copied,
+        scratch_shapes=[pltpu.SemaphoreType.DMA((SHARED + TABLES,))],
         compiler_params=params(16),
         cost_estimate=cost(4 * cells * sum(ranks) * size, 8 * cells * size),
         name="pack_coefficients",
-    )(in_vmem(u4), in_hbm(send), *[in_vmem(x) for x in edge])
+    )(in_vmem(u4), *[in_hbm(x) for x in (hazard, *tables)], *[in_vmem(x) for x in edge])
+    return out[: len(ranks)], out[len(ranks)], out[len(ranks) + 1 :]
 
 
 def pack_edges_kernel(ranks, sides, send_ref, *refs):
@@ -230,27 +247,18 @@
     )(*[in_vmem(x) for x in (send, *near, arrived)])
 
 
-def local_kernel(sides, u_ref, hazard_hbm, diffusion_hbm, drift_hbm, second_hbm, first_hbm, take_second_hbm,
-                 take_first_hbm, *refs):
-    edge_refs, refs = refs[:sides], refs[sides:]
-    z, beside, ends, take, hazard, diffusion, drift, second, first, own, take_second, take_first, sem = refs
+def local_kernel(sides, u_ref, hazard, diffusion, drift, second, first, take_second, take_first, *refs):
+    edge_refs, fields, (beside, ends, take, own) = refs[:sides], refs[sides : sides + SUBSTEPS], refs[sides + SUBSTEPS :]
+    z = fields[0]
     halves, rows, _, _ = z.shape
     _, wears, ages, size = u_ref.shape
-    at = lax.axis_index("cheb")
-    moves = (
-        (second_hbm.at[at], second), (first_hbm.at[at], first), (diffusion_hbm.at[at], diffusion),
-        (drift_hbm.at[at], drift), (hazard_hbm, hazard), (take_second_hbm.at[at], take_second),
-        (take_first_hbm.at[at], take_first),
-    )
-    copies = [pltpu.make_async_copy(src, dst, sem.at[i]) for i, (src, dst) in enumerate(moves)]
-    for copy in copies:
-        copy.start()
     for l in range(halves):
         zero = jnp.zeros((rows, 16, 128), f32)
         z[l, :, :ROW0, :] = zero
         z[l, :, ROW0 + ages :, :] = zero
-    for copy in copies:
-        copy.wait()
+        for later in fields[1:]:
+            later[l, :, ROW0 - 8 : ROW0, :] = zero[:, :8]
+            later[l, :, ROW0 + ages : ROW0 + ages + 8, :] = zero[:, :8]
     scaled, moved = START * diffusion[...], START * drift[...]
     own[...] = (second[...] * scaled + first[...] * moved).astype(bf16)
     take[...] = (take_second[...] * scaled + take_first[...] * moved).astype(bf16)
@@ -272,46 +280,31 @@
         count = 2 * wears * HALO
         parts = ref[count : count + HAZARD_ROWS].astype(f32)
         near = START - START * (parts[:HALO, : 2 * wears] + parts[HALO : 2 * HALO, : 2 * wears])
-        near = jnp.concatenate([near, near], axis=0)
+        rate = jnp.dot(ref[:count], own[...], preferred_element_type=f32)
         for w in range(0, 2 * wears, 4):
             place = slice(w * HALO, (w + 4) * HALO)
-            u = ref[place]
-            rate = jnp.dot(u, own[...], preferred_element_type=f32)
-            columns = [
-                jnp.broadcast_to(near[:HALO, w + j : w + j + 1], (HALO, size)) for j in range(4)
-            ]
-            beside[s, place] = rate + jnp.concatenate(columns, axis=0) * u.astype(f32)
-
-
-def local(u4, hazard, diffusion, drift, tables, near, sides):
+            columns = [jnp.broadcast_to(near[:, w + j : w + j + 1], (HALO, size)) for j in range(4)]
+            beside[s, place] = rate[place] + jnp.concatenate(columns, axis=0) * ref[place].astype(f32)
+
+
+def local(u4, tables, near, sides):
     _, wears, ages, size = u4.shape
     cells = 2 * wears * ages
-    wide = tables[2].shape[2]
     return pl.pallas_call(
         functools.partial(local_kernel, sides),
-        in_specs=[VMEM] + [ANY] * 7 + [VMEM] * sides,
-        out_specs=[VMEM] * 4,
-        out_shape=[
-            pltpu.VMEM((size // 128, 2 * wears + 2 * HALO, ages + 32, 128), f32),
+        in_specs=[VMEM] * (1 + len(tables) + sides),
+        out_specs=[VMEM] * (SUBSTEPS + 3),
+        out_shape=[pltpu.VMEM((size // 128, 2 * wears + 2 * HALO, ages + 32, 128), f32)] * SUBSTEPS
+        + [
             pltpu.VMEM((sides, 2 * wears * HALO, size), f32),
             pltpu.VMEM((2, HALO * ages, size), f32),
-            pltpu.VMEM((2, wide, size), bf16),
+            pltpu.VMEM(tables[-1].shape, bf16),
         ],
-        scratch_shapes=[
-            pltpu.VMEM(hazard.shape, f32),
-            pltpu.VMEM((1, size), f32),
-            pltpu.VMEM((1, size), f32),
-            pltpu.VMEM((size, size), f32),
-            pltpu.VMEM((size, size), f32),
-            pltpu.VMEM((size, size), bf16),
-            pltpu.VMEM((2, wide, size), f32),
-            pltpu.VMEM((2, wide, size), f32),
-            pltpu.SemaphoreType.DMA((7,)),
-        ],
+        scratch_shapes=[pltpu.VMEM((size, size), bf16)],
         compiler_params=params(16),
         cost_estimate=cost(2 * cells * size * size, 8 * cells * size),
         name="local_rate",
-    )(in_vmem(u4), *[in_hbm(x) for x in (hazard, diffusion, drift, *tables)], *[in_vmem(x) for x in near])
+    )(*[in_vmem(x) for x in (u4, *tables, *near)])
 
 
 def distant(ranks, q_refs, take_ref, half, columns):
@@ -426,6 +419,11 @@
 
     _, _, less0 = row_terms(src, l, start - 1, lo, hi, *factors)
     centre1, _, less1 = row_terms(src, l, start, lo, hi, *factors)
+    if stop - start == unroll:
+        carry = (centre1 + less0, less1)
+        for w in range(start, stop):
+            carry = step(w, carry)
+        return
     lax.fori_loop(start, stop, step, (centre1 + less0, less1), unroll=unroll)
 
 
@@ -452,67 +450,75 @@
         run(ROW0 - 8, ROW0 + ages + 8, [jnp.zeros((8, 128), f32) + h for h in has])
 
 
-def inner_kernel(sides, z0, speed_ref, o_ref, z1, z2, z3, stage, out_sem):
+def inner_kernel(sides, z0, z1_in, z2_in, z3_in, speed_ref, o_ref, rest, z1, z2, z3, stage, out_sem):
+    del z1_in, z2_in, z3_in
     halves, rows, _, _ = z0.shape
-    count, ages = stage.shape[:2]
+    done, ages = stage.shape[:2]
     fields = (z0, z1, z2, z3)
 
     def run(low, high, keeps):
-        for z in fields[1:]:
-            for l in range(halves):
-                if low == ROW0:
-                    z[l, :, ROW0 - 8 : ROW0, :] = jnp.zeros((rows, 8, 128), f32)
-                if high == ROW0 + ages:
-                    z[l, :, high : high + 8, :] = jnp.zeros((rows, 8, 128), f32)
         for k in range(1, SUBSTEPS):
             for l in range(halves):
                 rows_step(
                     fields[k - 1], l, HALO + k, rows - HALO - k, low, high, lane_terms(speed_ref, l),
-                    put_in(fields[k], l, low, high, keeps), 2,
+                    put_in(fields[k], l, low, high, keeps), 4,
                 )
         stores = []
         first = HALO + SUBSTEPS
-        bounds = [0, count * 3 // 7, count * 5 // 7, count * 6 // 7, count]
+        bounds = [0, done * 3 // 5 // 8 * 8, done, done + rest.shape[0]]
         for a, b in zip(bounds, bounds[1:]):
             for l in range(halves):
-                def put(w, out, l=l):
-                    stage[w - first, :, l * 128 : (l + 1) * 128] = out
+                def put(w, out, l=l, a=a):
+                    if a < done:
+                        stage[w - first, :, l * 128 : (l + 1) * 128] = out
+                    else:
+                        rest[w - first - done, :, l * 128 : (l + 1) * 128] = out
 
                 rows_step(
                     fields[-1], l, first + a, first + b, ROW0, ROW0 + ages, lane_terms(speed_ref, l), put, 4,
                 )
-            copy = pltpu.make_async_copy(
-                stage.at[pl.ds(a, b - a)], o_ref.at[pl.ds(SUBSTEPS + a, b - a)], out_sem.at[len(stores)]
-            )
-            copy.start()
-            stores.append(copy)
+            if a < done:
+                copy = pltpu.make_async_copy(
+                    stage.at[pl.ds(a, b - a)], o_ref.at[pl.ds(SUBSTEPS + a, b - a)], out_sem.at[len(stores)]
+                )
+                copy.start()
+                stores.append(copy)
         for copy in stores:
             copy.wait()
 
     by_sides(sides, ages, run)
 
 
-def inner_substeps(z, speed, sides, wears, ages):
+def inner_substeps(fields, speed, sides, wears, ages):
+    z = fields[0]
     size = z.shape[0] * 128
     shape = (wears, ages, size)
+    kept = 16
     return pl.pallas_call(
         functools.partial(inner_kernel, sides),
-        out_shape=[jax.ShapeDtypeStruct(shape, f32)] + [pltpu.VMEM(z.shape, f32)] * 3,
-        in_specs=[VMEM] * 2,
-        out_specs=[ANY] + [VMEM] * 3,
-        scratch_shapes=[pltpu.VMEM((wears - 2 * SUBSTEPS, ages, size), f32), pltpu.SemaphoreType.DMA((4,))],
+        out_shape=[jax.ShapeDtypeStruct(shape, f32), pltpu.VMEM((kept, ages, size), f32)] + [pltpu.VMEM(z.shape, f32)] * 3,
+        in_specs=[VMEM] * 5,
+        out_specs=[ANY] + [VMEM] * 4,
+        scratch_shapes=[
+            pltpu.VMEM((wears - 2 * SUBSTEPS - kept, ages, size), f32),
+            pltpu.SemaphoreType.DMA((2,)),
+        ],
+        input_output_aliases={1: 2, 2: 3, 3: 4},
         compiler_params=params(16),
         cost_estimate=cost(10 * SUBSTEPS * wears * ages * size, 8 * wears * ages * size),
         name="inner_substeps",
-    )(in_vmem(z), speed)
-
-
-def outer_kernel(sides, o_in, z0_in, z1_in, z2_in, z3_in, speed_ref, up_ref, down_ref, o_ref, z0, z1, z2, z3,
+    )(*[in_vmem(x) for x in fields], speed)
+
+
+def outer_kernel(sides, o_in, z0_in, z1_in, z2_in, z3_in, rest, speed_ref, up_ref, down_ref, o_ref, z0, z1, z2, z3,
                  stage, out_sem):
     del o_in, z0_in, z1_in, z2_in, z3_in
     halves, rows, _, _ = z0.shape
     wears, ages = rows - 2 * HALO, stage.shape[2]
     fields = (z0, z1, z2, z3)
+    count = rest.shape[0]
+    stores = [pltpu.make_async_copy(rest, o_ref.at[pl.ds(wears - SUBSTEPS - count, count)], out_sem.at[2])]
+    stores[0].start()
     has = [jnp.where(at_end("age", i == 1), 0.0, 1.0).astype(f32) for i in range(2)]
     near = [jnp.where(at_end("wear", i == 1), 0.0, 1.0).astype(f32) for i in range(2)]
     for l in range(halves):
@@ -540,35 +546,34 @@
                             lambda w, e=e, beyond=beyond: jnp.where(beyond(w), near[e], 1.0).astype(f32),
                         ), 4,
                     )
-        stores = []
         for e, start in enumerate((HALO, rows - 2 * HALO)):
             for l in range(halves):
                 def put(w, out, l=l, e=e, start=start):
                     stage[e, w - start, :, l * 128 : (l + 1) * 128] = out
 
                 rows_step(fields[-1], l, start, start + HALO, ROW0, ROW0 + ages, lane_terms(speed_ref, l), put, 4)
-            copy = pltpu.make_async_copy(stage.at[e], o_ref.at[pl.ds(start - HALO, HALO)], out_sem.at[e])
-            copy.start()
-            stores.append(copy)
-        for copy in stores:
-            copy.wait()
+            pltpu.make_async_copy(stage.at[e], o_ref.at[pl.ds(start - HALO, HALO)], out_sem.at[e]).start()
 
     by_sides(sides, ages, run)
-
-
-def outer_substeps(o, fields, speed, up, down, sides):
+    for e, start in enumerate((HALO, rows - 2 * HALO)):
+        stores.append(pltpu.make_async_copy(stage.at[e], o_ref.at[pl.ds(start - HALO, HALO)], out_sem.at[e]))
+    for copy in stores:
+        copy.wait()
+
+
+def outer_substeps(o, fields, rest, speed, up, down, sides):
     wears, ages, size = o.shape
     return pl.pallas_call(
         functools.partial(outer_kernel, sides),
         out_shape=[jax.ShapeDtypeStruct(o.shape, f32)] + [pltpu.VMEM(z.shape, f32) for z in fields],
-        in_specs=[ANY] + [VMEM] * 7,
+        in_specs=[ANY] + [VMEM] * 8,
         out_specs=[ANY] + [VMEM] * 4,
-        scratch_shapes=[pltpu.VMEM((2, HALO, ages, size), f32), pltpu.SemaphoreType.DMA((2,))],
+        scratch_shapes=[pltpu.VMEM((2, HALO, ages, size), f32), pltpu.SemaphoreType.DMA((3,))],
         input_output_aliases={i: i for i in range(5)},
         compiler_params=params(16),
         cost_estimate=cost(20 * SUBSTEPS * 2 * HALO * ages * size, 2**20),
         name="outer_substeps",
-    )(o, *fields, speed, in_vmem(up), in_vmem(down))[0]
+    )(o, *[in_vmem(x) for x in (*fields, rest)], speed, in_vmem(up), in_vmem(down))[0]
 
 
 def body(adjoint_value, load_diffusion, load_drift, wear_speed, hazard):
@@ -592,19 +597,19 @@
     most = 2 * max(ranks) * (wears // 2 * ages) // size
     edge = edges(adjoint_value, hazard, sides, max(wears * HALO + HAZARD_ROWS, -(-most // 16) * 16))
     near = [lax.ppermute(x, "age", pairs) for x, pairs in zip(edge, ring(n_age))]
-    *q, send = pack(u4, jnp.asarray(send, bf16), edge, ranks)
+    q, send, tables = pack(u4, hazard, [jnp.asarray(send, bf16), diffusion, drift, *tables], edge, ranks)
     moves = [list(pairs) for pairs, _ in slots]
     arrived = [lax.ppermute(x, "cheb", pairs) for x, pairs in zip(q, moves)]
     arrived[0], *q_edges = pack_edges(send, near, arrived[0], ranks, sides, extra)
     arrived_edges = [lax.ppermute(x, "cheb", pairs) for x, pairs in zip(q_edges, moves)]
-    z, beside, ends, take = local(u4, hazard, diffusion, drift, tables, near, sides)
+    z, *later, beside, ends, take = local(u4, tables, near, sides)
     top, bottom = outer_rows(ends, beside, take, arrived, arrived_edges, ranks, sides, wears, ages)
     after, before = ring(n_wear)
     up, down = lax.ppermute(bottom, "wear", after), lax.ppermute(top, "wear", before)
     z = section(z, beside, take, arrived, arrived_edges, ranks, sides, wears, ages)
     speed = wear_speed.reshape(1, size)
-    o, *fields = inner_substeps(z, speed, sides, wears, ages)
-    return outer_substeps(o, [z, *fields], speed, up, down, sides)
+    o, rest, *later = inner_substeps([z, *later], speed, sides, wears, ages)
+    return outer_substeps(o, [z, *later], rest, speed, up, down, sides)
 
 
 def solution(mesh):

time: 30.1 us -> 27.6 us (0.917)
  Pallas kernels: 16.6 us -> 14.8 us
  waiting for transfers between devices: 1.85 us -> 1.28 us
    ppermute x1, waiting for transfers between devices: 1.16 us -> 0.01 us  [body(): lax.ppermute(x, 'age', pairs)]
    pallas_call x1, Pallas kernels: 8.01 us -> 7.03 us  [inner_substeps(): pl.pallas_call(functools.partial(inner_kernel, sides), out_shape=[jax.Sha...]
    pallas_call x2, Pallas kernels: 4.04 us -> 3.24 us  [the longest x1 1.69 us: local(): pl.pallas_call(functools.partial(local_kernel, sides), in_specs=[VMEM] *...]
    ppermute x3, waiting for transfers between devices: 0.64 us -> 1.22 us  [body(): arrived = [lax.ppermute(x, 'cheb', pairs) for x, pairs in zip(q, moves)]]
  transfers between devices with their start and end apart: 9 -> 9, of which waited for: 2 -> 1; matrix products, arithmetic and copies ran while one was open for 0% -> 0% of each run, Pallas kernels for 45% -> 42%
where the time goes in v4:
time: 27.6 us; the launch traced here: 27.4 us
  Pallas kernels  14.8 us (54%)
  starting transfers between devices  11.3 us (41%)
  waiting for transfers between devices  1.28 us (5%)
    pallas_call x1, Pallas kernels, inner_substeps(): pl.pallas_call(functools.partial(inner_kernel, sides), out_shape=[jax.Sha...  7.03 us
    ppermute x1, starting transfers between devices, body(): lax.ppermute(x, 'age', pairs)  3 us
    ppermute x1, starting transfers between devices, body(): lax.ppermute(top, 'wear', before)  2.26 us
    ppermute x3, starting transfers between devices, body(): arrived = [lax.ppermute(x, 'cheb', pairs) for x, pairs in zip(q, moves)]  2.21 us
    ppermute x3, starting transfers between devices, body(): lax.ppermute(x, 'cheb', pairs)  2.2 us
    pallas_call x1, Pallas kernels, local(): pl.pallas_call(functools.partial(local_kernel, sides), in_specs=[VMEM] *...  1.69 us
    pallas_call x1, Pallas kernels, outer_substeps(): pl.pallas_call(functools.partial(outer_kernel, sides), out_shape=[jax.Sha...  1.66 us
    ppermute x1, starting transfers between devices, body(): lax.ppermute(bottom, 'wear', after)  1.62 us
  transfers between devices with their start and end apart: 9, of which 1 were waited for; matrix products, arithmetic and copies ran while one was open for 0% of the time, Pallas kernels for 42%

profile of v4, /device:TPU:0, one launch (start us, length us, event | category | flops | bytes accessed | tf_op | source)
XLA Modules:
  0.0 27.4 jit_solution(5334743629116994998)
XLA Ops:
  0.0 0.0 copy-start
  0.0 1.3 %age_edges.1.refs_8_ = bf16[272,256]{1,0:T(8,128)(2,1)S(1)} custom-call(f32[64,64,256]{2,1,0:T(8,128)} %u_hbm.1, f32[64,64]{1,0:T(8,128)} %refs_0_.1), custom_call_target="tpu_custom_call" | custom-call | bytes 1048576 | tf_op jit(solution)/shard_map/age_edges/pallas_call | solution.py:151
  1.3 3.0 %collective-permute-start = (bf16[272,256]{1,0:T(8,128)(2,1)S(1)}, bf16[272,256]{1,0:T(8,128)(2,1)S(1)}, u32[]{:S(2)}, u32[]{:S(2)}) collective-permute-start(bf16[272,256]{1,0:T(8,128)(2,1)S(1)} %age_edges.1.refs_8_), channel_id=1, source_target_pairs={{0,1},{1,0},{2,3},{3,2},{4,5},{5,4},{6,7},{7,6},{8,9},{9,8},{10,11... | collective-permute-start | bytes 417800 | tf_op jit(solution)/shard_map/ppermute | solution.py:599
  4.3 0.0 copy-done
  4.3 1.5 %pack_coefficients.1 = (bf16[32,2048]{1,0:T(8,128)(2,1)S(1)}, bf16[16,2048]{1,0:T(8,128)(2,1)S(1)}, bf16[32,2048]{1,0:T(8,128)(2,1)S(1)}, bf16[40,256]{1,0:T(8,1...) custom-call(f32[2,32,64,256]{3,2,1,0:T(8,128)S(1)} %bitcast.4, ...), custom_call_target="tpu_custom_call" | custom-call | flops 83886080 | bytes 4194304 | tf_op jit(solution)/shard_map/pack_coefficients/pallas_call | solution.py:213
  5.9 0.1 collective-permute-start.1
  6.0 1.6 %collective-permute-start.3 = (bf16[32,2048]{1,0:T(8,128)(2,1)S(1)}, bf16[32,2048]{1,0:T(8,128)(2,1)S(1)}, u32[]{:S(2)}, u32[]{:S(2)}) collective-permute-start(bf16[32,2048]{1,0:T(8,128)(2,1)S(1)} %get-tuple-element.49), channel_id=1, source_target_pairs={{0,24},{8,16},{16,8},{24,0},{1,25},{9,17},{17,9},{25,1},{2,26},{10... | collective-permute-start | bytes 393224 | tf_op jit(solution)/shard_map/ppermute | solution.py:602
  7.6 0.5 %collective-permute-start.2 = (bf16[16,2048]{1,0:T(8,128)(2,1)S(1)}, bf16[16,2048]{1,0:T(8,128)(2,1)S(1)}, u32[]{:S(2)}, u32[]{:S(2)}) collective-permute-start(bf16[16,2048]{1,0:T(8,128)(2,1)S(1)} %get-tuple-element.48), channel_id=1, source_target_pairs={{0,16},{8,24},{16,0},{24,8},{1,17},{9,25},{17,1},{25,9},{2,18},{10... | collective-permute-start | bytes 196616 | tf_op jit(solution)/shard_map/ppermute | solution.py:602
  8.1 0.0 collective-permute-done.1.refs_1_
  8.1 0.0 collective-permute-done.refs_0_
  8.1 0.1 pack_edges.1
  8.3 1.7 %collective-permute-start.5 = (bf16[16,128]{1,0:T(8,128)(2,1)S(1)}, bf16[16,128]{1,0:T(8,128)(2,1)S(1)}, u32[]{:S(2)}, u32[]{:S(2)}) collective-permute-start(bf16[16,128]{1,0:T(8,128)(2,1)S(1)} %get-tuple-element.51), channel_id=1, source_target_pairs={{0,16},{8,24},{16,0},{24,8},{1,17},{9,25},{17,1},{25,9},{2,18},{10... | collective-permute-start | bytes 12296 | tf_op jit(solution)/shard_map/ppermute | solution.py:604
  10.0 0.0 collective-permute-start.4
  10.0 0.5 %collective-permute-start.6 = (bf16[32,128]{1,0:T(8,128)(2,1)S(1)}, bf16[32,128]{1,0:T(8,128)(2,1)S(1)}, u32[]{:S(2)}, u32[]{:S(2)}) collective-permute-start(bf16[32,128]{1,0:T(8,128)(2,1)S(1)} %get-tuple-element.52), channel_id=1, source_target_pairs={{0,24},{8,16},{16,8},{24,0},{1,25},{9,17},{17,9},{25,1},{2,26},{10... | collective-permute-start | bytes 24584 | tf_op jit(solution)/shard_map/ppermute | solution.py:604
  10.5 1.7 %local_rate.1 = (f32[2,72,96,128]{3,2,1,0:T(8,128)S(1)}, f32[2,72,96,128]{3,2,1,0:T(8,128)S(1)}, f32[2,72,96,128]{3,2,1,0:T(8,128)S(1)}, f32[2,72,96,128]{3,2,1,...) custom-call(f32[2,32,64,256]{3,2,1,0:T(8,128)S(1)} %bitcast.5, ...), custom_call_target="tpu_custom_call" | custom-call | flops 536870912 | bytes 8388608 | tf_op jit(solution)/shard_map/local_rate/pallas_call | solution.py:293
  12.1 1.2 %collective-permute-done.2.refs_1_ = bf16[16,2048]{1,0:T(8,128)(2,1)S(1)} collective-permute-done((bf16[16,2048]{1,0:T(8,128)(2,1)S(1)}, bf16[16,2048]{1,0:T(8,128)(2,1)S(1)}, u32[]{:S(2)}, u32[]{:S(2)}) %collective-permute-start.2) | collective-permute-done | bytes 65568 | tf_op jit(solution)/shard_map/ppermute | solution.py:602
  13.4 0.0 collective-permute-done.3.refs_2_
  13.4 0.0 collective-permute-done.5.refs_4_
  13.4 0.0 collective-permute-done.4.refs_3_
  13.4 0.0 collective-permute-done.6.refs_5_
  13.4 0.3 %outer_rows.1 = (bf16[272,256]{1,0:T(8,128)(2,1)S(1)}, bf16[272,256]{1,0:T(8,128)(2,1)S(1)}) custom-call(f32[2,256,256]{2,1,0:T(8,128)S(1)} %get-tuple-element.61.ends_ref, f32[1,256,256]{2,1,0:T(8,128)S(1)} %get-tuple-element.43.beside_ref, bf16[2,48,256]{2,1,0:T(8,128)(2,1)S(1)} %get-tuple-element.44.take_ref, ...), custom_call_target="tpu_custom_call" | custom-call | flops 12582912 | bytes 1048576 | tf_op jit(solution)/shard_map/outer_rows/pallas_call | solution.py:341
  13.7 1.6 %collective-permute-start.7 = (bf16[272,256]{1,0:T(8,128)(2,1)S(1)}, bf16[272,256]{1,0:T(8,128)(2,1)S(1)}, u32[]{:S(2)}, u32[]{:S(2)}) collective-permute-start(bf16[272,256]{1,0:T(8,128)(2,1)S(1)} %get-tuple-element.62), channel_id=1, source_target_pairs={{0,2},{2,4},{4,6},{6,0},{1,3},{3,5},{5,7},{7,1},{8,10},{10,12},{12... | collective-permute-start | bytes 417800 | tf_op jit(solution)/shard_map/ppermute | solution.py:608
  15.3 2.3 %collective-permute-start.8 = (bf16[272,256]{1,0:T(8,128)(2,1)S(1)}, bf16[272,256]{1,0:T(8,128)(2,1)S(1)}, u32[]{:S(2)}, u32[]{:S(2)}) collective-permute-start(bf16[272,256]{1,0:T(8,128)(2,1)S(1)} %get-tuple-element.63), channel_id=1, source_target_pairs={{2,0},{4,2},{6,4},{0,6},{3,1},{5,3},{7,5},{1,7},{10,8},{12,10},{14... | collective-permute-start | bytes 417800 | tf_op jit(solution)/shard_map/ppermute | solution.py:608
  17.6 0.0 copy-start.1
  17.6 1.1 %section.1.z0.z0_in = f32[2,72,96,128]{3,2,1,0:T(8,128)S(1)} custom-call(f32[2,72,96,128]{3,2,1,0:T(8,128)S(1)} %get-tuple-element.42.z_in, f32[1,256,256]{2,1,0:T(8,128)S(1)} %get-tuple-element.43.beside_ref, bf16[2,48,256]{2,1,0:T(8,128)(2,1)S(1)} %get-tuple-element.44.take_ref, ...), custom_call_target="tpu_custom_call", output_to_operand_aliasing={{}: (0, {})} | custom-call | flops 100663296 | bytes 8388608 | tf_op jit(solution)/shard_map/section/pallas_call | solution.py:385
  18.7 0.0 copy-done.1
  18.7 7.0 %inner_substeps.1 = (f32[64,64,256]{2,1,0:T(8,128)}, f32[16,64,256]{2,1,0:T(8,128)S(1)}, f32[2,72,96,128]{3,2,1,0:T(8,128)S(1)}, f32[2,72,96,128]{3,2,1,0:T(8,128)S(1)}, f32[2,72,96,128]{3,2,1,0:T(8,128)S(1)}) custom-call(f32[2,72,96,128]{3,2,1,0:T(8,128)S(1)} %section.1.z0.z0_in, ...), custom_call_target="tpu_custom_call", output_to_operand_aliasing={{2}: (1, {}), {3}: (2, {}), {4}: (3, {})} | custom-call | flops 41943040 | bytes 8388608 | tf_op jit(solution)/shard_map/inner_substeps/pallas_call | solution.py:497
  25.7 0.0 collective-permute-done.7.up_ref
  25.7 0.0 collective-permute-done.8.down_ref
  25.8 1.7 %outer_substeps.1 = (f32[64,64,256]{2,1,0:T(8,128)}, f32[2,72,96,128]{3,2,1,0:T(8,128)S(1)}, f32[2,72,96,128]{3,2,1,0:T(8,128)S(1)}, f32[2,72,96,128]{3,2,1,0:T(8,128)S(1)}, f32[2,72,96,128]{3,2,1,0:T(8,128)S(1)}) custom-call(f32[64,64,256]{2,1,0:T(8,128)} %get-tuple-element.56.o_in, ...), custom_call_target="tpu_custom_call", output_to_operand_aliasing={{0}: (0, {}), {1}: (1, {}), {2}: (2, {}), {3}: (3, {}), {4}... | custom-call | flops 10485760 | bytes 1048576 | tf_op jit(solution)/shard_map/outer_substeps/pallas_call | solution.py:566
Async XLA Ops:
  0.0 4.3 %copy-start = (f32[64,64,256]{2,1,0:T(8,128)S(1)}, f32[64,64,256]{2,1,0:T(8,128)}, u32[]{:S(2)}) copy-start(f32[64,64,256]{2,1,0:T(8,128)} %u_hbm.1) | copy-start | bytes 12582916
  1.3 6.8 %collective-permute-start = (bf16[272,256]{1,0:T(8,128)(2,1)S(1)}, bf16[272,256]{1,0:T(8,128)(2,1)S(1)}, u32[]{:S(2)}, u32[]{:S(2)}) collective-permute-start(bf16[272,256]{1,0:T(8,128)(2,1)S(1)} %age_edges.1.refs_8_), channel_id=1, source_target_pairs={{0,1},{1,0},{2,3},{3,2},{4,5},{5,4},{6,7},{7,6},{8,9},{9,8},{10,11... | collective-permute-start | bytes 417800 | tf_op jit(solution)/shard_map/ppermute | solution.py:599
  5.9 2.2 %collective-permute-start.1 = (bf16[32,2048]{1,0:T(8,128)(2,1)S(1)}, bf16[32,2048]{1,0:T(8,128)(2,1)S(1)}, u32[]{:S(2)}, u32[]{:S(2)}) collective-permute-start(bf16[32,2048]{1,0:T(8,128)(2,1)S(1)} %get-tuple-element.46), channel_id=1, source_target_pairs={{0,8},{8,0},{16,24},{24,16},{1,9},{9,1},{17,25},{25,17},{2,10},{10... | collective-permute-start | bytes 393224 | tf_op jit(solution)/shard_map/ppermute | solution.py:602
  6.0 7.4 %collective-permute-start.3 = (bf16[32,2048]{1,0:T(8,128)(2,1)S(1)}, bf16[32,2048]{1,0:T(8,128)(2,1)S(1)}, u32[]{:S(2)}, u32[]{:S(2)}) collective-permute-start(bf16[32,2048]{1,0:T(8,128)(2,1)S(1)} %get-tuple-element.49), channel_id=1, source_target_pairs={{0,24},{8,16},{16,8},{24,0},{1,25},{9,17},{17,9},{25,1},{2,26},{10... | collective-permute-start | bytes 393224 | tf_op jit(solution)/shard_map/ppermute | solution.py:602
  7.6 5.8 %collective-permute-start.2 = (bf16[16,2048]{1,0:T(8,128)(2,1)S(1)}, bf16[16,2048]{1,0:T(8,128)(2,1)S(1)}, u32[]{:S(2)}, u32[]{:S(2)}) collective-permute-start(bf16[16,2048]{1,0:T(8,128)(2,1)S(1)} %get-tuple-element.48), channel_id=1, source_target_pairs={{0,16},{8,24},{16,0},{24,8},{1,17},{9,25},{17,1},{25,9},{2,18},{10... | collective-permute-start | bytes 196616 | tf_op jit(solution)/shard_map/ppermute | solution.py:602
  8.3 5.2 %collective-permute-start.5 = (bf16[16,128]{1,0:T(8,128)(2,1)S(1)}, bf16[16,128]{1,0:T(8,128)(2,1)S(1)}, u32[]{:S(2)}, u32[]{:S(2)}) collective-permute-start(bf16[16,128]{1,0:T(8,128)(2,1)S(1)} %get-tuple-element.51), channel_id=1, source_target_pairs={{0,16},{8,24},{16,0},{24,8},{1,17},{9,25},{17,1},{25,9},{2,18},{10... | collective-permute-start | bytes 12296 | tf_op jit(solution)/shard_map/ppermute | solution.py:604
  10.0 3.5 %collective-permute-start.4 = (bf16[32,128]{1,0:T(8,128)(2,1)S(1)}, bf16[32,128]{1,0:T(8,128)(2,1)S(1)}, u32[]{:S(2)}, u32[]{:S(2)}) collective-permute-start(bf16[32,128]{1,0:T(8,128)(2,1)S(1)} %get-tuple-element.50), channel_id=1, source_target_pairs={{0,8},{8,0},{16,24},{24,16},{1,9},{9,1},{17,25},{25,17},{2,10},{10... | collective-permute-start | bytes 24584 | tf_op jit(solution)/shard_map/ppermute | solution.py:604
  10.0 3.5 %collective-permute-start.6 = (bf16[32,128]{1,0:T(8,128)(2,1)S(1)}, bf16[32,128]{1,0:T(8,128)(2,1)S(1)}, u32[]{:S(2)}, u32[]{:S(2)}) collective-permute-start(bf16[32,128]{1,0:T(8,128)(2,1)S(1)} %get-tuple-element.52), channel_id=1, source_target_pairs={{0,24},{8,16},{16,8},{24,0},{1,25},{9,17},{17,9},{25,1},{2,26},{10... | collective-permute-start | bytes 24584 | tf_op jit(solution)/shard_map/ppermute | solution.py:604
  13.7 12.0 %collective-permute-start.7 = (bf16[272,256]{1,0:T(8,128)(2,1)S(1)}, bf16[272,256]{1,0:T(8,128)(2,1)S(1)}, u32[]{:S(2)}, u32[]{:S(2)}) collective-permute-start(bf16[272,256]{1,0:T(8,128)(2,1)S(1)} %get-tuple-element.62), channel_id=1, source_target_pairs={{0,2},{2,4},{4,6},{6,0},{1,3},{3,5},{5,7},{7,1},{8,10},{10,12},{12... | collective-permute-start | bytes 417800 | tf_op jit(solution)/shard_map/ppermute | solution.py:608
  15.3 10.4 %collective-permute-start.8 = (bf16[272,256]{1,0:T(8,128)(2,1)S(1)}, bf16[272,256]{1,0:T(8,128)(2,1)S(1)}, u32[]{:S(2)}, u32[]{:S(2)}) collective-permute-start(bf16[272,256]{1,0:T(8,128)(2,1)S(1)} %get-tuple-element.63), channel_id=1, source_target_pairs={{2,0},{4,2},{6,4},{0,6},{3,1},{5,3},{7,5},{1,7},{10,8},{12,10},{14... | collective-permute-start | bytes 417800 | tf_op jit(solution)/shard_map/ppermute | solution.py:608
  17.6 1.1 %copy-start.1 = (f32[256]{0:T(256)S(1)}, f32[256]{0:T(256)}, u32[]{:S(2)}) copy-start(f32[256]{0:T(256)} %param.13) | copy-start | bytes 3076

commit v5 on v4

--- a/solution.py
+++ b/solution.py
@@ -320,19 +320,29 @@
     )
 
 
+def odd_age():
+    return lax.rem(lax.axis_index("age"), 2) == 1
+
+
 def rows_kernel(ranks, sides, wears, ages, ends_ref, beside_ref, take_ref, *refs):
     q_refs, edge_refs, out_refs = refs[: len(ranks)], refs[len(ranks) : -2], refs[-2:]
     each, corner = wears // 2 * HALO, HALO * HALO
-    for half, (start, out_ref) in enumerate(zip((0, wears - HALO), out_refs)):
+    odd = odd_age()
+    first_rows, last_rows = [], []
+    for half, (start, rows) in enumerate(((0, first_rows), (wears - HALO, last_rows))):
         v = (start - half * wears // 2) * ages
         rate = distant(ranks, q_refs, take_ref, half, [slice(v, v + HALO * ages)] * len(ranks))
-        out_ref[: HALO * ages] = (rate + ends_ref[half]).astype(bf16)
+        rows.append(rate + ends_ref[half])
         first = 0 if half == 0 else each - corner
         for s in range(sides):
             rate = distant(ranks, edge_refs, take_ref, half, [slice(s * each, (s + 1) * each)] * len(ranks))
-            place = slice(start * HALO, start * HALO + corner)
-            row = HALO * ages + s * corner
-            out_ref[row : row + corner] = (rate[first : first + corner] + beside_ref[s, place]).astype(bf16)
+            rows.append(rate[first : first + corner] + beside_ref[s, start * HALO : start * HALO + corner])
+    row = 0
+    for top, bottom in zip(first_rows, last_rows):
+        place = slice(row, row + top.shape[0])
+        out_refs[0][place] = jnp.where(odd, top, bottom).astype(bf16)
+        out_refs[1][place] = jnp.where(odd, bottom, top).astype(bf16)
+        row += top.shape[0]
 
 
 def outer_rows(ends, beside, take, q, q_edges, ranks, sides, wears, ages):
@@ -510,12 +520,13 @@
     )(*[in_vmem(x) for x in fields], speed)
 
 
-def outer_kernel(sides, o_in, z0_in, z1_in, z2_in, z3_in, rest, speed_ref, up_ref, down_ref, o_ref, z0, z1, z2, z3,
+def outer_kernel(sides, o_in, z0_in, z1_in, z2_in, z3_in, rest, speed_ref, first_ref, second_ref, o_ref, z0, z1, z2, z3,
                  stage, out_sem):
     del o_in, z0_in, z1_in, z2_in, z3_in
     halves, rows, _, _ = z0.shape
     wears, ages = rows - 2 * HALO, stage.shape[2]
     fields = (z0, z1, z2, z3)
+    odd = odd_age()
     count = rest.shape[0]
     stores = [pltpu.make_async_copy(rest, o_ref.at[pl.ds(wears - SUBSTEPS - count, count)], out_sem.at[2])]
     stores[0].start()
@@ -523,8 +534,9 @@
     near = [jnp.where(at_end("wear", i == 1), 0.0, 1.0).astype(f32) for i in range(2)]
     for l in range(halves):
         lanes = pl.ds(l * 128, 128)
-        for e, (ref, at) in enumerate(((up_ref, 0), (down_ref, HALO + wears))):
-            values = ref[:, lanes].astype(f32) * near[e]
+        first, second = first_ref[:, lanes].astype(f32), second_ref[:, lanes].astype(f32)
+        for e, at in enumerate((0, HALO + wears)):
+            values = jnp.where(odd, *((second, first) if e == 0 else (first, second))) * near[e]
             z0[l, at : at + HALO, ROW0 : ROW0 + ages, :] = values[: HALO * ages].reshape(HALO, ages, 128)
             for s in range(sides):
                 corner = values[HALO * (ages + s * HALO) : HALO * (ages + (s + 1) * HALO)]
@@ -561,7 +573,7 @@
         copy.wait()
 
 
-def outer_substeps(o, fields, rest, speed, up, down, sides):
+def outer_substeps(o, fields, rest, speed, first, second, sides):
     wears, ages, size = o.shape
     return pl.pallas_call(
         functools.partial(outer_kernel, sides),
@@ -573,7 +585,7 @@
         compiler_params=params(16),
         cost_estimate=cost(20 * SUBSTEPS * 2 * HALO * ages * size, 2**20),
         name="outer_substeps",
-    )(o, *[in_vmem(x) for x in (*fields, rest)], speed, in_vmem(up), in_vmem(down))[0]
+    )(o, *[in_vmem(x) for x in (*fields, rest)], speed, in_vmem(first), in_vmem(second))[0]
 
 
 def body(adjoint_value, load_diffusion, load_drift, wear_speed, hazard):
@@ -603,13 +615,21 @@
     arrived[0], *q_edges = pack_edges(send, near, arrived[0], ranks, sides, extra)
     arrived_edges = [lax.ppermute(x, "cheb", pairs) for x, pairs in zip(q_edges, moves)]
     z, *later, beside, ends, take = local(u4, tables, near, sides)
-    top, bottom = outer_rows(ends, beside, take, arrived, arrived_edges, ranks, sides, wears, ages)
-    after, before = ring(n_wear)
-    up, down = lax.ppermute(bottom, "wear", after), lax.ppermute(top, "wear", before)
+    messages = outer_rows(ends, beside, take, arrived, arrived_edges, ranks, sides, wears, ages)
+    around = []
+    for w in range(n_wear):
+        for a in range(n_age):
+            to = w + 1 if a % 2 == 0 else w - 1
+            if 0 <= to < n_wear:
+                around.append((w * n_age + a, to * n_age + a))
+            elif n_age % 2 == 0:
+                around.append((w * n_age + a, w * n_age + (a ^ 1)))
+    turns = (around, [(j, i) for i, j in around])
+    first, second = (lax.ppermute(x, ("wear", "age"), turn) for x, turn in zip(messages, turns))
     z = section(z, beside, take, arrived, arrived_edges, ranks, sides, wears, ages)
     speed = wear_speed.reshape(1, size)
     o, rest, *later = inner_substeps([z, *later], speed, sides, wears, ages)
-    return outer_substeps(o, [z, *later], rest, speed, up, down, sides)
+    return outer_substeps(o, [z, *later], rest, speed, first, second, sides)
 
 
 def solution(mesh):

time: 27.6 us -> 25.8 us (0.935)
  starting transfers between devices: 11.3 us -> 9.49 us
    ppermute x2, starting transfers between devices: 3.88 us -> 2.08 us  [body(): lax.ppermute(x, ('wear', 'age'), turn)]
  transfers between devices with their start and end apart: 9 -> 9, of which waited for: 1 -> 1; matrix products, arithmetic and copies ran while one was open for 0% -> 0% of each run, Pallas kernels for 42% -> 45%
where the time goes in v5:
time: 25.8 us; the launch traced here: 25.7 us
  Pallas kernels  14.8 us (57%)
  starting transfers between devices  9.49 us (37%)
  waiting for transfers between devices  1.28 us (5%)
    pallas_call x1, Pallas kernels, inner_substeps(): pl.pallas_call(functools.partial(inner_kernel, sides), out_shape=[jax.Sha...  7.03 us
    ppermute x1, starting transfers between devices, body(): lax.ppermute(x, 'age', pairs)  3 us
    ppermute x3, starting transfers between devices, body(): arrived = [lax.ppermute(x, 'cheb', pairs) for x, pairs in zip(q, moves)]  2.21 us
    ppermute x3, starting transfers between devices, body(): lax.ppermute(x, 'cheb', pairs)  2.2 us
    ppermute x2, starting transfers between devices, body(): lax.ppermute(x, ('wear', 'age'), turn)  2.08 us
    pallas_call x1, Pallas kernels, outer_substeps(): pl.pallas_call(functools.partial(outer_kernel, sides), out_shape=[jax.Sha...  1.7 us
    pallas_call x1, Pallas kernels, local(): pl.pallas_call(functools.partial(local_kernel, sides), in_specs=[VMEM] *...  1.69 us
    pallas_call x1, Pallas kernels, pack(): pl.pallas_call(functools.partial(pack_kernel, ranks), in_specs=[VMEM] + [...  1.55 us
  transfers between devices with their start and end apart: 9, of which 1 were waited for; matrix products, arithmetic and copies ran while one was open for 0% of the time, Pallas kernels for 45%

profile of v5, /device:TPU:0, one launch (start us, length us, event | category | flops | bytes accessed | tf_op | source)
XLA Modules:
  0.0 25.7 jit_solution(14834667837727782353)
XLA Ops:
  0.0 0.0 copy-start
  0.0 1.3 %age_edges.1.refs_8_ = bf16[272,256]{1,0:T(8,128)(2,1)S(1)} custom-call(f32[64,64,256]{2,1,0:T(8,128)} %u_hbm.1, f32[64,64]{1,0:T(8,128)} %refs_0_.1), custom_call_target="tpu_custom_call" | custom-call | bytes 1048576 | tf_op jit(solution)/shard_map/age_edges/pallas_call | solution.py:151
  1.3 3.0 %collective-permute-start = (bf16[272,256]{1,0:T(8,128)(2,1)S(1)}, bf16[272,256]{1,0:T(8,128)(2,1)S(1)}, u32[]{:S(2)}, u32[]{:S(2)}) collective-permute-start(bf16[272,256]{1,0:T(8,128)(2,1)S(1)} %age_edges.1.refs_8_), channel_id=1, source_target_pairs={{0,1},{1,0},{2,3},{3,2},{4,5},{5,4},{6,7},{7,6},{8,9},{9,8},{10,11... | collective-permute-start | bytes 417800 | tf_op jit(solution)/shard_map/ppermute | solution.py:611
  4.3 0.0 copy-done
  4.3 1.5 %pack_coefficients.1 = (bf16[32,2048]{1,0:T(8,128)(2,1)S(1)}, bf16[16,2048]{1,0:T(8,128)(2,1)S(1)}, bf16[32,2048]{1,0:T(8,128)(2,1)S(1)}, bf16[40,256]{1,0:T(8,1...) custom-call(f32[2,32,64,256]{3,2,1,0:T(8,128)S(1)} %bitcast.4, ...), custom_call_target="tpu_custom_call" | custom-call | flops 83886080 | bytes 4194304 | tf_op jit(solution)/shard_map/pack_coefficients/pallas_call | solution.py:213
  5.9 0.1 collective-permute-start.1
  6.0 1.6 %collective-permute-start.3 = (bf16[32,2048]{1,0:T(8,128)(2,1)S(1)}, bf16[32,2048]{1,0:T(8,128)(2,1)S(1)}, u32[]{:S(2)}, u32[]{:S(2)}) collective-permute-start(bf16[32,2048]{1,0:T(8,128)(2,1)S(1)} %get-tuple-element.49), channel_id=1, source_target_pairs={{0,24},{8,16},{16,8},{24,0},{1,25},{9,17},{17,9},{25,1},{2,26},{10... | collective-permute-start | bytes 393224 | tf_op jit(solution)/shard_map/ppermute | solution.py:614
  7.6 0.5 %collective-permute-start.2 = (bf16[16,2048]{1,0:T(8,128)(2,1)S(1)}, bf16[16,2048]{1,0:T(8,128)(2,1)S(1)}, u32[]{:S(2)}, u32[]{:S(2)}) collective-permute-start(bf16[16,2048]{1,0:T(8,128)(2,1)S(1)} %get-tuple-element.48), channel_id=1, source_target_pairs={{0,16},{8,24},{16,0},{24,8},{1,17},{9,25},{17,1},{25,9},{2,18},{10... | collective-permute-start | bytes 196616 | tf_op jit(solution)/shard_map/ppermute | solution.py:614
  8.1 0.0 collective-permute-done.1.refs_1_
  8.1 0.0 collective-permute-done.refs_0_
  8.1 0.1 pack_edges.1
  8.3 1.7 %collective-permute-start.5 = (bf16[16,128]{1,0:T(8,128)(2,1)S(1)}, bf16[16,128]{1,0:T(8,128)(2,1)S(1)}, u32[]{:S(2)}, u32[]{:S(2)}) collective-permute-start(bf16[16,128]{1,0:T(8,128)(2,1)S(1)} %get-tuple-element.51), channel_id=1, source_target_pairs={{0,16},{8,24},{16,0},{24,8},{1,17},{9,25},{17,1},{25,9},{2,18},{10... | collective-permute-start | bytes 12296 | tf_op jit(solution)/shard_map/ppermute | solution.py:616
  10.0 0.0 collective-permute-start.4
  10.0 0.5 %collective-permute-start.6 = (bf16[32,128]{1,0:T(8,128)(2,1)S(1)}, bf16[32,128]{1,0:T(8,128)(2,1)S(1)}, u32[]{:S(2)}, u32[]{:S(2)}) collective-permute-start(bf16[32,128]{1,0:T(8,128)(2,1)S(1)} %get-tuple-element.52), channel_id=1, source_target_pairs={{0,24},{8,16},{16,8},{24,0},{1,25},{9,17},{17,9},{25,1},{2,26},{10... | collective-permute-start | bytes 24584 | tf_op jit(solution)/shard_map/ppermute | solution.py:616
  10.5 1.7 %local_rate.1 = (f32[2,72,96,128]{3,2,1,0:T(8,128)S(1)}, f32[2,72,96,128]{3,2,1,0:T(8,128)S(1)}, f32[2,72,96,128]{3,2,1,0:T(8,128)S(1)}, f32[2,72,96,128]{3,2,1,...) custom-call(f32[2,32,64,256]{3,2,1,0:T(8,128)S(1)} %bitcast.5, ...), custom_call_target="tpu_custom_call" | custom-call | flops 536870912 | bytes 8388608 | tf_op jit(solution)/shard_map/local_rate/pallas_call | solution.py:293
  12.1 1.2 %collective-permute-done.2.refs_1_ = bf16[16,2048]{1,0:T(8,128)(2,1)S(1)} collective-permute-done((bf16[16,2048]{1,0:T(8,128)(2,1)S(1)}, bf16[16,2048]{1,0:T(8,128)(2,1)S(1)}, u32[]{:S(2)}, u32[]{:S(2)}) %collective-permute-start.2) | collective-permute-done | bytes 65568 | tf_op jit(solution)/shard_map/ppermute | solution.py:614
  13.4 0.0 collective-permute-done.3.refs_2_
  13.4 0.0 collective-permute-done.5.refs_4_
  13.4 0.0 collective-permute-done.4.refs_3_
  13.4 0.0 collective-permute-done.6.refs_5_
  13.4 0.3 %outer_rows.1 = (bf16[272,256]{1,0:T(8,128)(2,1)S(1)}, bf16[272,256]{1,0:T(8,128)(2,1)S(1)}) custom-call(f32[2,256,256]{2,1,0:T(8,128)S(1)} %get-tuple-element.61.ends_ref, f32[1,256,256]{2,1,0:T(8,128)S(1)} %get-tuple-element.43.beside_ref, bf16[2,48,256]{2,1,0:T(8,128)(2,1)S(1)} %get-tuple-element.44.take_ref, ...), custom_call_target="tpu_custom_call" | custom-call | flops 12582912 | bytes 1048576 | tf_op jit(solution)/shard_map/outer_rows/pallas_call | solution.py:351
  13.7 1.6 %collective-permute-start.7 = (bf16[272,256]{1,0:T(8,128)(2,1)S(1)}, bf16[272,256]{1,0:T(8,128)(2,1)S(1)}, u32[]{:S(2)}, u32[]{:S(2)}) collective-permute-start(bf16[272,256]{1,0:T(8,128)(2,1)S(1)} %get-tuple-element.62), channel_id=1, source_target_pairs={{0,2},{1,0},{2,4},{3,1},{4,6},{5,3},{6,7},{7,5},{8,10},{9,8},{10,1... | collective-permute-start | bytes 417800 | tf_op jit(solution)/shard_map/ppermute | solution.py:628
  15.3 0.5 %collective-permute-start.8 = (bf16[272,256]{1,0:T(8,128)(2,1)S(1)}, bf16[272,256]{1,0:T(8,128)(2,1)S(1)}, u32[]{:S(2)}, u32[]{:S(2)}) collective-permute-start(bf16[272,256]{1,0:T(8,128)(2,1)S(1)} %get-tuple-element.63), channel_id=1, source_target_pairs={{2,0},{0,1},{4,2},{1,3},{6,4},{3,5},{7,6},{5,7},{10,8},{8,9},{12,1... | collective-permute-start | bytes 417800 | tf_op jit(solution)/shard_map/ppermute | solution.py:628
  15.8 0.0 copy-start.1
  15.8 1.1 %section.1.z0.z0_in = f32[2,72,96,128]{3,2,1,0:T(8,128)S(1)} custom-call(f32[2,72,96,128]{3,2,1,0:T(8,128)S(1)} %get-tuple-element.42.z_in, f32[1,256,256]{2,1,0:T(8,128)S(1)} %get-tuple-element.43.beside_ref, bf16[2,48,256]{2,1,0:T(8,128)(2,1)S(1)} %get-tuple-element.44.take_ref, ...), custom_call_target="tpu_custom_call", output_to_operand_aliasing={{}: (0, {})} | custom-call | flops 100663296 | bytes 8388608 | tf_op jit(solution)/shard_map/section/pallas_call | solution.py:395
  16.9 0.0 copy-done.1
  16.9 7.0 %inner_substeps.1 = (f32[64,64,256]{2,1,0:T(8,128)}, f32[16,64,256]{2,1,0:T(8,128)S(1)}, f32[2,72,96,128]{3,2,1,0:T(8,128)S(1)}, f32[2,72,96,128]{3,2,1,0:T(8,128)S(1)}, f32[2,72,96,128]{3,2,1,0:T(8,128)S(1)}) custom-call(f32[2,72,96,128]{3,2,1,0:T(8,128)S(1)} %section.1.z0.z0_in, ...), custom_call_target="tpu_custom_call", output_to_operand_aliasing={{2}: (1, {}), {3}: (2, {}), {4}: (3, {})} | custom-call | flops 41943040 | bytes 8388608 | tf_op jit(solution)/shard_map/inner_substeps/pallas_call | solution.py:507
  23.9 0.0 collective-permute-done.7.first_ref
  24.0 0.0 collective-permute-done.8.second_ref
  24.0 1.7 %outer_substeps.1 = (f32[64,64,256]{2,1,0:T(8,128)}, f32[2,72,96,128]{3,2,1,0:T(8,128)S(1)}, f32[2,72,96,128]{3,2,1,0:T(8,128)S(1)}, f32[2,72,96,128]{3,2,1,0:T(8,128)S(1)}, f32[2,72,96,128]{3,2,1,0:T(8,128)S(1)}) custom-call(f32[64,64,256]{2,1,0:T(8,128)} %get-tuple-element.56.o_in, ...), custom_call_target="tpu_custom_call", output_to_operand_aliasing={{0}: (0, {}), {1}: (1, {}), {2}: (2, {}), {3}: (3, {}), {4}... | custom-call | flops 10485760 | bytes 1048576 | tf_op jit(solution)/shard_map/outer_substeps/pallas_call | solution.py:578
Async XLA Ops:
  0.0 4.3 %copy-start = (f32[64,64,256]{2,1,0:T(8,128)S(1)}, f32[64,64,256]{2,1,0:T(8,128)}, u32[]{:S(2)}) copy-start(f32[64,64,256]{2,1,0:T(8,128)} %u_hbm.1) | copy-start | bytes 12582916
  1.3 6.8 %collective-permute-start = (bf16[272,256]{1,0:T(8,128)(2,1)S(1)}, bf16[272,256]{1,0:T(8,128)(2,1)S(1)}, u32[]{:S(2)}, u32[]{:S(2)}) collective-permute-start(bf16[272,256]{1,0:T(8,128)(2,1)S(1)} %age_edges.1.refs_8_), channel_id=1, source_target_pairs={{0,1},{1,0},{2,3},{3,2},{4,5},{5,4},{6,7},{7,6},{8,9},{9,8},{10,11... | collective-permute-start | bytes 417800 | tf_op jit(solution)/shard_map/ppermute | solution.py:611
  5.9 2.2 %collective-permute-start.1 = (bf16[32,2048]{1,0:T(8,128)(2,1)S(1)}, bf16[32,2048]{1,0:T(8,128)(2,1)S(1)}, u32[]{:S(2)}, u32[]{:S(2)}) collective-permute-start(bf16[32,2048]{1,0:T(8,128)(2,1)S(1)} %get-tuple-element.46), channel_id=1, source_target_pairs={{0,8},{8,0},{16,24},{24,16},{1,9},{9,1},{17,25},{25,17},{2,10},{10... | collective-permute-start | bytes 393224 | tf_op jit(solution)/shard_map/ppermute | solution.py:614
  6.0 7.4 %collective-permute-start.3 = (bf16[32,2048]{1,0:T(8,128)(2,1)S(1)}, bf16[32,2048]{1,0:T(8,128)(2,1)S(1)}, u32[]{:S(2)}, u32[]{:S(2)}) collective-permute-start(bf16[32,2048]{1,0:T(8,128)(2,1)S(1)} %get-tuple-element.49), channel_id=1, source_target_pairs={{0,24},{8,16},{16,8},{24,0},{1,25},{9,17},{17,9},{25,1},{2,26},{10... | collective-permute-start | bytes 393224 | tf_op jit(solution)/shard_map/ppermute | solution.py:614
  7.6 5.8 %collective-permute-start.2 = (bf16[16,2048]{1,0:T(8,128)(2,1)S(1)}, bf16[16,2048]{1,0:T(8,128)(2,1)S(1)}, u32[]{:S(2)}, u32[]{:S(2)}) collective-permute-start(bf16[16,2048]{1,0:T(8,128)(2,1)S(1)} %get-tuple-element.48), channel_id=1, source_target_pairs={{0,16},{8,24},{16,0},{24,8},{1,17},{9,25},{17,1},{25,9},{2,18},{10... | collective-permute-start | bytes 196616 | tf_op jit(solution)/shard_map/ppermute | solution.py:614
  8.3 5.2 %collective-permute-start.5 = (bf16[16,128]{1,0:T(8,128)(2,1)S(1)}, bf16[16,128]{1,0:T(8,128)(2,1)S(1)}, u32[]{:S(2)}, u32[]{:S(2)}) collective-permute-start(bf16[16,128]{1,0:T(8,128)(2,1)S(1)} %get-tuple-element.51), channel_id=1, source_target_pairs={{0,16},{8,24},{16,0},{24,8},{1,17},{9,25},{17,1},{25,9},{2,18},{10... | collective-permute-start | bytes 12296 | tf_op jit(solution)/shard_map/ppermute | solution.py:616
  10.0 3.5 %collective-permute-start.4 = (bf16[32,128]{1,0:T(8,128)(2,1)S(1)}, bf16[32,128]{1,0:T(8,128)(2,1)S(1)}, u32[]{:S(2)}, u32[]{:S(2)}) collective-permute-start(bf16[32,128]{1,0:T(8,128)(2,1)S(1)} %get-tuple-element.50), channel_id=1, source_target_pairs={{0,8},{8,0},{16,24},{24,16},{1,9},{9,1},{17,25},{25,17},{2,10},{10... | collective-permute-start | bytes 24584 | tf_op jit(solution)/shard_map/ppermute | solution.py:616
  10.0 3.5 %collective-permute-start.6 = (bf16[32,128]{1,0:T(8,128)(2,1)S(1)}, bf16[32,128]{1,0:T(8,128)(2,1)S(1)}, u32[]{:S(2)}, u32[]{:S(2)}) collective-permute-start(bf16[32,128]{1,0:T(8,128)(2,1)S(1)} %get-tuple-element.52), channel_id=1, source_target_pairs={{0,24},{8,16},{16,8},{24,0},{1,25},{9,17},{17,9},{25,1},{2,26},{10... | collective-permute-start | bytes 24584 | tf_op jit(solution)/shard_map/ppermute | solution.py:616
  13.7 10.2 %collective-permute-start.7 = (bf16[272,256]{1,0:T(8,128)(2,1)S(1)}, bf16[272,256]{1,0:T(8,128)(2,1)S(1)}, u32[]{:S(2)}, u32[]{:S(2)}) collective-permute-start(bf16[272,256]{1,0:T(8,128)(2,1)S(1)} %get-tuple-element.62), channel_id=1, source_target_pairs={{0,2},{1,0},{2,4},{3,1},{4,6},{5,3},{6,7},{7,5},{8,10},{9,8},{10,1... | collective-permute-start | bytes 417800 | tf_op jit(solution)/shard_map/ppermute | solution.py:628
  15.3 8.6 %collective-permute-start.8 = (bf16[272,256]{1,0:T(8,128)(2,1)S(1)}, bf16[272,256]{1,0:T(8,128)(2,1)S(1)}, u32[]{:S(2)}, u32[]{:S(2)}) collective-permute-start(bf16[272,256]{1,0:T(8,128)(2,1)S(1)} %get-tuple-element.63), channel_id=1, source_target_pairs={{2,0},{0,1},{4,2},{1,3},{6,4},{3,5},{7,6},{5,7},{10,8},{8,9},{12,1... | collective-permute-start | bytes 417800 | tf_op jit(solution)/shard_map/ppermute | solution.py:628
  15.8 1.1 %copy-start.1 = (f32[256]{0:T(256)S(1)}, f32[256]{0:T(256)}, u32[]{:S(2)}) copy-start(f32[256]{0:T(256)} %param.13) | copy-start | bytes 3076

commit v6 on v5

--- a/solution.py
+++ b/solution.py
@@ -107,10 +107,13 @@
     return pl.CostEstimate(flops=flops, bytes_accessed=bytes_accessed, transcendentals=0)
 
 
-def edge_kernel(sides, u_hbm, hazard_hbm, *refs):
-    out_refs, (tiles, hazard, sem) = refs[:sides], refs[sides:]
+def edge_kernel(sides, u_hbm, hazard_hbm, send_hbm, *refs):
+    out_refs, (send, tiles, hazard, sem) = refs[:sides], refs[sides:]
     wears, ages, size = u_hbm.shape
-    copies = [pltpu.make_async_copy(hazard_hbm, hazard, sem.at[sides])]
+    copies = [
+        pltpu.make_async_copy(hazard_hbm, hazard, sem.at[sides]),
+        pltpu.make_async_copy(send_hbm.at[lax.axis_index("cheb")], send, sem.at[sides + 1]),
+    ]
     for i in range(sides):
         if sides == 1:
             start = pl.multiple_of(jnp.where(at_end("age", False), ages - 8, 0), 8)
@@ -119,49 +122,46 @@
         copies.append(pltpu.make_async_copy(u_hbm.at[:, pl.ds(start, 8)], tiles.at[i], sem.at[i]))
     for copy in copies:
         copy.start()
-    for copy in copies:
-        copy.wait()
+    first = at_end("age", False)
+    count = wears * HALO
+    copies[0].wait()
     by_age = jnp.transpose(hazard[...])
     last, early = by_age[ages - HALO :], by_age[:HALO]
+    for i, out_ref in enumerate(out_refs):
+        exact = jnp.where(first, last, early) if sides == 1 else (last, early)[i]
+        high = exact.astype(bf16).astype(f32)
+        rows = jnp.concatenate([high, exact - high, jnp.zeros((HAZARD_ROWS - 2 * HALO, wears), f32)], axis=0)
+        rows = jnp.concatenate([rows, jnp.zeros((HAZARD_ROWS, size - wears), f32)], axis=1)
+        out_ref[count : count + HAZARD_ROWS] = rows.astype(bf16)
+        if out_ref.shape[0] > count + HAZARD_ROWS:
+            out_ref[count + HAZARD_ROWS :] = jnp.zeros((out_ref.shape[0] - count - HAZARD_ROWS, size), bf16)
+    for copy in copies[1:]:
+        copy.wait()
     for i, out_ref in enumerate(out_refs):
         for w in range(0, wears, 4):
             late = [tiles[i, w + j, 8 - HALO :] for j in range(4)]
             soon = [tiles[i, w + j, :HALO] for j in range(4)]
             late, soon = jnp.concatenate(late, axis=0), jnp.concatenate(soon, axis=0)
-            if sides == 1:
-                cells = jnp.where(at_end("age", False), late, soon)
-            else:
-                cells = (late, soon)[i]
+            cells = jnp.where(first, late, soon) if sides == 1 else (late, soon)[i]
             out_ref[w * HALO : (w + 4) * HALO] = cells.astype(bf16)
-        if sides == 1:
-            exact = jnp.where(at_end("age", False), last, early)
-        else:
-            exact = (last, early)[i]
-        high = exact.astype(bf16).astype(f32)
-        rows = jnp.concatenate([high, exact - high, jnp.zeros((HAZARD_ROWS - 2 * HALO, wears), f32)], axis=0)
-        rows = jnp.concatenate([rows, jnp.zeros((HAZARD_ROWS, size - wears), f32)], axis=1)
-        out_ref[wears * HALO : wears * HALO + HAZARD_ROWS] = rows.astype(bf16)
-        used = wears * HALO + HAZARD_ROWS
-        if out_ref.shape[0] > used:
-            out_ref[used:] = jnp.zeros((out_ref.shape[0] - used, size), bf16)
-
-
-def edges(u, hazard, sides, rows):
+
+
+def edges(u, hazard, send, sides, rows):
     wears, ages, size = u.shape
     return pl.pallas_call(
         functools.partial(edge_kernel, sides),
-        in_specs=[ANY, ANY],
-        out_specs=[VMEM] * sides,
-        out_shape=[PIN((rows, size), bf16)] * sides,
+        in_specs=[ANY] * 3,
+        out_specs=[VMEM] * (sides + 1),
+        out_shape=[PIN((rows, size), bf16)] * sides + [PIN(send.shape[1:], bf16)],
         scratch_shapes=[
             pltpu.VMEM((sides, wears, 8, size), f32),
             pltpu.VMEM((wears, ages), f32),
-            pltpu.SemaphoreType.DMA((sides + 1,)),
+            pltpu.SemaphoreType.DMA((sides + 2,)),
         ],
-        compiler_params=params(16),
+        compiler_params=params(8),
         cost_estimate=cost(0, 8 * wears * 8 * size),
         name="age_edges",
-    )(in_hbm(u), in_hbm(hazard))
+    )(*[in_hbm(x) for x in (u, hazard, send)])
 
 
 def pack_rows(ranks, halves):
@@ -179,18 +179,9 @@
     return lax.dot_general(table, cells, (((1,), (1,)), ((), ())), preferred_element_type=f32)
 
 
-def pack_kernel(ranks, u_ref, *refs):
-    shared, refs = refs[:SHARED], refs[SHARED:]
-    tables, refs = refs[:TABLES], refs[-(len(ranks) + SHARED + TABLES + 1) :]
-    q_refs, send = refs[: len(ranks)], refs[len(ranks)]
-    copied, sem = refs[len(ranks) + 1 : -1], refs[-1]
+def pack_kernel(ranks, u_ref, send, *refs):
+    q_refs = refs[-len(ranks) :]
     _, wears, ages, size = u_ref.shape
-    at = lax.axis_index("cheb")
-    sources = [t.at[at] for t in tables[:1]] + list(shared) + [t.at[at] for t in tables[1:]]
-    copies = [pltpu.make_async_copy(a, b, sem.at[i]) for i, (a, b) in enumerate(zip(sources, (send, *copied)))]
-    for copy in copies:
-        copy.start()
-    copies[0].wait()
     chunk = 4
     for g in range(wears // chunk):
         halves = [
@@ -199,28 +190,20 @@
         ]
         for q_ref, rows in zip(q_refs, pack_rows(ranks, halves)):
             q_ref[:, g * chunk * ages : (g + 1) * chunk * ages] = rows
-    for copy in copies[1:]:
-        copy.wait()
-
-
-SHARED, TABLES = 1, 7
-
-
-def pack(u4, hazard, tables, edge, ranks):
+
+
+def pack(u4, send, edge, ranks):
     _, wears, ages, size = u4.shape
     cells = wears * ages
-    copied = [PIN(hazard.shape, f32)] + [PIN(t.shape[1:], f32) for t in tables[1:]]
-    out = pl.pallas_call(
+    return pl.pallas_call(
         functools.partial(pack_kernel, ranks),
-        in_specs=[VMEM] + [ANY] * (SHARED + TABLES + len(edge)),
-        out_specs=[VMEM] * (len(ranks) + SHARED + TABLES),
-        out_shape=[PIN((2 * r, cells), bf16) for r in ranks] + [PIN(tables[0].shape[1:], bf16)] + copied,
-        scratch_shapes=[pltpu.SemaphoreType.DMA((SHARED + TABLES,))],
-        compiler_params=params(16),
+        in_specs=[VMEM] * 2 + [ANY] * len(edge),
+        out_specs=[VMEM] * len(ranks),
+        out_shape=[PIN((2 * r, cells), bf16) for r in ranks],
+        compiler_params=params(8),
         cost_estimate=cost(4 * cells * sum(ranks) * size, 8 * cells * size),
         name="pack_coefficients",
-    )(in_vmem(u4), *[in_hbm(x) for x in (hazard, *tables)], *[in_vmem(x) for x in edge])
-    return out[: len(ranks)], out[len(ranks)], out[len(ranks) + 1 :]
+    )(*[in_vmem(x) for x in (u4, send, *edge)])
 
 
 def pack_edges_kernel(ranks, sides, send_ref, *refs):
@@ -241,17 +224,19 @@
         out_specs=[VMEM] * (1 + len(ranks)),
         out_shape=[PIN(arrived.shape, bf16)] + [PIN((2 * r, extra), bf16) for r in ranks],
         input_output_aliases={1 + sides: 0},
-        compiler_params=params(16),
+        compiler_params=params(8),
         cost_estimate=cost(0, 2**18),
         name="pack_edges",
     )(*[in_vmem(x) for x in (send, *near, arrived)])
 
 
-def local_kernel(sides, u_ref, hazard, diffusion, drift, second, first, take_second, take_first, *refs):
-    edge_refs, fields, (beside, ends, take, own) = refs[:sides], refs[sides : sides + SUBSTEPS], refs[sides + SUBSTEPS :]
+def local_kernel(sides, u_ref, tables, hazard, diffusion, drift, *refs):
+    edge_refs, fields, refs = refs[:sides], refs[sides : sides + SUBSTEPS], refs[sides + SUBSTEPS :]
+    beside, ends, take, own = refs
     z = fields[0]
     halves, rows, _, _ = z.shape
     _, wears, ages, size = u_ref.shape
+    at = lax.axis_index("cheb")
     for l in range(halves):
         zero = jnp.zeros((rows, 16, 128), f32)
         z[l, :, :ROW0, :] = zero
@@ -259,9 +244,9 @@
         for later in fields[1:]:
             later[l, :, ROW0 - 8 : ROW0, :] = zero[:, :8]
             later[l, :, ROW0 + ages : ROW0 + ages + 8, :] = zero[:, :8]
-    scaled, moved = START * diffusion[...], START * drift[...]
-    own[...] = (second[...] * scaled + first[...] * moved).astype(bf16)
-    take[...] = (take_second[...] * scaled + take_first[...] * moved).astype(bf16)
+    both = tables[at, 0] * (START * diffusion[at]) + tables[at, 1] * (START * drift[at])
+    own[...] = both[:size].astype(bf16)
+    take[...] = both[size:].reshape(take.shape).astype(bf16)
     keep = jnp.transpose(START - START * hazard[...])
     chunk = 4
     for w in range(0, 2 * wears, chunk):
@@ -287,24 +272,27 @@
             beside[s, place] = rate[place] + jnp.concatenate(columns, axis=0) * ref[place].astype(f32)
 
 
-def local(u4, tables, near, sides):
+def local(u4, tables, hazard, diffusion, drift, near, sides):
     _, wears, ages, size = u4.shape
     cells = 2 * wears * ages
+    wide = (tables.shape[2] - size) // 2
     return pl.pallas_call(
         functools.partial(local_kernel, sides),
-        in_specs=[VMEM] * (1 + len(tables) + sides),
+        in_specs=[VMEM] * (5 + sides),
         out_specs=[VMEM] * (SUBSTEPS + 3),
         out_shape=[pltpu.VMEM((size // 128, 2 * wears + 2 * HALO, ages + 32, 128), f32)] * SUBSTEPS
         + [
             pltpu.VMEM((sides, 2 * wears * HALO, size), f32),
             pltpu.VMEM((2, HALO * ages, size), f32),
-            pltpu.VMEM(tables[-1].shape, bf16),
+            pltpu.VMEM((2, wide, size), bf16),
         ],
-        scratch_shapes=[pltpu.VMEM((size, size), bf16)],
-        compiler_params=params(16),
+        scratch_shapes=[
+            pltpu.VMEM((size, size), bf16),
+        ],
+        compiler_params=params(8),
         cost_estimate=cost(2 * cells * size * size, 8 * cells * size),
         name="local_rate",
-    )(*[in_vmem(x) for x in (u4, *tables, *near)])
+    )(*[in_vmem(x) for x in (u4, tables, hazard, diffusion, drift, *near)])
 
 
 def distant(ranks, q_refs, take_ref, half, columns):
@@ -353,7 +341,7 @@
         in_specs=[VMEM] * (3 + 2 * len(ranks)),
         out_specs=[VMEM] * 2,
         out_shape=[message, message],
-        compiler_params=params(16),
+        compiler_params=params(8),
         cost_estimate=cost(2 * 8 * ages * take.shape[1] * size, 2**20),
         name="outer_rows",
     )(*[in_vmem(x) for x in (ends, beside, take, *q, *q_edges)])
@@ -398,7 +386,7 @@
         out_specs=VMEM,
         out_shape=pltpu.VMEM(z.shape, f32),
         input_output_aliases={0: 0},
-        compiler_params=params(16),
+        compiler_params=params(8),
         cost_estimate=cost(2 * cells * take.shape[1] * size, 8 * cells * size),
         name="section",
     )(z, *[in_vmem(x) for x in (beside, take, *q, *q_edges)])
@@ -437,10 +425,10 @@
     lax.fori_loop(start, stop, step, (centre1 + less0, less1), unroll=unroll)
 
 
-def put_in(dst, l, lo, hi, keeps, factor=None):
+def put_in(dst, l, lo, hi, keeps, beyond=None, factor=None):
     def put(w, out):
-        if factor is not None:
-            out = out * factor(w)
+        if factor is not None and beyond(w):
+            out = out * factor
         if keeps is None:
             dst[l, w, lo:hi, :] = out
         else:
@@ -514,7 +502,7 @@
             pltpu.SemaphoreType.DMA((2,)),
         ],
         input_output_aliases={1: 2, 2: 3, 3: 4},
-        compiler_params=params(16),
+        compiler_params=params(8),
         cost_estimate=cost(10 * SUBSTEPS * wears * ages * size, 8 * wears * ages * size),
         name="inner_substeps",
     )(*[in_vmem(x) for x in fields], speed)
@@ -553,10 +541,7 @@
                     beyond = (lambda w: w < HALO, lambda w: w >= HALO + wears)[e]
                     rows_step(
                         fields[k - 1], l, start, start + HALO, low, high, lane_terms(speed_ref, l),
-                        put_in(
-                            fields[k], l, low, high, keeps,
-                            lambda w, e=e, beyond=beyond: jnp.where(beyond(w), near[e], 1.0).astype(f32),
-                        ), 4,
+                        put_in(fields[k], l, low, high, keeps, beyond, near[e]), HALO,
                     )
         for e, start in enumerate((HALO, rows - 2 * HALO)):
             for l in range(halves):
@@ -582,7 +567,7 @@
         out_specs=[ANY] + [VMEM] * 4,
         scratch_shapes=[pltpu.VMEM((2, HALO, ages, size), f32), pltpu.SemaphoreType.DMA((3,))],
         input_output_aliases={i: i for i in range(5)},
-        compiler_params=params(16),
+        compiler_params=params(8),
         cost_estimate=cost(20 * SUBSTEPS * 2 * HALO * ages * size, 2**20),
         name="outer_substeps",
     )(o, *[in_vmem(x) for x in (*fields, rest)], speed, in_vmem(first), in_vmem(second))[0]
@@ -598,23 +583,34 @@
     sides = 1 if n_age == 2 else 2
     extra = sides * wears // 2 * HALO
     u4 = adjoint_value.reshape(2, wears // 2, ages, size)
+    sides = 1 if n_age == 2 else 2
+    extra = sides * wears // 2 * HALO
+    u4 = adjoint_value.reshape(2, wears // 2, ages, size)
     diffusion = load_diffusion.reshape(devices, 1, size)
     drift = load_drift.reshape(devices, 1, size)
-    tables = [jnp.asarray(t, f32) for t in (own_second, own_first, take_second, take_first)]
+    tables = np.stack(
+        [
+            np.concatenate([own, take.reshape(devices, -1, size)], axis=1)
+            for own, take in ((own_second, take_second), (own_first, take_first))
+        ],
+        axis=1,
+    )
+    diffusion = load_diffusion.reshape(devices, 1, size)
+    drift = load_drift.reshape(devices, 1, size)
 
     def ring(n):
         after = [(i, (i + 1) % n) for i in range(n)]
         return after, [(j, i) for i, j in after]
 
     most = 2 * max(ranks) * (wears // 2 * ages) // size
-    edge = edges(adjoint_value, hazard, sides, max(wears * HALO + HAZARD_ROWS, -(-most // 16) * 16))
+    *edge, send = edges(adjoint_value, hazard, jnp.asarray(send, bf16), sides, max(wears * HALO + HAZARD_ROWS, -(-most // 16) * 16))
     near = [lax.ppermute(x, "age", pairs) for x, pairs in zip(edge, ring(n_age))]
-    q, send, tables = pack(u4, hazard, [jnp.asarray(send, bf16), diffusion, drift, *tables], edge, ranks)
+    q = pack(u4, send, edge, ranks)
     moves = [list(pairs) for pairs, _ in slots]
     arrived = [lax.ppermute(x, "cheb", pairs) for x, pairs in zip(q, moves)]
     arrived[0], *q_edges = pack_edges(send, near, arrived[0], ranks, sides, extra)
     arrived_edges = [lax.ppermute(x, "cheb", pairs) for x, pairs in zip(q_edges, moves)]
-    z, *later, beside, ends, take = local(u4, tables, near, sides)
+    z, *later, beside, ends, take = local(u4, jnp.asarray(tables, f32), hazard, diffusion, drift, near, sides)
     messages = outer_rows(ends, beside, take, arrived, arrived_edges, ranks, sides, wears, ages)
     around = []
     for w in range(n_wear):

time: 25.8 us -> 25.4 us (0.984)
  Pallas kernels: 14.8 us -> 13.9 us
  waiting for transfers between devices: 1.28 us -> 1.82 us
    pallas_call x2, Pallas kernels: 2.86 us -> 2.05 us  [the longest x1 1.32 us: edges(): pl.pallas_call(functools.partial(edge_kernel, sides), in_specs=[ANY] * 3,...]
    ppermute x1, waiting for transfers between devices: 0.01 us -> 0.7 us  [body(): lax.ppermute(x, 'age', pairs)]
    ppermute x3, waiting for transfers between devices: 1.22 us -> 0.54 us  [body(): arrived = [lax.ppermute(x, 'cheb', pairs) for x, pairs in zip(q, moves)]]
    ppermute x3, waiting for transfers between devices: 0.05 us -> 0.57 us  [body(): lax.ppermute(x, 'cheb', pairs)]
  transfers between devices with their start and end apart: 9 -> 9, of which waited for: 1 -> 3; matrix products, arithmetic and copies ran while one was open for 0% -> 0% of each run, Pallas kernels for 45% -> 42%
where the time goes in v6:
time: 25.4 us; the launch traced here: 25.3 us
  Pallas kernels  13.9 us (55%)
  starting transfers between devices  9.51 us (37%)
  waiting for transfers between devices  1.82 us (7%)
    pallas_call x1, Pallas kernels, inner_substeps(): pl.pallas_call(functools.partial(inner_kernel, sides), out_shape=[jax.Sha...  7.03 us
    ppermute x1, starting transfers between devices, body(): lax.ppermute(x, 'age', pairs)  3.02 us
    ppermute x3, starting transfers between devices, body(): arrived = [lax.ppermute(x, 'cheb', pairs) for x, pairs in zip(q, moves)]  2.21 us
    ppermute x3, starting transfers between devices, body(): lax.ppermute(x, 'cheb', pairs)  2.2 us
    ppermute x2, starting transfers between devices, body(): lax.ppermute(x, ('wear', 'age'), turn)  2.08 us
    pallas_call x1, Pallas kernels, outer_substeps(): pl.pallas_call(functools.partial(outer_kernel, sides), out_shape=[jax.Sha...  1.68 us
    pallas_call x1, Pallas kernels, local(): pl.pallas_call(functools.partial(local_kernel, sides), in_specs=[VMEM] *...  1.58 us
    pallas_call x1, Pallas kernels, edges(): pl.pallas_call(functools.partial(edge_kernel, sides), in_specs=[ANY] * 3,...  1.32 us
  transfers between devices with their start and end apart: 9, of which 3 were waited for; matrix products, arithmetic and copies ran while one was open for 0% of the time, Pallas kernels for 42%

profile of v6, /device:TPU:0, one launch (start us, length us, event | category | flops | bytes accessed | tf_op | source)
XLA Modules:
  0.0 25.3 jit_solution(6065344305630116665)
XLA Ops:
  0.0 0.0 copy-start.2
  0.0 0.0 copy-start
  0.0 0.0 copy-start.1
  0.0 0.0 copy-start.5
  0.0 0.0 copy-start.4
  0.0 1.3 %age_edges.1 = (bf16[272,256]{1,0:T(8,128)(2,1)S(1)}, bf16[40,256]{1,0:T(8,128)(2,1)S(1)}) custom-call(f32[64,64,256]{2,1,0:T(8,128)} %u_hbm.1, f32[64,64]{1,0:T(8,128)} %hazard.1, bf16[4,40,256]{2,1,0:T(8,128)(2,1)} %constant.4.clone.send_hbm), custom_call_target="tpu_custom_call" | custom-call | bytes 1048576 | tf_op jit(solution)/shard_map/age_edges/pallas_call | solution.py:151
  1.3 3.0 %collective-permute-start = (bf16[272,256]{1,0:T(8,128)(2,1)S(1)}, bf16[272,256]{1,0:T(8,128)(2,1)S(1)}, u32[]{:S(2)}, u32[]{:S(2)}) collective-permute-start(bf16[272,256]{1,0:T(8,128)(2,1)S(1)} %get-tuple-element.29.refs_0_), channel_id=1, source_target_pairs={{0,1},{1,0},{2,3},{3,2},{4,5},{5,4},{6,7},{7,6},{8,9},{9,8},{10,11... | collective-permute-start | bytes 417800 | tf_op jit(solution)/shard_map/ppermute | solution.py:607
  4.4 0.0 copy-done
  4.4 0.7 %pack_coefficients.1 = (bf16[32,2048]{1,0:T(8,128)(2,1)S(1)}, bf16[16,2048]{1,0:T(8,128)(2,1)S(1)}, bf16[32,2048]{1,0:T(8,128)(2,1)S(1)}) custom-call(f32[2,32,64,256]{3,2,1,0:T(8,128)S(1)} %bitcast.4, bf16[40,256]{1,0:T(8,128)(2,1)S(1)} %get-tuple-element.33.send.send_ref, bf16[272,256]{1,0:T(8,128)(2,1)S(1)} %get-tuple-element.29.refs_0_), custom_call_target="tpu_custom_call" | custom-call | flops 83886080 | bytes 4194304 | tf_op jit(solution)/shard_map/pack_coefficients/pallas_call | solution.py:198
  5.1 0.1 collective-permute-start.1
  5.2 1.6 %collective-permute-start.3 = (bf16[32,2048]{1,0:T(8,128)(2,1)S(1)}, bf16[32,2048]{1,0:T(8,128)(2,1)S(1)}, u32[]{:S(2)}, u32[]{:S(2)}) collective-permute-start(bf16[32,2048]{1,0:T(8,128)(2,1)S(1)} %get-tuple-element.37), channel_id=1, source_target_pairs={{0,24},{8,16},{16,8},{24,0},{1,25},{9,17},{17,9},{25,1},{2,26},{10... | collective-permute-start | bytes 393224 | tf_op jit(solution)/shard_map/ppermute | solution.py:610
  6.8 0.5 %collective-permute-start.2 = (bf16[16,2048]{1,0:T(8,128)(2,1)S(1)}, bf16[16,2048]{1,0:T(8,128)(2,1)S(1)}, u32[]{:S(2)}, u32[]{:S(2)}) collective-permute-start(bf16[16,2048]{1,0:T(8,128)(2,1)S(1)} %get-tuple-element.36), channel_id=1, source_target_pairs={{0,16},{8,24},{16,0},{24,8},{1,17},{9,25},{17,1},{25,9},{2,18},{10... | collective-permute-start | bytes 196616 | tf_op jit(solution)/shard_map/ppermute | solution.py:610
  7.3 0.0 collective-permute-done.1.refs_1_
  7.3 0.7 %collective-permute-done.refs_0_ = bf16[272,256]{1,0:T(8,128)(2,1)S(1)} collective-permute-done((bf16[272,256]{1,0:T(8,128)(2,1)S(1)}, bf16[272,256]{1,0:T(8,128)(2,1)S(1)}, u32[]{:S(2)}, u32[]{:S(2)}) %collective-permute-start) | collective-permute-done | bytes 139296 | tf_op jit(solution)/shard_map/ppermute | solution.py:607
  8.0 0.1 pack_edges.1
  8.2 1.8 %collective-permute-start.5 = (bf16[16,128]{1,0:T(8,128)(2,1)S(1)}, bf16[16,128]{1,0:T(8,128)(2,1)S(1)}, u32[]{:S(2)}, u32[]{:S(2)}) collective-permute-start(bf16[16,128]{1,0:T(8,128)(2,1)S(1)} %get-tuple-element.39), channel_id=1, source_target_pairs={{0,16},{8,24},{16,0},{24,8},{1,17},{9,25},{17,1},{25,9},{2,18},{10... | collective-permute-start | bytes 12296 | tf_op jit(solution)/shard_map/ppermute | solution.py:612
  10.0 0.0 collective-permute-start.4
  10.0 0.4 %collective-permute-start.6 = (bf16[32,128]{1,0:T(8,128)(2,1)S(1)}, bf16[32,128]{1,0:T(8,128)(2,1)S(1)}, u32[]{:S(2)}, u32[]{:S(2)}) collective-permute-start(bf16[32,128]{1,0:T(8,128)(2,1)S(1)} %get-tuple-element.40), channel_id=1, source_target_pairs={{0,24},{8,16},{16,8},{24,0},{1,25},{9,17},{17,9},{25,1},{2,26},{10... | collective-permute-start | bytes 24584 | tf_op jit(solution)/shard_map/ppermute | solution.py:612
  10.4 0.0 copy-done.2
  10.4 0.0 copy-done.1
  10.4 0.0 copy-done.5
  10.4 0.0 copy-done.4
  10.4 1.6 %local_rate.1 = (f32[2,72,96,128]{3,2,1,0:T(8,128)S(1)}, f32[2,72,96,128]{3,2,1,0:T(8,128)S(1)}, f32[2,72,96,128]{3,2,1,0:T(8,128)S(1)}, f32[2,72,96,128]{3,2,1,...) custom-call(f32[2,32,64,256]{3,2,1,0:T(8,128)S(1)} %bitcast.5, ...), custom_call_target="tpu_custom_call" | custom-call | flops 536870912 | bytes 8388608 | tf_op jit(solution)/shard_map/local_rate/pallas_call | solution.py:279
  12.0 0.5 %collective-permute-done.2.refs_1_ = bf16[16,2048]{1,0:T(8,128)(2,1)S(1)} collective-permute-done((bf16[16,2048]{1,0:T(8,128)(2,1)S(1)}, bf16[16,2048]{1,0:T(8,128)(2,1)S(1)}, u32[]{:S(2)}, u32[]{:S(2)}) %collective-permute-start.2) | collective-permute-done | bytes 65568 | tf_op jit(solution)/shard_map/ppermute | solution.py:610
  12.5 0.0 collective-permute-done.3.refs_2_
  12.5 0.0 collective-permute-done.5.refs_4_
  12.5 0.0 collective-permute-done.4.refs_3_
  12.5 0.5 %collective-permute-done.6.refs_5_ = bf16[32,128]{1,0:T(8,128)(2,1)S(1)} collective-permute-done((bf16[32,128]{1,0:T(8,128)(2,1)S(1)}, bf16[32,128]{1,0:T(8,128)(2,1)S(1)}, u32[]{:S(2)}, u32[]{:S(2)}) %collective-permute-start.6) | collective-permute-done | bytes 8224 | tf_op jit(solution)/shard_map/ppermute | solution.py:612
  13.1 0.3 %outer_rows.1 = (bf16[272,256]{1,0:T(8,128)(2,1)S(1)}, bf16[272,256]{1,0:T(8,128)(2,1)S(1)}) custom-call(f32[2,256,256]{2,1,0:T(8,128)S(1)} %get-tuple-element.49.ends_ref, f32[1,256,256]{2,1,0:T(8,128)S(1)} %get-tuple-element.31.beside_ref, bf16[2,48,256]{2,1,0:T(8,128)(2,1)S(1)} %get-tuple-element.32.take_ref, ...), custom_call_target="tpu_custom_call" | custom-call | flops 12582912 | bytes 1048576 | tf_op jit(solution)/shard_map/outer_rows/pallas_call | solution.py:339
  13.4 1.6 %collective-permute-start.7 = (bf16[272,256]{1,0:T(8,128)(2,1)S(1)}, bf16[272,256]{1,0:T(8,128)(2,1)S(1)}, u32[]{:S(2)}, u32[]{:S(2)}) collective-permute-start(bf16[272,256]{1,0:T(8,128)(2,1)S(1)} %get-tuple-element.50), channel_id=1, source_target_pairs={{0,2},{1,0},{2,4},{3,1},{4,6},{5,3},{6,7},{7,5},{8,10},{9,8},{10,1... | collective-permute-start | bytes 417800 | tf_op jit(solution)/shard_map/ppermute | solution.py:624
  15.0 0.5 %collective-permute-start.8 = (bf16[272,256]{1,0:T(8,128)(2,1)S(1)}, bf16[272,256]{1,0:T(8,128)(2,1)S(1)}, u32[]{:S(2)}, u32[]{:S(2)}) collective-permute-start(bf16[272,256]{1,0:T(8,128)(2,1)S(1)} %get-tuple-element.51), channel_id=1, source_target_pairs={{2,0},{0,1},{4,2},{1,3},{6,4},{3,5},{7,6},{5,7},{10,8},{8,9},{12,1... | collective-permute-start | bytes 417800 | tf_op jit(solution)/shard_map/ppermute | solution.py:624
  15.5 0.0 copy-start.3
  15.5 1.1 %section.1.z0.z0_in = f32[2,72,96,128]{3,2,1,0:T(8,128)S(1)} custom-call(f32[2,72,96,128]{3,2,1,0:T(8,128)S(1)} %get-tuple-element.30.z_in, f32[1,256,256]{2,1,0:T(8,128)S(1)} %get-tuple-element.31.beside_ref, bf16[2,48,256]{2,1,0:T(8,128)(2,1)S(1)} %get-tuple-element.32.take_ref, ...), custom_call_target="tpu_custom_call", output_to_operand_aliasing={{}: (0, {})} | custom-call | flops 100663296 | bytes 8388608 | tf_op jit(solution)/shard_map/section/pallas_call | solution.py:383
  16.6 0.0 copy-done.3
  16.6 7.0 %inner_substeps.1 = (f32[64,64,256]{2,1,0:T(8,128)}, f32[16,64,256]{2,1,0:T(8,128)S(1)}, f32[2,72,96,128]{3,2,1,0:T(8,128)S(1)}, f32[2,72,96,128]{3,2,1,0:T(8,128)S(1)}, f32[2,72,96,128]{3,2,1,0:T(8,128)S(1)}) custom-call(f32[2,72,96,128]{3,2,1,0:T(8,128)S(1)} %section.1.z0.z0_in, ...), custom_call_target="tpu_custom_call", output_to_operand_aliasing={{2}: (1, {}), {3}: (2, {}), {4}: (3, {})} | custom-call | flops 41943040 | bytes 8388608 | tf_op jit(solution)/shard_map/inner_substeps/pallas_call | solution.py:495
  23.6 0.0 collective-permute-done.7.first_ref
  23.6 0.0 collective-permute-done.8.second_ref
  23.6 1.7 %outer_substeps.1 = (f32[64,64,256]{2,1,0:T(8,128)}, f32[2,72,96,128]{3,2,1,0:T(8,128)S(1)}, f32[2,72,96,128]{3,2,1,0:T(8,128)S(1)}, f32[2,72,96,128]{3,2,1,0:T(8,128)S(1)}, f32[2,72,96,128]{3,2,1,0:T(8,128)S(1)}) custom-call(f32[64,64,256]{2,1,0:T(8,128)} %get-tuple-element.44.o_in, ...), custom_call_target="tpu_custom_call", output_to_operand_aliasing={{0}: (0, {}), {1}: (1, {}), {2}: (2, {}), {3}: (3, {}), {4}... | custom-call | flops 10485760 | bytes 1048576 | tf_op jit(solution)/shard_map/outer_substeps/pallas_call | solution.py:563
Async XLA Ops:
  0.0 10.4 %copy-start.2 = (f32[64,64]{1,0:T(8,128)S(1)}, f32[64,64]{1,0:T(8,128)}, u32[]{:S(2)}) copy-start(f32[64,64]{1,0:T(8,128)} %hazard.1) | copy-start | bytes 49156
  0.0 4.4 %copy-start = (f32[64,64,256]{2,1,0:T(8,128)S(1)}, f32[64,64,256]{2,1,0:T(8,128)}, u32[]{:S(2)}) copy-start(f32[64,64,256]{2,1,0:T(8,128)} %u_hbm.1) | copy-start | bytes 12582916
  0.0 10.4 %copy-start.1 = (f32[4,2,352,256]{3,2,1,0:T(8,128)S(1)}, f32[4,2,352,256]{3,2,1,0:T(8,128)}, u32[]{:S(2)}) copy-start(f32[4,2,352,256]{3,2,1,0:T(8,128)} %constant.5.clone.tables) | copy-start | bytes 8650756
  0.0 10.4 %copy-start.5 = (f32[1024]{0:T(1024)S(1)}, f32[1024]{0:T(1024)}, u32[]{:S(2)}) copy-start(f32[1024]{0:T(1024)} %param.9) | copy-start | bytes 12292
  0.0 10.4 %copy-start.4 = (f32[1024]{0:T(1024)S(1)}, f32[1024]{0:T(1024)}, u32[]{:S(2)}) copy-start(f32[1024]{0:T(1024)} %param.8) | copy-start | bytes 12292
  1.3 6.7 %collective-permute-start = (bf16[272,256]{1,0:T(8,128)(2,1)S(1)}, bf16[272,256]{1,0:T(8,128)(2,1)S(1)}, u32[]{:S(2)}, u32[]{:S(2)}) collective-permute-start(bf16[272,256]{1,0:T(8,128)(2,1)S(1)} %get-tuple-element.29.refs_0_), channel_id=1, source_target_pairs={{0,1},{1,0},{2,3},{3,2},{4,5},{5,4},{6,7},{7,6},{8,9},{9,8},{10,11... | collective-permute-start | bytes 417800 | tf_op jit(solution)/shard_map/ppermute | solution.py:607
  5.1 2.2 %collective-permute-start.1 = (bf16[32,2048]{1,0:T(8,128)(2,1)S(1)}, bf16[32,2048]{1,0:T(8,128)(2,1)S(1)}, u32[]{:S(2)}, u32[]{:S(2)}) collective-permute-start(bf16[32,2048]{1,0:T(8,128)(2,1)S(1)} %get-tuple-element.34), channel_id=1, source_target_pairs={{0,8},{8,0},{16,24},{24,16},{1,9},{9,1},{17,25},{25,17},{2,10},{10... | collective-permute-start | bytes 393224 | tf_op jit(solution)/shard_map/ppermute | solution.py:610
  5.2 7.3 %collective-permute-start.3 = (bf16[32,2048]{1,0:T(8,128)(2,1)S(1)}, bf16[32,2048]{1,0:T(8,128)(2,1)S(1)}, u32[]{:S(2)}, u32[]{:S(2)}) collective-permute-start(bf16[32,2048]{1,0:T(8,128)(2,1)S(1)} %get-tuple-element.37), channel_id=1, source_target_pairs={{0,24},{8,16},{16,8},{24,0},{1,25},{9,17},{17,9},{25,1},{2,26},{10... | collective-permute-start | bytes 393224 | tf_op jit(solution)/shard_map/ppermute | solution.py:610
  6.8 5.7 %collective-permute-start.2 = (bf16[16,2048]{1,0:T(8,128)(2,1)S(1)}, bf16[16,2048]{1,0:T(8,128)(2,1)S(1)}, u32[]{:S(2)}, u32[]{:S(2)}) collective-permute-start(bf16[16,2048]{1,0:T(8,128)(2,1)S(1)} %get-tuple-element.36), channel_id=1, source_target_pairs={{0,16},{8,24},{16,0},{24,8},{1,17},{9,25},{17,1},{25,9},{2,18},{10... | collective-permute-start | bytes 196616 | tf_op jit(solution)/shard_map/ppermute | solution.py:610
  8.2 4.4 %collective-permute-start.5 = (bf16[16,128]{1,0:T(8,128)(2,1)S(1)}, bf16[16,128]{1,0:T(8,128)(2,1)S(1)}, u32[]{:S(2)}, u32[]{:S(2)}) collective-permute-start(bf16[16,128]{1,0:T(8,128)(2,1)S(1)} %get-tuple-element.39), channel_id=1, source_target_pairs={{0,16},{8,24},{16,0},{24,8},{1,17},{9,25},{17,1},{25,9},{2,18},{10... | collective-permute-start | bytes 12296 | tf_op jit(solution)/shard_map/ppermute | solution.py:612
  10.0 2.5 %collective-permute-start.4 = (bf16[32,128]{1,0:T(8,128)(2,1)S(1)}, bf16[32,128]{1,0:T(8,128)(2,1)S(1)}, u32[]{:S(2)}, u32[]{:S(2)}) collective-permute-start(bf16[32,128]{1,0:T(8,128)(2,1)S(1)} %get-tuple-element.38), channel_id=1, source_target_pairs={{0,8},{8,0},{16,24},{24,16},{1,9},{9,1},{17,25},{25,17},{2,10},{10... | collective-permute-start | bytes 24584 | tf_op jit(solution)/shard_map/ppermute | solution.py:612
  10.0 3.1 %collective-permute-start.6 = (bf16[32,128]{1,0:T(8,128)(2,1)S(1)}, bf16[32,128]{1,0:T(8,128)(2,1)S(1)}, u32[]{:S(2)}, u32[]{:S(2)}) collective-permute-start(bf16[32,128]{1,0:T(8,128)(2,1)S(1)} %get-tuple-element.40), channel_id=1, source_target_pairs={{0,24},{8,16},{16,8},{24,0},{1,25},{9,17},{17,9},{25,1},{2,26},{10... | collective-permute-start | bytes 24584 | tf_op jit(solution)/shard_map/ppermute | solution.py:612
  13.4 10.2 %collective-permute-start.7 = (bf16[272,256]{1,0:T(8,128)(2,1)S(1)}, bf16[272,256]{1,0:T(8,128)(2,1)S(1)}, u32[]{:S(2)}, u32[]{:S(2)}) collective-permute-start(bf16[272,256]{1,0:T(8,128)(2,1)S(1)} %get-tuple-element.50), channel_id=1, source_target_pairs={{0,2},{1,0},{2,4},{3,1},{4,6},{5,3},{6,7},{7,5},{8,10},{9,8},{10,1... | collective-permute-start | bytes 417800 | tf_op jit(solution)/shard_map/ppermute | solution.py:624
  15.0 8.6 %collective-permute-start.8 = (bf16[272,256]{1,0:T(8,128)(2,1)S(1)}, bf16[272,256]{1,0:T(8,128)(2,1)S(1)}, u32[]{:S(2)}, u32[]{:S(2)}) collective-permute-start(bf16[272,256]{1,0:T(8,128)(2,1)S(1)} %get-tuple-element.51), channel_id=1, source_target_pairs={{2,0},{0,1},{4,2},{1,3},{6,4},{3,5},{7,6},{5,7},{10,8},{8,9},{12,1... | collective-permute-start | bytes 417800 | tf_op jit(solution)/shard_map/ppermute | solution.py:624
  15.5 1.1 %copy-start.3 = (f32[256]{0:T(256)S(1)}, f32[256]{0:T(256)}, u32[]{:S(2)}) copy-start(f32[256]{0:T(256)} %param.10) | copy-start | bytes 3076

commit v7 on v6

--- a/solution.py
+++ b/solution.py
@@ -230,6 +230,10 @@
     )(*[in_vmem(x) for x in (send, *near, arrived)])
 
 
+def own_rate(u, own):
+    return jnp.dot(jnp.concatenate([u, u], axis=1), own[...], preferred_element_type=f32)
+
+
 def local_kernel(sides, u_ref, tables, hazard, diffusion, drift, *refs):
     edge_refs, fields, refs = refs[:sides], refs[sides : sides + SUBSTEPS], refs[sides + SUBSTEPS :]
     beside, ends, take, own = refs
@@ -245,14 +249,16 @@
             later[l, :, ROW0 - 8 : ROW0, :] = zero[:, :8]
             later[l, :, ROW0 + ages : ROW0 + ages + 8, :] = zero[:, :8]
     both = tables[at, 0] * (START * diffusion[at]) + tables[at, 1] * (START * drift[at])
-    own[...] = both[:size].astype(bf16)
+    high = both[:size].astype(bf16)
+    own[:size] = high
+    own[size:] = (both[:size] - high.astype(f32)).astype(bf16)
     take[...] = both[size:].reshape(take.shape).astype(bf16)
     keep = jnp.transpose(START - START * hazard[...])
     chunk = 4
     for w in range(0, 2 * wears, chunk):
         half, v = divmod(w, wears)
         u = u_ref[half, v : v + chunk].reshape(chunk * ages, size)
-        rate = jnp.dot(u.astype(bf16), own[...], preferred_element_type=f32)
+        rate = own_rate(u.astype(bf16), own)
         for i in range(chunk):
             cells = slice(i * ages, (i + 1) * ages)
             value = rate[cells] + keep[:, w + i : w + i + 1] * u[cells]
@@ -265,7 +271,7 @@
         count = 2 * wears * HALO
         parts = ref[count : count + HAZARD_ROWS].astype(f32)
         near = START - START * (parts[:HALO, : 2 * wears] + parts[HALO : 2 * HALO, : 2 * wears])
-        rate = jnp.dot(ref[:count], own[...], preferred_element_type=f32)
+        rate = own_rate(ref[:count], own)
         for w in range(0, 2 * wears, 4):
             place = slice(w * HALO, (w + 4) * HALO)
             columns = [jnp.broadcast_to(near[:, w + j : w + j + 1], (HALO, size)) for j in range(4)]
@@ -286,11 +292,9 @@
             pltpu.VMEM((2, HALO * ages, size), f32),
             pltpu.VMEM((2, wide, size), bf16),
         ],
-        scratch_shapes=[
-            pltpu.VMEM((size, size), bf16),
-        ],
-        compiler_params=params(8),
-        cost_estimate=cost(2 * cells * size * size, 8 * cells * size),
+        scratch_shapes=[pltpu.VMEM((2 * size, size), bf16)],
+        compiler_params=params(8),
+        cost_estimate=cost(4 * cells * size * size, 8 * cells * size),
         name="local_rate",
     )(*[in_vmem(x) for x in (u4, tables, hazard, diffusion, drift, *near)])
 

time: 25.4 us -> 25.4 us (level)
  waiting for transfers between devices: 1.82 us -> 1.43 us
  Pallas kernels: 13.9 us -> 14.2 us
    ppermute x3, waiting for transfers between devices: 0.54 us -> 0.15 us  [body(): arrived = [lax.ppermute(x, 'cheb', pairs) for x, pairs in zip(q, moves)]]
    pallas_call x1, Pallas kernels: 1.58 us -> 1.96 us  [local(): pl.pallas_call(functools.partial(local_kernel, sides), in_specs=[VMEM] *...]
  transfers between devices with their start and end apart: 9 -> 9, of which waited for: 3 -> 3; matrix products, arithmetic and copies ran while one was open for 0% -> 0% of each run, Pallas kernels for 42% -> 43%
where the time goes in v7:
time: 25.4 us; the launch traced here: 25.3 us
  Pallas kernels  14.2 us (56%)
  starting transfers between devices  9.51 us (37%)
  waiting for transfers between devices  1.43 us (6%)
    pallas_call x1, Pallas kernels, inner_substeps(): pl.pallas_call(functools.partial(inner_kernel, sides), out_shape=[jax.Sha...  7.03 us
    ppermute x1, starting transfers between devices, body(): lax.ppermute(x, 'age', pairs)  3.02 us
    ppermute x3, starting transfers between devices, body(): arrived = [lax.ppermute(x, 'cheb', pairs) for x, pairs in zip(q, moves)]  2.21 us
    ppermute x3, starting transfers between devices, body(): lax.ppermute(x, 'cheb', pairs)  2.2 us
    ppermute x2, starting transfers between devices, body(): lax.ppermute(x, ('wear', 'age'), turn)  2.08 us
    pallas_call x1, Pallas kernels, local(): pl.pallas_call(functools.partial(local_kernel, sides), in_specs=[VMEM] *...  1.96 us
    pallas_call x1, Pallas kernels, outer_substeps(): pl.pallas_call(functools.partial(outer_kernel, sides), out_shape=[jax.Sha...  1.68 us
    pallas_call x1, Pallas kernels, edges(): pl.pallas_call(functools.partial(edge_kernel, sides), in_specs=[ANY] * 3,...  1.32 us
  transfers between devices with their start and end apart: 9, of which 3 were waited for; matrix products, arithmetic and copies ran while one was open for 0% of the time, Pallas kernels for 43%

profile of v7, /device:TPU:0, one launch (start us, length us, event | category | flops | bytes accessed | tf_op | source)
XLA Modules:
  0.0 25.3 jit_solution(16713317982616487434)
XLA Ops:
  0.0 0.0 copy-start.2
  0.0 0.0 copy-start
  0.0 0.0 copy-start.1
  0.0 0.0 copy-start.5
  0.0 0.0 copy-start.4
  0.0 1.3 %age_edges.1 = (bf16[272,256]{1,0:T(8,128)(2,1)S(1)}, bf16[40,256]{1,0:T(8,128)(2,1)S(1)}) custom-call(f32[64,64,256]{2,1,0:T(8,128)} %u_hbm.1, f32[64,64]{1,0:T(8,128)} %hazard.1, bf16[4,40,256]{2,1,0:T(8,128)(2,1)} %constant.4.clone.send_hbm), custom_call_target="tpu_custom_call" | custom-call | bytes 1048576 | tf_op jit(solution)/shard_map/age_edges/pallas_call | solution.py:151
  1.3 3.0 %collective-permute-start = (bf16[272,256]{1,0:T(8,128)(2,1)S(1)}, bf16[272,256]{1,0:T(8,128)(2,1)S(1)}, u32[]{:S(2)}, u32[]{:S(2)}) collective-permute-start(bf16[272,256]{1,0:T(8,128)(2,1)S(1)} %get-tuple-element.29.refs_0_), channel_id=1, source_target_pairs={{0,1},{1,0},{2,3},{3,2},{4,5},{5,4},{6,7},{7,6},{8,9},{9,8},{10,11... | collective-permute-start | bytes 417800 | tf_op jit(solution)/shard_map/ppermute | solution.py:611
  4.4 0.0 copy-done
  4.4 0.7 %pack_coefficients.1 = (bf16[32,2048]{1,0:T(8,128)(2,1)S(1)}, bf16[16,2048]{1,0:T(8,128)(2,1)S(1)}, bf16[32,2048]{1,0:T(8,128)(2,1)S(1)}) custom-call(f32[2,32,64,256]{3,2,1,0:T(8,128)S(1)} %bitcast.4, bf16[40,256]{1,0:T(8,128)(2,1)S(1)} %get-tuple-element.33.send.send_ref, bf16[272,256]{1,0:T(8,128)(2,1)S(1)} %get-tuple-element.29.refs_0_), custom_call_target="tpu_custom_call" | custom-call | flops 83886080 | bytes 4194304 | tf_op jit(solution)/shard_map/pack_coefficients/pallas_call | solution.py:198
  5.1 0.1 collective-permute-start.1
  5.2 1.6 %collective-permute-start.3 = (bf16[32,2048]{1,0:T(8,128)(2,1)S(1)}, bf16[32,2048]{1,0:T(8,128)(2,1)S(1)}, u32[]{:S(2)}, u32[]{:S(2)}) collective-permute-start(bf16[32,2048]{1,0:T(8,128)(2,1)S(1)} %get-tuple-element.37), channel_id=1, source_target_pairs={{0,24},{8,16},{16,8},{24,0},{1,25},{9,17},{17,9},{25,1},{2,26},{10... | collective-permute-start | bytes 393224 | tf_op jit(solution)/shard_map/ppermute | solution.py:614
  6.8 0.5 %collective-permute-start.2 = (bf16[16,2048]{1,0:T(8,128)(2,1)S(1)}, bf16[16,2048]{1,0:T(8,128)(2,1)S(1)}, u32[]{:S(2)}, u32[]{:S(2)}) collective-permute-start(bf16[16,2048]{1,0:T(8,128)(2,1)S(1)} %get-tuple-element.36), channel_id=1, source_target_pairs={{0,16},{8,24},{16,0},{24,8},{1,17},{9,25},{17,1},{25,9},{2,18},{10... | collective-permute-start | bytes 196616 | tf_op jit(solution)/shard_map/ppermute | solution.py:614
  7.3 0.0 collective-permute-done.1.refs_1_
  7.3 0.7 %collective-permute-done.refs_0_ = bf16[272,256]{1,0:T(8,128)(2,1)S(1)} collective-permute-done((bf16[272,256]{1,0:T(8,128)(2,1)S(1)}, bf16[272,256]{1,0:T(8,128)(2,1)S(1)}, u32[]{:S(2)}, u32[]{:S(2)}) %collective-permute-start) | collective-permute-done | bytes 139296 | tf_op jit(solution)/shard_map/ppermute | solution.py:611
  8.0 0.1 pack_edges.1
  8.2 1.8 %collective-permute-start.5 = (bf16[16,128]{1,0:T(8,128)(2,1)S(1)}, bf16[16,128]{1,0:T(8,128)(2,1)S(1)}, u32[]{:S(2)}, u32[]{:S(2)}) collective-permute-start(bf16[16,128]{1,0:T(8,128)(2,1)S(1)} %get-tuple-element.39), channel_id=1, source_target_pairs={{0,16},{8,24},{16,0},{24,8},{1,17},{9,25},{17,1},{25,9},{2,18},{10... | collective-permute-start | bytes 12296 | tf_op jit(solution)/shard_map/ppermute | solution.py:616
  10.0 0.0 collective-permute-start.4
  10.0 0.4 %collective-permute-start.6 = (bf16[32,128]{1,0:T(8,128)(2,1)S(1)}, bf16[32,128]{1,0:T(8,128)(2,1)S(1)}, u32[]{:S(2)}, u32[]{:S(2)}) collective-permute-start(bf16[32,128]{1,0:T(8,128)(2,1)S(1)} %get-tuple-element.40), channel_id=1, source_target_pairs={{0,24},{8,16},{16,8},{24,0},{1,25},{9,17},{17,9},{25,1},{2,26},{10... | collective-permute-start | bytes 24584 | tf_op jit(solution)/shard_map/ppermute | solution.py:616
  10.4 0.0 copy-done.2
  10.4 0.0 copy-done.1
  10.4 0.0 copy-done.5
  10.4 0.0 copy-done.4
  10.4 2.0 %local_rate.1 = (f32[2,72,96,128]{3,2,1,0:T(8,128)S(1)}, f32[2,72,96,128]{3,2,1,0:T(8,128)S(1)}, f32[2,72,96,128]{3,2,1,0:T(8,128)S(1)}, f32[2,72,96,128]{3,2,1,...) custom-call(f32[2,32,64,256]{3,2,1,0:T(8,128)S(1)} %bitcast.5, ...), custom_call_target="tpu_custom_call" | custom-call | flops 1073741824 | bytes 8388608 | tf_op jit(solution)/shard_map/local_rate/pallas_call | solution.py:285
  12.3 0.1 collective-permute-done.2.refs_1_
  12.5 0.0 collective-permute-done.3.refs_2_
  12.5 0.0 collective-permute-done.5.refs_4_
  12.5 0.0 collective-permute-done.4.refs_3_
  12.5 0.5 %collective-permute-done.6.refs_5_ = bf16[32,128]{1,0:T(8,128)(2,1)S(1)} collective-permute-done((bf16[32,128]{1,0:T(8,128)(2,1)S(1)}, bf16[32,128]{1,0:T(8,128)(2,1)S(1)}, u32[]{:S(2)}, u32[]{:S(2)}) %collective-permute-start.6) | collective-permute-done | bytes 8224 | tf_op jit(solution)/shard_map/ppermute | solution.py:616
  13.1 0.3 %outer_rows.1 = (bf16[272,256]{1,0:T(8,128)(2,1)S(1)}, bf16[272,256]{1,0:T(8,128)(2,1)S(1)}) custom-call(f32[2,256,256]{2,1,0:T(8,128)S(1)} %get-tuple-element.49.ends_ref, f32[1,256,256]{2,1,0:T(8,128)S(1)} %get-tuple-element.31.beside_ref, bf16[2,48,256]{2,1,0:T(8,128)(2,1)S(1)} %get-tuple-element.32.take_ref, ...), custom_call_target="tpu_custom_call" | custom-call | flops 12582912 | bytes 1048576 | tf_op jit(solution)/shard_map/outer_rows/pallas_call | solution.py:343
  13.4 1.6 %collective-permute-start.7 = (bf16[272,256]{1,0:T(8,128)(2,1)S(1)}, bf16[272,256]{1,0:T(8,128)(2,1)S(1)}, u32[]{:S(2)}, u32[]{:S(2)}) collective-permute-start(bf16[272,256]{1,0:T(8,128)(2,1)S(1)} %get-tuple-element.50), channel_id=1, source_target_pairs={{0,2},{1,0},{2,4},{3,1},{4,6},{5,3},{6,7},{7,5},{8,10},{9,8},{10,1... | collective-permute-start | bytes 417800 | tf_op jit(solution)/shard_map/ppermute | solution.py:628
  15.0 0.5 %collective-permute-start.8 = (bf16[272,256]{1,0:T(8,128)(2,1)S(1)}, bf16[272,256]{1,0:T(8,128)(2,1)S(1)}, u32[]{:S(2)}, u32[]{:S(2)}) collective-permute-start(bf16[272,256]{1,0:T(8,128)(2,1)S(1)} %get-tuple-element.51), channel_id=1, source_target_pairs={{2,0},{0,1},{4,2},{1,3},{6,4},{3,5},{7,6},{5,7},{10,8},{8,9},{12,1... | collective-permute-start | bytes 417800 | tf_op jit(solution)/shard_map/ppermute | solution.py:628
  15.5 0.0 copy-start.3
  15.5 1.1 %section.1.z0.z0_in = f32[2,72,96,128]{3,2,1,0:T(8,128)S(1)} custom-call(f32[2,72,96,128]{3,2,1,0:T(8,128)S(1)} %get-tuple-element.30.z_in, f32[1,256,256]{2,1,0:T(8,128)S(1)} %get-tuple-element.31.beside_ref, bf16[2,48,256]{2,1,0:T(8,128)(2,1)S(1)} %get-tuple-element.32.take_ref, ...), custom_call_target="tpu_custom_call", output_to_operand_aliasing={{}: (0, {})} | custom-call | flops 100663296 | bytes 8388608 | tf_op jit(solution)/shard_map/section/pallas_call | solution.py:387
  16.6 0.0 copy-done.3
  16.6 7.0 %inner_substeps.1 = (f32[64,64,256]{2,1,0:T(8,128)}, f32[16,64,256]{2,1,0:T(8,128)S(1)}, f32[2,72,96,128]{3,2,1,0:T(8,128)S(1)}, f32[2,72,96,128]{3,2,1,0:T(8,128)S(1)}, f32[2,72,96,128]{3,2,1,0:T(8,128)S(1)}) custom-call(f32[2,72,96,128]{3,2,1,0:T(8,128)S(1)} %section.1.z0.z0_in, ...), custom_call_target="tpu_custom_call", output_to_operand_aliasing={{2}: (1, {}), {3}: (2, {}), {4}: (3, {})} | custom-call | flops 41943040 | bytes 8388608 | tf_op jit(solution)/shard_map/inner_substeps/pallas_call | solution.py:499
  23.6 0.0 collective-permute-done.7.first_ref
  23.6 0.0 collective-permute-done.8.second_ref
  23.6 1.7 %outer_substeps.1 = (f32[64,64,256]{2,1,0:T(8,128)}, f32[2,72,96,128]{3,2,1,0:T(8,128)S(1)}, f32[2,72,96,128]{3,2,1,0:T(8,128)S(1)}, f32[2,72,96,128]{3,2,1,0:T(8,128)S(1)}, f32[2,72,96,128]{3,2,1,0:T(8,128)S(1)}) custom-call(f32[64,64,256]{2,1,0:T(8,128)} %get-tuple-element.44.o_in, ...), custom_call_target="tpu_custom_call", output_to_operand_aliasing={{0}: (0, {}), {1}: (1, {}), {2}: (2, {}), {3}: (3, {}), {4}... | custom-call | flops 10485760 | bytes 1048576 | tf_op jit(solution)/shard_map/outer_substeps/pallas_call | solution.py:567
Async XLA Ops:
  0.0 10.4 %copy-start.2 = (f32[64,64]{1,0:T(8,128)S(1)}, f32[64,64]{1,0:T(8,128)}, u32[]{:S(2)}) copy-start(f32[64,64]{1,0:T(8,128)} %hazard.1) | copy-start | bytes 49156
  0.0 4.4 %copy-start = (f32[64,64,256]{2,1,0:T(8,128)S(1)}, f32[64,64,256]{2,1,0:T(8,128)}, u32[]{:S(2)}) copy-start(f32[64,64,256]{2,1,0:T(8,128)} %u_hbm.1) | copy-start | bytes 12582916
  0.0 10.4 %copy-start.1 = (f32[4,2,352,256]{3,2,1,0:T(8,128)S(1)}, f32[4,2,352,256]{3,2,1,0:T(8,128)}, u32[]{:S(2)}) copy-start(f32[4,2,352,256]{3,2,1,0:T(8,128)} %constant.5.clone.tables) | copy-start | bytes 8650756
  0.0 10.4 %copy-start.5 = (f32[1024]{0:T(1024)S(1)}, f32[1024]{0:T(1024)}, u32[]{:S(2)}) copy-start(f32[1024]{0:T(1024)} %param.9) | copy-start | bytes 12292
  0.0 10.4 %copy-start.4 = (f32[1024]{0:T(1024)S(1)}, f32[1024]{0:T(1024)}, u32[]{:S(2)}) copy-start(f32[1024]{0:T(1024)} %param.8) | copy-start | bytes 12292
  1.3 6.7 %collective-permute-start = (bf16[272,256]{1,0:T(8,128)(2,1)S(1)}, bf16[272,256]{1,0:T(8,128)(2,1)S(1)}, u32[]{:S(2)}, u32[]{:S(2)}) collective-permute-start(bf16[272,256]{1,0:T(8,128)(2,1)S(1)} %get-tuple-element.29.refs_0_), channel_id=1, source_target_pairs={{0,1},{1,0},{2,3},{3,2},{4,5},{5,4},{6,7},{7,6},{8,9},{9,8},{10,11... | collective-permute-start | bytes 417800 | tf_op jit(solution)/shard_map/ppermute | solution.py:611
  5.1 2.2 %collective-permute-start.1 = (bf16[32,2048]{1,0:T(8,128)(2,1)S(1)}, bf16[32,2048]{1,0:T(8,128)(2,1)S(1)}, u32[]{:S(2)}, u32[]{:S(2)}) collective-permute-start(bf16[32,2048]{1,0:T(8,128)(2,1)S(1)} %get-tuple-element.34), channel_id=1, source_target_pairs={{0,8},{8,0},{16,24},{24,16},{1,9},{9,1},{17,25},{25,17},{2,10},{10... | collective-permute-start | bytes 393224 | tf_op jit(solution)/shard_map/ppermute | solution.py:614
  5.2 7.3 %collective-permute-start.3 = (bf16[32,2048]{1,0:T(8,128)(2,1)S(1)}, bf16[32,2048]{1,0:T(8,128)(2,1)S(1)}, u32[]{:S(2)}, u32[]{:S(2)}) collective-permute-start(bf16[32,2048]{1,0:T(8,128)(2,1)S(1)} %get-tuple-element.37), channel_id=1, source_target_pairs={{0,24},{8,16},{16,8},{24,0},{1,25},{9,17},{17,9},{25,1},{2,26},{10... | collective-permute-start | bytes 393224 | tf_op jit(solution)/shard_map/ppermute | solution.py:614
  6.8 5.7 %collective-permute-start.2 = (bf16[16,2048]{1,0:T(8,128)(2,1)S(1)}, bf16[16,2048]{1,0:T(8,128)(2,1)S(1)}, u32[]{:S(2)}, u32[]{:S(2)}) collective-permute-start(bf16[16,2048]{1,0:T(8,128)(2,1)S(1)} %get-tuple-element.36), channel_id=1, source_target_pairs={{0,16},{8,24},{16,0},{24,8},{1,17},{9,25},{17,1},{25,9},{2,18},{10... | collective-permute-start | bytes 196616 | tf_op jit(solution)/shard_map/ppermute | solution.py:614
  8.2 4.4 %collective-permute-start.5 = (bf16[16,128]{1,0:T(8,128)(2,1)S(1)}, bf16[16,128]{1,0:T(8,128)(2,1)S(1)}, u32[]{:S(2)}, u32[]{:S(2)}) collective-permute-start(bf16[16,128]{1,0:T(8,128)(2,1)S(1)} %get-tuple-element.39), channel_id=1, source_target_pairs={{0,16},{8,24},{16,0},{24,8},{1,17},{9,25},{17,1},{25,9},{2,18},{10... | collective-permute-start | bytes 12296 | tf_op jit(solution)/shard_map/ppermute | solution.py:616
  10.0 2.5 %collective-permute-start.4 = (bf16[32,128]{1,0:T(8,128)(2,1)S(1)}, bf16[32,128]{1,0:T(8,128)(2,1)S(1)}, u32[]{:S(2)}, u32[]{:S(2)}) collective-permute-start(bf16[32,128]{1,0:T(8,128)(2,1)S(1)} %get-tuple-element.38), channel_id=1, source_target_pairs={{0,8},{8,0},{16,24},{24,16},{1,9},{9,1},{17,25},{25,17},{2,10},{10... | collective-permute-start | bytes 24584 | tf_op jit(solution)/shard_map/ppermute | solution.py:616
  10.0 3.1 %collective-permute-start.6 = (bf16[32,128]{1,0:T(8,128)(2,1)S(1)}, bf16[32,128]{1,0:T(8,128)(2,1)S(1)}, u32[]{:S(2)}, u32[]{:S(2)}) collective-permute-start(bf16[32,128]{1,0:T(8,128)(2,1)S(1)} %get-tuple-element.40), channel_id=1, source_target_pairs={{0,24},{8,16},{16,8},{24,0},{1,25},{9,17},{17,9},{25,1},{2,26},{10... | collective-permute-start | bytes 24584 | tf_op jit(solution)/shard_map/ppermute | solution.py:616
  13.4 10.2 %collective-permute-start.7 = (bf16[272,256]{1,0:T(8,128)(2,1)S(1)}, bf16[272,256]{1,0:T(8,128)(2,1)S(1)}, u32[]{:S(2)}, u32[]{:S(2)}) collective-permute-start(bf16[272,256]{1,0:T(8,128)(2,1)S(1)} %get-tuple-element.50), channel_id=1, source_target_pairs={{0,2},{1,0},{2,4},{3,1},{4,6},{5,3},{6,7},{7,5},{8,10},{9,8},{10,1... | collective-permute-start | bytes 417800 | tf_op jit(solution)/shard_map/ppermute | solution.py:628
  15.0 8.6 %collective-permute-start.8 = (bf16[272,256]{1,0:T(8,128)(2,1)S(1)}, bf16[272,256]{1,0:T(8,128)(2,1)S(1)}, u32[]{:S(2)}, u32[]{:S(2)}) collective-permute-start(bf16[272,256]{1,0:T(8,128)(2,1)S(1)} %get-tuple-element.51), channel_id=1, source_target_pairs={{2,0},{0,1},{4,2},{1,3},{6,4},{3,5},{7,6},{5,7},{10,8},{8,9},{12,1... | collective-permute-start | bytes 417800 | tf_op jit(solution)/shard_map/ppermute | solution.py:628
  15.5 1.1 %copy-start.3 = (f32[256]{0:T(256)S(1)}, f32[256]{0:T(256)}, u32[]{:S(2)}) copy-start(f32[256]{0:T(256)} %param.10) | copy-start | bytes 3076

commit v8 on v7

--- a/solution.py
+++ b/solution.py
@@ -463,7 +463,7 @@
             for l in range(halves):
                 rows_step(
                     fields[k - 1], l, HALO + k, rows - HALO - k, low, high, lane_terms(speed_ref, l),
-                    put_in(fields[k], l, low, high, keeps), 4,
+                    put_in(fields[k], l, low, high, keeps), 10,
                 )
         stores = []
         first = HALO + SUBSTEPS
@@ -477,7 +477,7 @@
                         rest[w - first - done, :, l * 128 : (l + 1) * 128] = out
 
                 rows_step(
-                    fields[-1], l, first + a, first + b, ROW0, ROW0 + ages, lane_terms(speed_ref, l), put, 4,
+                    fields[-1], l, first + a, first + b, ROW0, ROW0 + ages, lane_terms(speed_ref, l), put, 8,
                 )
             if a < done:
                 copy = pltpu.make_async_copy(

time: 25.4 us -> 25.2 us (level)
  no operation moved by 1% of the time
where the time goes in v8:
time: 25.2 us; the launch traced here: 25.1 us
  Pallas kernels  14 us (56%)
  starting transfers between devices  9.51 us (38%)
  waiting for transfers between devices  1.43 us (6%)
    pallas_call x1, Pallas kernels, inner_substeps(): pl.pallas_call(functools.partial(inner_kernel, sides), out_shape=[jax.Sha...  6.79 us
    ppermute x1, starting transfers between devices, body(): lax.ppermute(x, 'age', pairs)  3.02 us
    ppermute x3, starting transfers between devices, body(): arrived = [lax.ppermute(x, 'cheb', pairs) for x, pairs in zip(q, moves)]  2.21 us
    ppermute x3, starting transfers between devices, body(): lax.ppermute(x, 'cheb', pairs)  2.2 us
    ppermute x2, starting transfers between devices, body(): lax.ppermute(x, ('wear', 'age'), turn)  2.08 us
    pallas_call x1, Pallas kernels, local(): pl.pallas_call(functools.partial(local_kernel, sides), in_specs=[VMEM] *...  1.96 us
    pallas_call x1, Pallas kernels, outer_substeps(): pl.pallas_call(functools.partial(outer_kernel, sides), out_shape=[jax.Sha...  1.68 us
    pallas_call x1, Pallas kernels, edges(): pl.pallas_call(functools.partial(edge_kernel, sides), in_specs=[ANY] * 3,...  1.32 us
  transfers between devices with their start and end apart: 9, of which 3 were waited for; matrix products, arithmetic and copies ran while one was open for 0% of the time, Pallas kernels for 43%

profile of v8, /device:TPU:0, one launch (start us, length us, event | category | flops | bytes accessed | tf_op | source)
XLA Modules:
  0.0 25.1 jit_solution(11941042203792927202)
XLA Ops:
  0.0 0.0 copy-start.2
  0.0 0.0 copy-start
  0.0 0.0 copy-start.1
  0.0 0.0 copy-start.5
  0.0 0.0 copy-start.4
  0.0 1.3 %age_edges.1 = (bf16[272,256]{1,0:T(8,128)(2,1)S(1)}, bf16[40,256]{1,0:T(8,128)(2,1)S(1)}) custom-call(f32[64,64,256]{2,1,0:T(8,128)} %u_hbm.1, f32[64,64]{1,0:T(8,128)} %hazard.1, bf16[4,40,256]{2,1,0:T(8,128)(2,1)} %constant.4.clone.send_hbm), custom_call_target="tpu_custom_call" | custom-call | bytes 1048576 | tf_op jit(solution)/shard_map/age_edges/pallas_call | solution.py:151
  1.3 3.0 %collective-permute-start = (bf16[272,256]{1,0:T(8,128)(2,1)S(1)}, bf16[272,256]{1,0:T(8,128)(2,1)S(1)}, u32[]{:S(2)}, u32[]{:S(2)}) collective-permute-start(bf16[272,256]{1,0:T(8,128)(2,1)S(1)} %get-tuple-element.29.refs_0_), channel_id=1, source_target_pairs={{0,1},{1,0},{2,3},{3,2},{4,5},{5,4},{6,7},{7,6},{8,9},{9,8},{10,11... | collective-permute-start | bytes 417800 | tf_op jit(solution)/shard_map/ppermute | solution.py:611
  4.4 0.0 copy-done
  4.4 0.7 %pack_coefficients.1 = (bf16[32,2048]{1,0:T(8,128)(2,1)S(1)}, bf16[16,2048]{1,0:T(8,128)(2,1)S(1)}, bf16[32,2048]{1,0:T(8,128)(2,1)S(1)}) custom-call(f32[2,32,64,256]{3,2,1,0:T(8,128)S(1)} %bitcast.4, bf16[40,256]{1,0:T(8,128)(2,1)S(1)} %get-tuple-element.33.send.send_ref, bf16[272,256]{1,0:T(8,128)(2,1)S(1)} %get-tuple-element.29.refs_0_), custom_call_target="tpu_custom_call" | custom-call | flops 83886080 | bytes 4194304 | tf_op jit(solution)/shard_map/pack_coefficients/pallas_call | solution.py:198
  5.1 0.1 collective-permute-start.1
  5.2 1.6 %collective-permute-start.3 = (bf16[32,2048]{1,0:T(8,128)(2,1)S(1)}, bf16[32,2048]{1,0:T(8,128)(2,1)S(1)}, u32[]{:S(2)}, u32[]{:S(2)}) collective-permute-start(bf16[32,2048]{1,0:T(8,128)(2,1)S(1)} %get-tuple-element.37), channel_id=1, source_target_pairs={{0,24},{8,16},{16,8},{24,0},{1,25},{9,17},{17,9},{25,1},{2,26},{10... | collective-permute-start | bytes 393224 | tf_op jit(solution)/shard_map/ppermute | solution.py:614
  6.8 0.5 %collective-permute-start.2 = (bf16[16,2048]{1,0:T(8,128)(2,1)S(1)}, bf16[16,2048]{1,0:T(8,128)(2,1)S(1)}, u32[]{:S(2)}, u32[]{:S(2)}) collective-permute-start(bf16[16,2048]{1,0:T(8,128)(2,1)S(1)} %get-tuple-element.36), channel_id=1, source_target_pairs={{0,16},{8,24},{16,0},{24,8},{1,17},{9,25},{17,1},{25,9},{2,18},{10... | collective-permute-start | bytes 196616 | tf_op jit(solution)/shard_map/ppermute | solution.py:614
  7.3 0.0 collective-permute-done.1.refs_1_
  7.3 0.7 %collective-permute-done.refs_0_ = bf16[272,256]{1,0:T(8,128)(2,1)S(1)} collective-permute-done((bf16[272,256]{1,0:T(8,128)(2,1)S(1)}, bf16[272,256]{1,0:T(8,128)(2,1)S(1)}, u32[]{:S(2)}, u32[]{:S(2)}) %collective-permute-start) | collective-permute-done | bytes 139296 | tf_op jit(solution)/shard_map/ppermute | solution.py:611
  8.0 0.1 pack_edges.1
  8.2 1.8 %collective-permute-start.5 = (bf16[16,128]{1,0:T(8,128)(2,1)S(1)}, bf16[16,128]{1,0:T(8,128)(2,1)S(1)}, u32[]{:S(2)}, u32[]{:S(2)}) collective-permute-start(bf16[16,128]{1,0:T(8,128)(2,1)S(1)} %get-tuple-element.39), channel_id=1, source_target_pairs={{0,16},{8,24},{16,0},{24,8},{1,17},{9,25},{17,1},{25,9},{2,18},{10... | collective-permute-start | bytes 12296 | tf_op jit(solution)/shard_map/ppermute | solution.py:616
  10.0 0.0 collective-permute-start.4
  10.0 0.4 %collective-permute-start.6 = (bf16[32,128]{1,0:T(8,128)(2,1)S(1)}, bf16[32,128]{1,0:T(8,128)(2,1)S(1)}, u32[]{:S(2)}, u32[]{:S(2)}) collective-permute-start(bf16[32,128]{1,0:T(8,128)(2,1)S(1)} %get-tuple-element.40), channel_id=1, source_target_pairs={{0,24},{8,16},{16,8},{24,0},{1,25},{9,17},{17,9},{25,1},{2,26},{10... | collective-permute-start | bytes 24584 | tf_op jit(solution)/shard_map/ppermute | solution.py:616
  10.4 0.0 copy-done.2
  10.4 0.0 copy-done.1
  10.4 0.0 copy-done.5
  10.4 0.0 copy-done.4
  10.4 2.0 %local_rate.1 = (f32[2,72,96,128]{3,2,1,0:T(8,128)S(1)}, f32[2,72,96,128]{3,2,1,0:T(8,128)S(1)}, f32[2,72,96,128]{3,2,1,0:T(8,128)S(1)}, f32[2,72,96,128]{3,2,1,...) custom-call(f32[2,32,64,256]{3,2,1,0:T(8,128)S(1)} %bitcast.5, ...), custom_call_target="tpu_custom_call" | custom-call | flops 1073741824 | bytes 8388608 | tf_op jit(solution)/shard_map/local_rate/pallas_call | solution.py:285
  12.3 0.1 collective-permute-done.2.refs_1_
  12.5 0.0 collective-permute-done.3.refs_2_
  12.5 0.0 collective-permute-done.5.refs_4_
  12.5 0.0 collective-permute-done.4.refs_3_
  12.5 0.5 %collective-permute-done.6.refs_5_ = bf16[32,128]{1,0:T(8,128)(2,1)S(1)} collective-permute-done((bf16[32,128]{1,0:T(8,128)(2,1)S(1)}, bf16[32,128]{1,0:T(8,128)(2,1)S(1)}, u32[]{:S(2)}, u32[]{:S(2)}) %collective-permute-start.6) | collective-permute-done | bytes 8224 | tf_op jit(solution)/shard_map/ppermute | solution.py:616
  13.1 0.3 %outer_rows.1 = (bf16[272,256]{1,0:T(8,128)(2,1)S(1)}, bf16[272,256]{1,0:T(8,128)(2,1)S(1)}) custom-call(f32[2,256,256]{2,1,0:T(8,128)S(1)} %get-tuple-element.49.ends_ref, f32[1,256,256]{2,1,0:T(8,128)S(1)} %get-tuple-element.31.beside_ref, bf16[2,48,256]{2,1,0:T(8,128)(2,1)S(1)} %get-tuple-element.32.take_ref, ...), custom_call_target="tpu_custom_call" | custom-call | flops 12582912 | bytes 1048576 | tf_op jit(solution)/shard_map/outer_rows/pallas_call | solution.py:343
  13.4 1.6 %collective-permute-start.7 = (bf16[272,256]{1,0:T(8,128)(2,1)S(1)}, bf16[272,256]{1,0:T(8,128)(2,1)S(1)}, u32[]{:S(2)}, u32[]{:S(2)}) collective-permute-start(bf16[272,256]{1,0:T(8,128)(2,1)S(1)} %get-tuple-element.50), channel_id=1, source_target_pairs={{0,2},{1,0},{2,4},{3,1},{4,6},{5,3},{6,7},{7,5},{8,10},{9,8},{10,1... | collective-permute-start | bytes 417800 | tf_op jit(solution)/shard_map/ppermute | solution.py:628
  15.0 0.5 %collective-permute-start.8 = (bf16[272,256]{1,0:T(8,128)(2,1)S(1)}, bf16[272,256]{1,0:T(8,128)(2,1)S(1)}, u32[]{:S(2)}, u32[]{:S(2)}) collective-permute-start(bf16[272,256]{1,0:T(8,128)(2,1)S(1)} %get-tuple-element.51), channel_id=1, source_target_pairs={{2,0},{0,1},{4,2},{1,3},{6,4},{3,5},{7,6},{5,7},{10,8},{8,9},{12,1... | collective-permute-start | bytes 417800 | tf_op jit(solution)/shard_map/ppermute | solution.py:628
  15.5 0.0 copy-start.3
  15.5 1.1 %section.1.z0.z0_in = f32[2,72,96,128]{3,2,1,0:T(8,128)S(1)} custom-call(f32[2,72,96,128]{3,2,1,0:T(8,128)S(1)} %get-tuple-element.30.z_in, f32[1,256,256]{2,1,0:T(8,128)S(1)} %get-tuple-element.31.beside_ref, bf16[2,48,256]{2,1,0:T(8,128)(2,1)S(1)} %get-tuple-element.32.take_ref, ...), custom_call_target="tpu_custom_call", output_to_operand_aliasing={{}: (0, {})} | custom-call | flops 100663296 | bytes 8388608 | tf_op jit(solution)/shard_map/section/pallas_call | solution.py:387
  16.6 0.0 copy-done.3
  16.6 6.8 %inner_substeps.1 = (f32[64,64,256]{2,1,0:T(8,128)}, f32[16,64,256]{2,1,0:T(8,128)S(1)}, f32[2,72,96,128]{3,2,1,0:T(8,128)S(1)}, f32[2,72,96,128]{3,2,1,0:T(8,128)S(1)}, f32[2,72,96,128]{3,2,1,0:T(8,128)S(1)}) custom-call(f32[2,72,96,128]{3,2,1,0:T(8,128)S(1)} %section.1.z0.z0_in, ...), custom_call_target="tpu_custom_call", output_to_operand_aliasing={{2}: (1, {}), {3}: (2, {}), {4}: (3, {})} | custom-call | flops 41943040 | bytes 8388608 | tf_op jit(solution)/shard_map/inner_substeps/pallas_call | solution.py:499
  23.4 0.0 collective-permute-done.7.first_ref
  23.4 0.0 collective-permute-done.8.second_ref
  23.4 1.7 %outer_substeps.1 = (f32[64,64,256]{2,1,0:T(8,128)}, f32[2,72,96,128]{3,2,1,0:T(8,128)S(1)}, f32[2,72,96,128]{3,2,1,0:T(8,128)S(1)}, f32[2,72,96,128]{3,2,1,0:T(8,128)S(1)}, f32[2,72,96,128]{3,2,1,0:T(8,128)S(1)}) custom-call(f32[64,64,256]{2,1,0:T(8,128)} %get-tuple-element.44.o_in, ...), custom_call_target="tpu_custom_call", output_to_operand_aliasing={{0}: (0, {}), {1}: (1, {}), {2}: (2, {}), {3}: (3, {}), {4}... | custom-call | flops 10485760 | bytes 1048576 | tf_op jit(solution)/shard_map/outer_substeps/pallas_call | solution.py:567
Async XLA Ops:
  0.0 10.4 %copy-start.2 = (f32[64,64]{1,0:T(8,128)S(1)}, f32[64,64]{1,0:T(8,128)}, u32[]{:S(2)}) copy-start(f32[64,64]{1,0:T(8,128)} %hazard.1) | copy-start | bytes 49156
  0.0 4.4 %copy-start = (f32[64,64,256]{2,1,0:T(8,128)S(1)}, f32[64,64,256]{2,1,0:T(8,128)}, u32[]{:S(2)}) copy-start(f32[64,64,256]{2,1,0:T(8,128)} %u_hbm.1) | copy-start | bytes 12582916
  0.0 10.4 %copy-start.1 = (f32[4,2,352,256]{3,2,1,0:T(8,128)S(1)}, f32[4,2,352,256]{3,2,1,0:T(8,128)}, u32[]{:S(2)}) copy-start(f32[4,2,352,256]{3,2,1,0:T(8,128)} %constant.5.clone.tables) | copy-start | bytes 8650756
  0.0 10.4 %copy-start.5 = (f32[1024]{0:T(1024)S(1)}, f32[1024]{0:T(1024)}, u32[]{:S(2)}) copy-start(f32[1024]{0:T(1024)} %param.9) | copy-start | bytes 12292
  0.0 10.4 %copy-start.4 = (f32[1024]{0:T(1024)S(1)}, f32[1024]{0:T(1024)}, u32[]{:S(2)}) copy-start(f32[1024]{0:T(1024)} %param.8) | copy-start | bytes 12292
  1.3 6.7 %collective-permute-start = (bf16[272,256]{1,0:T(8,128)(2,1)S(1)}, bf16[272,256]{1,0:T(8,128)(2,1)S(1)}, u32[]{:S(2)}, u32[]{:S(2)}) collective-permute-start(bf16[272,256]{1,0:T(8,128)(2,1)S(1)} %get-tuple-element.29.refs_0_), channel_id=1, source_target_pairs={{0,1},{1,0},{2,3},{3,2},{4,5},{5,4},{6,7},{7,6},{8,9},{9,8},{10,11... | collective-permute-start | bytes 417800 | tf_op jit(solution)/shard_map/ppermute | solution.py:611
  5.1 2.2 %collective-permute-start.1 = (bf16[32,2048]{1,0:T(8,128)(2,1)S(1)}, bf16[32,2048]{1,0:T(8,128)(2,1)S(1)}, u32[]{:S(2)}, u32[]{:S(2)}) collective-permute-start(bf16[32,2048]{1,0:T(8,128)(2,1)S(1)} %get-tuple-element.34), channel_id=1, source_target_pairs={{0,8},{8,0},{16,24},{24,16},{1,9},{9,1},{17,25},{25,17},{2,10},{10... | collective-permute-start | bytes 393224 | tf_op jit(solution)/shard_map/ppermute | solution.py:614
  5.2 7.3 %collective-permute-start.3 = (bf16[32,2048]{1,0:T(8,128)(2,1)S(1)}, bf16[32,2048]{1,0:T(8,128)(2,1)S(1)}, u32[]{:S(2)}, u32[]{:S(2)}) collective-permute-start(bf16[32,2048]{1,0:T(8,128)(2,1)S(1)} %get-tuple-element.37), channel_id=1, source_target_pairs={{0,24},{8,16},{16,8},{24,0},{1,25},{9,17},{17,9},{25,1},{2,26},{10... | collective-permute-start | bytes 393224 | tf_op jit(solution)/shard_map/ppermute | solution.py:614
  6.8 5.7 %collective-permute-start.2 = (bf16[16,2048]{1,0:T(8,128)(2,1)S(1)}, bf16[16,2048]{1,0:T(8,128)(2,1)S(1)}, u32[]{:S(2)}, u32[]{:S(2)}) collective-permute-start(bf16[16,2048]{1,0:T(8,128)(2,1)S(1)} %get-tuple-element.36), channel_id=1, source_target_pairs={{0,16},{8,24},{16,0},{24,8},{1,17},{9,25},{17,1},{25,9},{2,18},{10... | collective-permute-start | bytes 196616 | tf_op jit(solution)/shard_map/ppermute | solution.py:614
  8.2 4.4 %collective-permute-start.5 = (bf16[16,128]{1,0:T(8,128)(2,1)S(1)}, bf16[16,128]{1,0:T(8,128)(2,1)S(1)}, u32[]{:S(2)}, u32[]{:S(2)}) collective-permute-start(bf16[16,128]{1,0:T(8,128)(2,1)S(1)} %get-tuple-element.39), channel_id=1, source_target_pairs={{0,16},{8,24},{16,0},{24,8},{1,17},{9,25},{17,1},{25,9},{2,18},{10... | collective-permute-start | bytes 12296 | tf_op jit(solution)/shard_map/ppermute | solution.py:616
  10.0 2.5 %collective-permute-start.4 = (bf16[32,128]{1,0:T(8,128)(2,1)S(1)}, bf16[32,128]{1,0:T(8,128)(2,1)S(1)}, u32[]{:S(2)}, u32[]{:S(2)}) collective-permute-start(bf16[32,128]{1,0:T(8,128)(2,1)S(1)} %get-tuple-element.38), channel_id=1, source_target_pairs={{0,8},{8,0},{16,24},{24,16},{1,9},{9,1},{17,25},{25,17},{2,10},{10... | collective-permute-start | bytes 24584 | tf_op jit(solution)/shard_map/ppermute | solution.py:616
  10.0 3.1 %collective-permute-start.6 = (bf16[32,128]{1,0:T(8,128)(2,1)S(1)}, bf16[32,128]{1,0:T(8,128)(2,1)S(1)}, u32[]{:S(2)}, u32[]{:S(2)}) collective-permute-start(bf16[32,128]{1,0:T(8,128)(2,1)S(1)} %get-tuple-element.40), channel_id=1, source_target_pairs={{0,24},{8,16},{16,8},{24,0},{1,25},{9,17},{17,9},{25,1},{2,26},{10... | collective-permute-start | bytes 24584 | tf_op jit(solution)/shard_map/ppermute | solution.py:616
  13.4 10.0 %collective-permute-start.7 = (bf16[272,256]{1,0:T(8,128)(2,1)S(1)}, bf16[272,256]{1,0:T(8,128)(2,1)S(1)}, u32[]{:S(2)}, u32[]{:S(2)}) collective-permute-start(bf16[272,256]{1,0:T(8,128)(2,1)S(1)} %get-tuple-element.50), channel_id=1, source_target_pairs={{0,2},{1,0},{2,4},{3,1},{4,6},{5,3},{6,7},{7,5},{8,10},{9,8},{10,1... | collective-permute-start | bytes 417800 | tf_op jit(solution)/shard_map/ppermute | solution.py:628
  15.0 8.4 %collective-permute-start.8 = (bf16[272,256]{1,0:T(8,128)(2,1)S(1)}, bf16[272,256]{1,0:T(8,128)(2,1)S(1)}, u32[]{:S(2)}, u32[]{:S(2)}) collective-permute-start(bf16[272,256]{1,0:T(8,128)(2,1)S(1)} %get-tuple-element.51), channel_id=1, source_target_pairs={{2,0},{0,1},{4,2},{1,3},{6,4},{3,5},{7,6},{5,7},{10,8},{8,9},{12,1... | collective-permute-start | bytes 417800 | tf_op jit(solution)/shard_map/ppermute | solution.py:628
  15.5 1.1 %copy-start.3 = (f32[256]{0:T(256)S(1)}, f32[256]{0:T(256)}, u32[]{:S(2)}) copy-start(f32[256]{0:T(256)} %param.10) | copy-start | bytes 3076
